TPU v7x, 32 devices: a whole 2x2x4 slice. The times are simulated.
32 devices in a mesh: scan: 2 (over y), ang: 4 (over z), row: 4 (over x, core).
Axes of the slice: x: 2, y: 2, z: 4, core: 2. Of those that a mesh axis runs over, the one named last changes fastest.
Arguments:
- raw_frames: bfloat16 [96, 128, 2560], P(('scan', 'ang'), 'row'), parts along dimension 0, may hold values from 0.099609375 to 1.5
- dark_field: bfloat16 [128, 2560], P('row'), may hold values from 0 to 0.079589844
- flat_field: bfloat16 [128, 2560], P('row'), may hold values from 0.796875 to 1.1953125
- kernel_taps: float32 [31], replicated, may hold values from 0.1 to 0.4
- partner: int32 [48], P('scan'), parts along dimension 0, may hold values from 24 to 47, as said below
- shifts: int32 [256], replicated, may hold values from -256 to 255, as said below
Outputs:
- sinograms: bfloat16 [96, 128, 2560], P('scan', ('ang', 'row')), parts along dimension 0
- correlation: float32 [256, 256], P(('scan', 'ang', 'row')), parts along dimension 0
There are 2 independent parts, one for each index of `scan`. A program takes and returns all parts, laid end to end along the dimension named above; an argument that names none is the same for every part. Nothing has to cross between parts.
Inputs may be any that keep to these rules, and one draw needn't show every extreme that they name: partner[i] - i - 24 is -1, 0 or 1 for every i; partner[0] = 24 and partner[23] = 47. shifts[0] = -256 and shifts[255] = 255; values may repeat.
All inputs are finite; a program needn't handle non-finite values.
Results may differ from a plain program's by a relative error of at most 0.012.
The roundings to bfloat16 on the way count: a program that leaves them out, or rounds other values in their place, can miss the bound.
Values may be sent and summed in bfloat16 or wider, within the bound.
No kernel may reach another device: no remote copies, remote signals or barrier semaphores. Data moves between devices by JAX's collectives and lax.ppermute only.
A program may use at most 128 MiB of HBM per device.

v0:
```python
import math

import jax
import jax.numpy as jnp
from jax import lax
from jax.sharding import PartitionSpec as P

SPAN = 256


def padded_2(cells, sides, width):
    for axis, dim in sides:
        count = lax.axis_size(axis)
        ends = count - 1
        head = lax.slice_in_dim(cells, 0, width, axis=dim)
        tail = lax.slice_in_dim(cells, cells.shape[dim] - width, cells.shape[dim], axis=dim)
        cells = jnp.concatenate(
            [
                lax.ppermute(tail, axis, [(i, (i + 1) % count) for i in range(ends)]),
                cells,
                lax.ppermute(head, axis, [((i + 1) % count, i) for i in range(ends)]),
            ],
            axis=dim,
        )
    return cells


def absorb(raw_frames, dark_field, flat_field):
    counts = raw_frames.astype(jnp.float32)
    darkness = dark_field.astype(jnp.float32)
    brightness = flat_field.astype(jnp.float32)
    return -jnp.log((counts - darkness) / (brightness - darkness))


def column_pass(signal, kernel_taps):
    margin = kernel_taps.shape[0] // 2
    col_count = signal.shape[-1]
    padding = [(0, 0)] * (signal.ndim - 1) + [(margin, margin)]
    padded = jnp.pad(signal, padding)
    summed = kernel_taps[0] * padded[..., 0:col_count]
    for tap_index in range(1, kernel_taps.shape[0]):
        summed = summed + kernel_taps[tap_index] * padded[..., tap_index : tap_index + col_count]
    return summed


def row_pass(extended, kernel_taps, row_count, row_axis):
    summed = kernel_taps[0] * lax.slice_in_dim(extended, 0, row_count, axis=row_axis)
    for tap_index in range(1, kernel_taps.shape[0]):
        summed = summed + kernel_taps[tap_index] * lax.slice_in_dim(
            extended, tap_index, tap_index + row_count, axis=row_axis
        )
    return summed


def center_lines(lowpassed):
    return (lowpassed - jnp.mean(lowpassed, axis=-1, keepdims=True)).astype(jnp.bfloat16)


def ramp_matrix(col_count):
    distance = lax.iota(jnp.int32, col_count)[:, None] - lax.iota(jnp.int32, col_count)[None, :]
    spacing = distance.astype(jnp.float32)
    odd_distance = distance % 2 != 0
    falloff = -4.0 / (math.pi * math.pi * jnp.maximum(spacing * spacing, 1.0))
    kernel = jnp.where(distance == 0, 1.0, jnp.where(odd_distance, falloff, 0.0))
    return kernel.astype(jnp.bfloat16)


def apply_ramp(lines, ramp_kernel):
    col_count = lines.shape[-1]
    ramped = jnp.dot(lines.reshape(-1, col_count), ramp_kernel, preferred_element_type=jnp.float32)
    return ramped.astype(jnp.bfloat16).reshape(lines.shape)


def shards(raw_frames, dark_field, flat_field, kernel_taps, partner, shifts):
    planes, row_count, col_count = raw_frames.shape
    margin = kernel_taps.shape[0] // 2
    smooth = column_pass(absorb(raw_frames, dark_field[None], flat_field[None]), kernel_taps)
    extended = padded_2(smooth, (("row", 1),), margin)
    lowpassed = row_pass(extended, kernel_taps, row_count, 1)
    centered = center_lines(lowpassed)
    ang_count = lax.axis_size("ang")
    row_devices = lax.axis_size("row")
    upper_count = ang_count // row_devices
    row_share = row_count // ang_count
    shaped = centered.reshape(planes, upper_count, row_devices, row_share, col_count)
    ramp_kernel = ramp_matrix(col_count)
    across = lax.all_to_all(shaped, "row", split_axis=2, concat_axis=1, tiled=True)
    gathered = lax.all_to_all(across, "ang", split_axis=1, concat_axis=0, tiled=True)
    sinogram = gathered.reshape(-1, row_share, col_count)
    filtered = apply_ramp(sinogram, ramp_kernel)
    half_count = sinogram.shape[0] // 2
    leading = sinogram[:half_count]
    offset = partner - lax.iota(jnp.int32, half_count) - half_count
    earlier = sinogram[half_count - 1 : -1]
    middle = sinogram[half_count:]
    following = jnp.concatenate([sinogram[half_count + 1 :], jnp.zeros_like(sinogram[:1])], axis=0)
    chooser = offset[:, None, None]
    partner_rows = jnp.where(chooser < 0, earlier, jnp.where(chooser > 0, following, middle))
    mirrored = jnp.flip(partner_rows, axis=2)
    spread = SPAN
    tile_width = 128
    tile_count = col_count // tile_width
    span_tiles = 2 * spread // tile_width + 1
    window_width = span_tiles * tile_width
    padded = jnp.pad(mirrored, ((0, 0), (0, 0), (spread, spread)))

    def row_profile(row_index):
        leading_row = lax.dynamic_index_in_dim(leading, row_index, 1, False).reshape(
            half_count, tile_count, tile_width
        )
        padded_row = lax.dynamic_index_in_dim(padded, row_index, 1, False).reshape(
            half_count, tile_count + span_tiles - 1, tile_width
        )
        windows = jnp.stack(
            [
                padded_row[:, shift_index : shift_index + tile_count]
                for shift_index in range(span_tiles)
            ],
            axis=2,
        )
        windows = windows.reshape(half_count, tile_count, window_width)
        products = jnp.einsum(
            "iqu,iqv->quv", leading_row, windows, preferred_element_type=jnp.float32
        )
        flattened = jnp.pad(
            products.reshape(tile_count, tile_width * window_width), ((0, 0), (0, tile_width))
        )
        skewed = flattened.reshape(tile_count, tile_width, window_width + 1)[:, :, : 2 * spread]
        return jnp.sum(skewed, axis=(0, 1))

    profile = lax.map(row_profile, lax.iota(jnp.int32, row_share))
    selector = (shifts[None, :] + spread == lax.iota(jnp.int32, 2 * spread)[:, None]).astype(
        jnp.float32
    )
    factor = (half_count * col_count) ** (-0.5)
    correlation = jnp.dot(profile, selector, precision=lax.Precision.HIGHEST) * factor
    return (filtered, correlation)


def solution(mesh):
    in_specs = (
        P(("scan", "ang"), "row", None),
        P("row", None),
        P("row", None),
        P(),
        P("scan"),
        P(),
    )
    out_specs = (P("scan", ("ang", "row"), None), P(("scan", "ang", "row"), None))
    return jax.shard_map(shards, mesh=mesh, in_specs=in_specs, out_specs=out_specs, check_vma=False)
```

profile of v0, /device:TPU:19, one launch (start us, length us, event | category | flops | bytes accessed | tf_op | source)
XLA Modules:
  0.0 509.3 jit_solution(13823215011532389307)
XLA Ops:
  8.7 50.3 %multiply_add_fusion = f32[12,32,2560]{2,1,0:T(8,128)S(1)} fusion(f32[12,32,2560]{2,1,0:T(8,128)S(1)} %log_negate_fusion, f32[]{:T(128)} %bitcast.37, f32[]{:T(128)} %bitcast.36, f32[]{:T(128)} %bitcast.35, f32[]{:T(128)} %bitcast.34, f32[]{:T(128)} %bitcast.33, f32[]{:T(128)} %bitcast.32, f32[]{:T(128)} %bitcast.31, f32[]{:T(128)} %bitcast.30, ...), kind=kLoop, calls=%fused_computation.175 | loop fusion | flops 59965440 | bytes 7864444 | tf_op jit(solution)/shard_map/add | solution.py:42
  62.1 4.6 collective-permute-start.1
  69.1 79.4 %fusion.140 = (f32[12,32]{1,0:T(8,128)S(1)}, f32[12,32,2560]{2,1,0:T(8,128)}) fusion(f32[12,15,2560]{2,1,0:T(8,128)} %collective-permute-done.1, f32[12,32,2560]{2,1,0:T(8,128)} %copy-done, f32[]{:T(128)} %bitcast.37, f32[]{:T(128)} %bitcast.36, f32[]{:T(128)} %bitcast.35, f32[]{:T(128)} %bitcast.34, f32[]{:T(128)} %bitcast.33, f32[]{:T(128)} %bitcast.32, ...), kind=kLoop, calls=%fused_computation.238 | loop fusion | flops 90439296 | bytes 11552380 | tf_op jit(solution)/shard_map/reduce_sum | solution.py:56
  151.0 45.9 %all_to_all.27 = bf16[12,1,4,8,2560]{4,3,0,1,2:T(8,128)(2,1)} all-to-all(bf16[12,1,4,8,2560]{4,3,0,1,2:T(8,128)(2,1)S(1)} %copy.38), channel_id=1, replica_groups=mesh['scan'=2,'ang'=4,'row'=4] {'row'}, dimensions={2} | all-to-all | bytes 3932160 | tf_op jit(solution)/shard_map/all_to_all | solution.py:87
  196.9 4.6 all-to-all-start.1
  202.1 41.4 %all-to-all-done.1 = bf16[12,4,1,8,2560]{4,3,0,2,1:T(8,128)(2,1)S(1)} async-done(((bf16[12,4,1,8,2560]{4,3,0,2,1:T(8,128)(2,1)}), bf16[12,4,1,8,2560]{4,3,0,2,1:T(8,128)(2,1)S(1)}, u32[]{:S(2)}, u32[]{:S(2)}) %all-to-all-start.1) | async-done | bytes 1966112 | tf_op jit(solution)/shard_map/all_to_all | solution.py:88
  245.2 7.4 %rev.4 = bf16[24,8,2560]{2,1,0:T(8,128)(2,1)} reverse(bf16[24,8,2560]{2,1,0:T(8,128)(2,1)S(1)} %slice_select_fusion), dimensions={2} | reverse | bytes 1966080 | tf_op jit(solution)/shard_map/jit(_flip)/rev | solution.py:99
  256.7 226.5 %while.12 = (s32[]{:T(128)}, f32[8,512]{1,0:T(8,128)S(1)}, s32[8]{0:T(128)S(1)}, bf16[24,8,2560]{2,0,1:T(8,128)(2,1)}, bf16[24,8,3072]{2,0,1:T(8,128)(2,1)S(1)},...) while((s32[]{:T(128)}, f32[8,512]{1,0:T(8,128)S(1)}, s32[8]{0:T(128)S(1)}, bf16[24,8,2560]{2,0,1:T(8,128)(2,1)}, ...), condition=%wide.region_3.4_spmd, body=%wide.region_1.3_spmd.sunk | while | flops 79953408 | bytes 73920672 | solution.py:131
  263.9 4.6 copy.55
  272.0 10.1 %reshape.75 = f32[20,128,641]{2,1,0:T(8,128)} reshape(f32[20,82048]{1,0:T(8,128)} %pad.485) | data formatting | bytes 13127680 | tf_op jit(solution)/shard_map/while/body/eval_jaxpr/reshape | solution.py:128
  292.2 4.6 copy.55
  300.3 10.1 %reshape.75 = f32[20,128,641]{2,1,0:T(8,128)} reshape(f32[20,82048]{1,0:T(8,128)} %pad.485) | data formatting | bytes 13127680 | tf_op jit(solution)/shard_map/while/body/eval_jaxpr/reshape | solution.py:128
  320.4 4.6 copy.55
  328.6 10.1 %reshape.75 = f32[20,128,641]{2,1,0:T(8,128)} reshape(f32[20,82048]{1,0:T(8,128)} %pad.485) | data formatting | bytes 13127680 | tf_op jit(solution)/shard_map/while/body/eval_jaxpr/reshape | solution.py:128
  356.8 10.1 %reshape.75 = f32[20,128,641]{2,1,0:T(8,128)} reshape(f32[20,82048]{1,0:T(8,128)} %pad.485) | data formatting | bytes 13127680 | tf_op jit(solution)/shard_map/while/body/eval_jaxpr/reshape | solution.py:128
  376.9 4.6 copy.55
  385.1 10.1 %reshape.75 = f32[20,128,641]{2,1,0:T(8,128)} reshape(f32[20,82048]{1,0:T(8,128)} %pad.485) | data formatting | bytes 13127680 | tf_op jit(solution)/shard_map/while/body/eval_jaxpr/reshape | solution.py:128
  405.2 4.6 copy.55
  413.3 10.1 %reshape.75 = f32[20,128,641]{2,1,0:T(8,128)} reshape(f32[20,82048]{1,0:T(8,128)} %pad.485) | data formatting | bytes 13127680 | tf_op jit(solution)/shard_map/while/body/eval_jaxpr/reshape | solution.py:128
  433.5 4.6 copy.55
  441.6 10.1 %reshape.75 = f32[20,128,641]{2,1,0:T(8,128)} reshape(f32[20,82048]{1,0:T(8,128)} %pad.485) | data formatting | bytes 13127680 | tf_op jit(solution)/shard_map/while/body/eval_jaxpr/reshape | solution.py:128
  461.7 4.6 copy.55
  469.9 10.1 %reshape.75 = f32[20,128,641]{2,1,0:T(8,128)} reshape(f32[20,82048]{1,0:T(8,128)} %pad.485) | data formatting | bytes 13127680 | tf_op jit(solution)/shard_map/while/body/eval_jaxpr/reshape | solution.py:128
  483.2 25.3 %fusion.130 = bf16[48,8,2560]{2,1,0:T(8,128)(2,1)} fusion(bf16[384,2560]{1,0:T(8,128)(2,1)} %bitcast.121), kind=kOutput, calls=%fused_computation.218 | convolution fusion | flops 5178327040 | bytes 3932160 | tf_op jit(solution)/shard_map/dot_general | solution.py:70
  (170 shorter events, 120.1 us)
Async XLA Ops:
  59.0 1.9 copy-start
  60.8 6.0 %collective-permute-start = (f32[12,15,2560]{2,1,0:T(8,128)S(1)}, f32[12,15,2560]{2,1,0:T(8,128)S(1)}, u32[]{:S(2)}, u32[]{:S(2)}) collective-permute-start(f32[12,15,2560]{2,1,0:T(8,128)S(1)} %get-tuple-element.95), channel_id=1, source_target_pairs={{0,1},{1,2},{2,3},{4,5},{5,6},{6,7},{8,9},{9,10},{10,11},{12,13},{... | collective-permute-start | bytes 5529608 | tf_op jit(solution)/shard_map/ppermute | solution.py:19
  62.1 6.9 %collective-permute-start.1 = (f32[12,15,2560]{2,1,0:T(8,128)S(1)}, f32[12,15,2560]{2,1,0:T(8,128)}, u32[]{:S(2)}, u32[]{:S(2)}) collective-permute-start(f32[12,15,2560]{2,1,0:T(8,128)S(1)} %get-tuple-element.96), channel_id=1, source_target_pairs={{1,0},{2,1},{3,2},{5,4},{6,5},{7,6},{9,8},{10,9},{11,10},{13,12},{... | collective-permute-start | bytes 5529608 | tf_op jit(solution)/shard_map/ppermute | solution.py:21
  151.0 50.5 %copy-start.4 = (s32[24]{0:T(128)S(1)}, s32[24]{0:T(128)}, u32[]{:S(2)}) copy-start(s32[24]{0:T(128)} %param.12) | copy-start | bytes 292
  151.0 50.5 %copy-start.2 = (s32[256]{0:T(256)S(1)}, s32[256]{0:T(256)}, u32[]{:S(2)}) copy-start(s32[256]{0:T(256)} %param.13) | copy-start | bytes 3076
  196.9 46.6 %all-to-all-start.1 = ((bf16[12,4,1,8,2560]{4,3,0,2,1:T(8,128)(2,1)}), bf16[12,4,1,8,2560]{4,3,0,2,1:T(8,128)(2,1)S(1)}, u32[]{:S(2)}, u32[]{:S(2)}) async-start(bf16[12,4,1,8,2560]{4,3,0,2,1:T(8,128)(2,1)} %bitcast.122), calls=%async_computation.1 | async-start | bytes 3932160 | tf_op jit(solution)/shard_map/all_to_all | solution.py:88
  243.5 1.7 copy-start.1
  483.2 25.3 %copy-start.3 = (s32[256]{0:T(256)S(1)}, s32[256]{0:T(256)}, u32[]{:S(2)}) copy-start(s32[256]{0:T(256)} %broadcast_add_fusion) | copy-start | bytes 3076
where the time goes:
time: 517 us; the launch traced here: 509 us
  local copies, waits for them, and re-layouts  197 us (38%)
  other arithmetic  160 us (31%)
  blocking collectives  45.9 us (9%)
  waiting for transfers between devices  43.7 us (8%)
  matrix products  34.6 us (7%)
  loops' own time  16.7 us (3%)
  starting transfers between devices  10.5 us (2%)
    reshape x8, local copies, waits for them, and re-layouts, row_profile(): flattened.reshape(tile_count, tile_width, window_width + 1)  81.2 us
    reduce_sum x1, other arithmetic, center_lines(): jnp.mean(lowpassed, axis=-1, keepdims=True)  79.4 us
    add x1, other arithmetic, column_pass(): summed + kernel_taps[tap_index] * padded[..., tap_index:tap_index + col_c...  50.3 us
    all_to_all x1, blocking collectives, shards(): lax.all_to_all(shaped, 'row', split_axis=2, concat_axis=1, tiled=True)  45.9 us
    while x64, local copies, waits for them, and re-layouts  45.6 us
    all_to_all x1, waiting for transfers between devices, shards(): lax.all_to_all(across, 'ang', split_axis=1, concat_axis=0, tiled=True)  41.4 us
    pad x8, local copies, waits for them, and re-layouts, row_profile(): jnp.pad(products.reshape(tile_count, tile_width * window_width), ((0, 0),...  28.6 us
    dot_general x1, matrix products, apply_ramp(): jnp.dot(lines.reshape(-1, col_count), ramp_kernel, preferred_element_type...  25.3 us
  transfers between devices with their start and end apart: 3, of which 3 were waited for; matrix products, arithmetic and copies ran while one was open for 0% of the time, Pallas kernels for 0%

commit v1 on v0

v1 whole, which is shorter than its diff:
```python
import functools
import math

import jax
import jax.numpy as jnp
from jax import lax
from jax.experimental import pallas as pl
from jax.experimental.pallas import tpu as pltpu
from jax.sharding import PartitionSpec as P

SPAN = 256
HALO = 16
GROUP = 4
TILE = 256
CELL = 128
VMEM_BYTES = 48 * 1024 * 1024

F32 = jnp.float32
BF16 = jnp.bfloat16


def call_params():
    return pltpu.CompilerParams(vmem_limit_bytes=VMEM_BYTES)


def whole(count):
    return [pl.BlockSpec(memory_space=pltpu.VMEM)] * count


def split_hi_lo(values):
    high = values.astype(BF16)
    return high, (values - high.astype(F32)).astype(BF16)


def banded(index, taps_ref, tap_count):
    total = jnp.zeros(index.shape, F32)
    for tap in range(tap_count):
        total = jnp.where(index == tap, taps_ref[tap], total)
    return total


def band_kernel(tap_count, rows, row_count, upper, share, place_ref, taps_ref, rowband_ref, colband_ref):
    me = place_ref[0]
    odd = lax.rem(me, 2)
    margin = tap_count // 2
    ext = rows + 2 * HALO
    height, depth = GROUP * rows, GROUP * ext
    out_at = lax.broadcasted_iota(jnp.int32, (height, depth), 0)
    in_at = lax.broadcasted_iota(jnp.int32, (height, depth), 1)
    line = out_at % share
    plane = (out_at // share) % GROUP
    block = out_at // (share * GROUP)
    step, up = block // upper, block % upper
    row = (up * row_count + (step ^ me)) * share + line
    place = in_at % ext
    straight = place - HALO
    crossed = jnp.where(place < HALO, rows + place, jnp.where(place >= rows + HALO, place - rows - 2 * HALO, straight))
    source = jnp.where(odd == 1, straight, crossed)
    index = jnp.where(in_at // ext == plane, source - row + margin, -1)
    high, low = split_hi_lo(banded(index, taps_ref, tap_count))
    rowband_ref[:height] = high
    rowband_ref[height:] = low
    width = TILE + 2 * CELL
    from_at = lax.broadcasted_iota(jnp.int32, (width, TILE), 0)
    to_at = lax.broadcasted_iota(jnp.int32, (width, TILE), 1)
    high, low = split_hi_lo(banded(from_at - CELL - to_at + margin, taps_ref, tap_count))
    colband_ref[0] = high
    colband_ref[1] = low


def lowpass_kernel(
    planes, rows, row_count, upper, share,
    place_ref, raw_ref, near_ref, far_ref, dark_ref, flat_ref, rowband_ref, colband_ref, *rest
):
    out_refs, (level_ref, dark_all_ref, absorbed_ref, high_ref, low_ref, smooth_ref) = rest[:row_count], rest[row_count:]
    cols = raw_ref.shape[-1]
    ext = rows + 2 * HALO
    far_ok = place_ref[1] == 1
    at = lax.broadcasted_iota(jnp.int32, (HALO, cols), 0)
    far_mask = (at * 0 + place_ref[1]) == 1
    spans = ((0, HALO), (HALO, rows), (HALO + rows, HALO))
    for (start, size), darkness, brightness in zip(
        spans,
        (near_ref[planes], dark_ref[...], far_ref[planes]),
        (near_ref[planes + 1], flat_ref[...], far_ref[planes + 1]),
    ):
        darkness = darkness.astype(F32)
        dark_all_ref[start : start + size] = darkness
        level_ref[start : start + size] = jnp.log(brightness.astype(F32) - darkness)
    for pad_ref in (high_ref, low_ref):
        pad_ref[:, :CELL] = jnp.zeros((pad_ref.shape[0], CELL), BF16)
        pad_ref[:, CELL + cols :] = jnp.zeros((pad_ref.shape[0], CELL), BF16)
    height = GROUP * rows
    for group in range(planes // GROUP):
        for inner in range(GROUP):
            plane = group * GROUP + inner
            for (start, size), counts_ref in zip(spans, (near_ref, raw_ref, far_ref)):
                counts = counts_ref[plane].astype(F32)
                absorbed = level_ref[start : start + size] - jnp.log(counts - dark_all_ref[start : start + size])
                if start > HALO:
                    absorbed = jnp.where(far_mask, absorbed, 0.0)
                absorbed_ref[inner * ext + start : inner * ext + start + size] = absorbed.astype(BF16)
        for at_col in range(0, cols, TILE):
            both = jnp.dot(rowband_ref[...], absorbed_ref[:, at_col : at_col + TILE], preferred_element_type=F32)
            high, low = split_hi_lo(both[:height] + both[height:])
            high_ref[:, CELL + at_col : CELL + at_col + TILE] = high
            low_ref[:, CELL + at_col : CELL + at_col + TILE] = low
        total = jnp.zeros((height, 1), F32)
        for at_col in range(0, cols, TILE):
            window = slice(at_col, at_col + TILE + 2 * CELL)
            piece = (
                jnp.dot(high_ref[:, window], colband_ref[0], preferred_element_type=F32)
                + jnp.dot(low_ref[:, window], colband_ref[0], preferred_element_type=F32)
                + jnp.dot(high_ref[:, window], colband_ref[1], preferred_element_type=F32)
            )
            smooth_ref[:, at_col : at_col + TILE] = piece
            total = total + jnp.sum(piece, axis=1, keepdims=True)
        mean = total / cols
        per_block = GROUP * share
        for step in range(row_count):
            for up in range(upper):
                start = (step * upper + up) * per_block
                centered = smooth_ref[start : start + per_block] - mean[start : start + per_block]
                out_refs[step][group, up] = centered.astype(BF16)


def lowpass(place, raw, near, far, dark, flat, rowband, colband, row_count, upper, share):
    planes, rows, cols = raw.shape
    ext = rows + 2 * HALO
    shape = jax.ShapeDtypeStruct((planes // GROUP, upper, GROUP * share, cols), BF16)
    height = GROUP * rows
    return pl.pallas_call(
        functools.partial(lowpass_kernel, planes, rows, row_count, upper, share),
        out_shape=[shape] * row_count,
        in_specs=[pl.BlockSpec(memory_space=pltpu.SMEM)] + whole(7),
        out_specs=whole(row_count),
        scratch_shapes=[
            pltpu.VMEM((ext, cols), F32),
            pltpu.VMEM((ext, cols), F32),
            pltpu.VMEM((GROUP * ext, cols), BF16),
            pltpu.VMEM((height, cols + 2 * CELL), BF16),
            pltpu.VMEM((height, cols + 2 * CELL), BF16),
            pltpu.VMEM((height, cols), F32),
        ],
        compiler_params=call_params(),
        cost_estimate=pl.CostEstimate(
            flops=2 * planes * rows * cols * 1500, bytes_accessed=planes * rows * cols * 6, transcendentals=planes * ext * cols
        ),
    )(place, raw, near, far, dark, flat, rowband, colband)


def ramp_kernel(cols, out_ref):
    steps = cols // TILE
    for block in range(2 * steps - 1):
        source = lax.broadcasted_iota(jnp.int32, (TILE, TILE), 0) + (block - (steps - 1)) * TILE
        distance = source - lax.broadcasted_iota(jnp.int32, (TILE, TILE), 1)
        spacing = distance.astype(F32)
        falloff = -4.0 / (math.pi * math.pi * jnp.maximum(spacing * spacing, 1.0))
        odd = (distance & 1) != 0
        values = jnp.where(distance == 0, 1.0, jnp.where(odd, falloff, 0.0))
        out_ref[block * TILE : (block + 1) * TILE] = values.astype(BF16)


def finish_kernel(half, share, pad_half, lines_ref, ramp_ref, partner_ref, shifts_ref, out_ref, corr_ref, lead_ref, mate_ref, ls_ref, ms_ref, prof_ref):
    count, cols = lines_ref.shape
    steps = cols // TILE
    for block in range(steps):
        start = (steps - 1 - block) * TILE
        panel = ramp_ref[start : start + cols]
        out_ref[:, block * TILE : (block + 1) * TILE] = jnp.dot(
            lines_ref[...], panel, preferred_element_type=F32
        ).astype(BF16)
    picks = share * pad_half
    pick_at = lax.broadcasted_iota(jnp.int32, (picks, count), 0)
    line_at = lax.broadcasted_iota(jnp.int32, (picks, count), 1)
    row, first = pick_at // pad_half, pick_at % pad_half
    wanted = jnp.where(first < half, first * share + row, -1)
    lead_pick = (line_at == wanted).astype(F32).astype(BF16)
    other = jnp.broadcast_to(partner_ref[...], (picks, count))
    wanted = jnp.where(other >= 0, other * share + row, -1)
    mate_pick = (line_at == wanted).astype(F32).astype(BF16)
    mate_ref[:, :SPAN] = jnp.zeros((picks, SPAN), BF16)
    mate_ref[:, SPAN + cols :] = jnp.zeros((picks, SPAN), BF16)
    for at_col in range(0, cols, TILE):
        piece = lines_ref[:, at_col : at_col + TILE]
        lead_ref[:, at_col : at_col + TILE] = jnp.dot(lead_pick, piece, preferred_element_type=F32).astype(BF16)
        mate_ref[:, SPAN + at_col : SPAN + at_col + TILE] = jnp.dot(
            mate_pick, piece, preferred_element_type=F32
        ).astype(BF16)
    cells = cols // CELL
    width = CELL + 2 * SPAN
    for row in range(share):
        lines = slice(row * pad_half, (row + 1) * pad_half)
        for cell in range(cells):
            ls_ref[cell * pad_half : (cell + 1) * pad_half] = lead_ref[lines, cell * CELL : (cell + 1) * CELL]
            back = (cells - 1 - cell) * CELL
            ms_ref[cell * pad_half : (cell + 1) * pad_half] = mate_ref[lines, back : back + width]
        products = lax.dot_general(
            ls_ref[...], ms_ref[...], (((0,), (0,)), ((), ())), preferred_element_type=F32
        )
        skewed = pltpu.roll(products, 0, 1, stride=1, stride_axis=0)
        prof_ref[row : row + 1] = jnp.sum(skewed[:, CELL:], axis=0, keepdims=True)
    number = shifts_ref.shape[1]
    at = lax.broadcasted_iota(jnp.int32, (2 * SPAN, number), 0)
    selector = (at == SPAN - 1 - shifts_ref[...]).astype(F32)
    picked = jnp.dot(prof_ref[...], selector, precision=lax.Precision.HIGHEST, preferred_element_type=F32)
    corr_ref[...] = picked * (half * cols) ** (-0.5)


def finish(lines, ramp, partner, shifts, share):
    count, cols = lines.shape
    half = partner.shape[0]
    pad_half = -(-half // 16) * 16
    padded = jnp.pad(partner, (0, pad_half - half), constant_values=-1)
    partner_column = jnp.tile(padded, share)[:, None]
    cells = cols // CELL
    return pl.pallas_call(
        functools.partial(finish_kernel, half, share, pad_half),
        out_shape=[
            jax.ShapeDtypeStruct((count, cols), BF16),
            jax.ShapeDtypeStruct((share, shifts.shape[0]), F32),
        ],
        in_specs=whole(4),
        out_specs=whole(2),
        scratch_shapes=[
            pltpu.VMEM((share * pad_half, cols), BF16),
            pltpu.VMEM((share * pad_half, cols + 2 * SPAN), BF16),
            pltpu.VMEM((cells * pad_half, CELL), BF16),
            pltpu.VMEM((cells * pad_half, CELL + 2 * SPAN), BF16),
            pltpu.VMEM((share, 2 * SPAN), F32),
        ],
        compiler_params=call_params(),
    )(lines, ramp, partner_column, shifts[None, :])


def shards(raw_frames, dark_field, flat_field, kernel_taps, partner, shifts):
    planes, rows, cols = raw_frames.shape
    tap_count = kernel_taps.shape[0]
    row_count, ang_count = lax.axis_size("row"), lax.axis_size("ang")
    upper, share = ang_count // row_count, rows // ang_count
    me, turn = lax.axis_index("row"), lax.axis_index("ang")
    odd = me % 2
    inner = jnp.logical_and(me > 0, me < row_count - 1)
    place = jnp.stack([me, inner.astype(jnp.int32)]).astype(jnp.int32)

    def edge(start):
        parts = [raw_frames, dark_field[None], flat_field[None]]
        return jnp.concatenate([lax.dynamic_slice_in_dim(part, start, HALO, 1) for part in parts])

    near = lax.ppermute(edge(jnp.where(odd == 1, 0, rows - HALO)), "row", [(i, i ^ 1) for i in range(row_count)])
    cross = [(i, i + 1) for i in range(1, row_count - 1, 2)]
    far = lax.ppermute(
        edge(jnp.where(odd == 1, rows - HALO, 0)), "row", cross + [(j, i) for i, j in cross]
    )
    ext = rows + 2 * HALO
    rowband, colband = pl.pallas_call(
        functools.partial(band_kernel, tap_count, rows, row_count, upper, share),
        out_shape=[
            jax.ShapeDtypeStruct((2 * GROUP * rows, GROUP * ext), BF16),
            jax.ShapeDtypeStruct((2, TILE + 2 * CELL, TILE), BF16),
        ],
        in_specs=[pl.BlockSpec(memory_space=pltpu.SMEM)] * 2,
        out_specs=whole(2),
        compiler_params=call_params(),
    )(place, kernel_taps)
    ramp = pl.pallas_call(
        functools.partial(ramp_kernel, cols),
        out_shape=jax.ShapeDtypeStruct(((2 * (cols // TILE) - 1) * TILE, TILE), BF16),
        out_specs=whole(1)[0],
        compiler_params=call_params(),
    )()
    sent = lowpass(place, raw_frames, near, far, dark_field, flat_field, rowband, colband, row_count, upper, share)
    held = [sent[0]]
    for step in range(1, row_count):
        held.append(lax.ppermute(sent[step], "row", [(i, i ^ step) for i in range(row_count)]))
    held = jnp.stack(held)
    lines = jnp.zeros((ang_count,) + held.shape[1:2] + held.shape[3:], BF16)
    for step in range(ang_count):
        target = turn ^ step
        piece = lax.dynamic_slice(
            held,
            (me ^ (target // upper), 0, target % upper, 0, 0),
            (1, held.shape[1], 1, held.shape[3], cols),
        ).reshape(lines.shape[1:])
        if step:
            piece = lax.ppermute(piece, "ang", [(i, i ^ step) for i in range(ang_count)])
        lines = lax.dynamic_update_slice_in_dim(lines, piece[None], turn ^ step, 0)
    filtered, correlation = finish(lines.reshape(-1, cols), ramp, partner, shifts, share)
    return filtered.reshape(-1, share, cols), correlation


def solution(mesh):
    in_specs = (
        P(("scan", "ang"), "row", None),
        P("row", None),
        P("row", None),
        P(),
        P("scan"),
        P(),
    )
    out_specs = (P("scan", ("ang", "row"), None), P(("scan", "ang", "row"), None))
    return jax.shard_map(shards, mesh=mesh, in_specs=in_specs, out_specs=out_specs, check_vma=False)
```

time: 517 us -> 113 us (0.22); the launches traced: 509 us -> 113 us
  local copies, waits for them, and re-layouts: 197 us -> 5.63 us
  other arithmetic: 160 us -> 2.65 us
  blocking collectives: 45.9 us -> 0 us
  matrix products: 34.6 us -> 0 us
  Pallas kernels: 0 us -> 22.6 us
  loops' own time: 16.7 us -> 0 us
  waiting for transfers between devices: 43.7 us -> 58.1 us
  starting transfers between devices: 10.5 us -> 22.9 us
    reduce_sum x9 -> x0, other arithmetic: 102 us -> none  [the longest x1 79.4 us: center_lines(): jnp.mean(lowpassed, axis=-1, keepdims=True)]
    reshape x25 -> x1, local copies, waits for them, and re-layouts: 87.8 us -> 1.14 us  [shards(): piece = lax.dynamic_slice(held, (me ^ target // upper, 0, target % upper,...]
    ppermute x2 -> x8, waiting for transfers between devices: 2.34 us -> 58.1 us  [the longest x3 41.5 us: shards(): lax.ppermute(piece, 'ang', [(i, i ^ step) for i in range(ang_count)])]
    add x2 -> x0, other arithmetic: 50.8 us -> none  [the longest x1 50.3 us: column_pass(): summed + kernel_taps[tap_index] * padded[..., tap_index:tap_index + col_c...]
    while x65 -> x0, local copies, waits for them, and re-layouts: 48.1 us -> none
    all_to_all x1 -> x0, blocking collectives: 45.9 us -> none  [shards(): lax.all_to_all(shaped, 'row', split_axis=2, concat_axis=1, tiled=True)]
    all_to_all x1 -> x0, waiting for transfers between devices: 41.4 us -> none  [shards(): lax.all_to_all(across, 'ang', split_axis=1, concat_axis=0, tiled=True)]
    dot_general x10 -> x0, matrix products: 34.6 us -> none  [the longest x1 25.3 us: apply_ramp(): jnp.dot(lines.reshape(-1, col_count), ramp_kernel, preferred_element_type...]
  transfers between devices with their start and end apart: 3 -> 8, of which waited for: 3 -> 4; matrix products, arithmetic and copies ran while one was open for 0% -> 2% of each run, Pallas kernels for 0% -> 3%
where the time goes in v1:
time: 113 us
  waiting for transfers between devices  58.1 us (51%)
  starting transfers between devices  22.9 us (20%)
  Pallas kernels  22.6 us (20%)
  local copies, waits for them, and re-layouts  5.63 us (5%)
  other arithmetic  2.65 us (2%)
    ppermute x3, waiting for transfers between devices, shards(): lax.ppermute(piece, 'ang', [(i, i ^ step) for i in range(ang_count)])  41.5 us
    ppermute x3, starting transfers between devices, shards(): lax.ppermute(sent[step], 'row', [(i, i ^ step) for i in range(row_count)])  18.8 us
    ppermute x3, waiting for transfers between devices, shards(): lax.ppermute(sent[step], 'row', [(i, i ^ step) for i in range(row_count)])  16.6 us
    pallas_call x1, Pallas kernels, finish(): pl.pallas_call(functools.partial(finish_kernel, half, share, pad_half), o...  10.2 us
    pallas_call x1, Pallas kernels, lowpass(): pl.pallas_call(functools.partial(lowpass_kernel, planes, rows, row_count,...  8.56 us
    ppermute x3, starting transfers between devices, shards(): lax.ppermute(piece, 'ang', [(i, i ^ step) for i in range(ang_count)])  2.73 us
    concatenate x2, other arithmetic, edge(): jnp.concatenate([lax.dynamic_slice_in_dim(part, start, HALO, 1) for part...  2.33 us
  transfers between devices with their start and end apart: 8, of which 4 were waited for; matrix products, arithmetic and copies ran while one was open for 2% of the time, Pallas kernels for 3%

profile of v1, /device:TPU:19, one launch (start us, length us, event | category | flops | bytes accessed | tf_op | source)
XLA Modules:
  0.0 112.7 jit_solution(12357245835679448453)
XLA Ops:
  0.7 1.7 %constant_dynamic-slice_fusion = (bf16[12,16,2560]{2,1,0:T(8,128)(2,1)S(1)}, bf16[12,16,2560]{2,1,0:T(8,128)(2,1)S(1)}) fusion(bf16[12,32,2560]{2,1,0:T(8,128)(2,1)} %raw_ref.1, s32[]{:T(128)S(6)} %select_n.63, s32[]{:T(128)S(6)} %select_n.62), kind=kLoop, calls=%fused_computation.14 | loop fusion | bytes 3932168 | tf_op jit(solution)/shard_map/dynamic_slice | solution.py:248
  2.4 1.1 %pad_maximum_fusion.1 = bf16[14,16,2560]{2,1,0:T(8,128)(2,1)} fusion(bf16[1,16,2560]{2,1,0:T(8,128)(2,1)S(1)} %get-tuple-element.26, bf16[1,16,2560]{2,1,0:T(8,128)(2,1)S(1)} %get-tuple-element.27, bf16[12,16,2560]{2,1,0:T(8,128)(2,1)S(1)} %get-tuple-element.22), kind=kLoop, calls=%fused_computation.1 | loop fusion | flops 1146880 | bytes 2293760 | tf_op jit(solution)/shard_map/concatenate | solution.py:248
  3.6 0.7 collective-permute-start
  4.3 1.2 %pad_maximum_fusion.2 = bf16[14,16,2560]{2,1,0:T(8,128)(2,1)} fusion(bf16[1,16,2560]{2,1,0:T(8,128)(2,1)S(1)} %get-tuple-element.25, bf16[1,16,2560]{2,1,0:T(8,128)(2,1)S(1)} %get-tuple-element.28, bf16[12,16,2560]{2,1,0:T(8,128)(2,1)S(1)} %get-tuple-element.21), kind=kLoop, calls=%fused_computation.2 | loop fusion | flops 1146880 | bytes 2293760 | tf_op jit(solution)/shard_map/concatenate | solution.py:248
  5.4 0.7 collective-permute-start.1
  6.2 2.0 %shard_map.77 = (bf16[256,256]{1,0:T(8,128)(2,1)S(1)}, bf16[2,512,256]{2,1,0:T(8,128)(2,1)S(1)}) custom-call(s32[2]{0:T(128)S(1)} %pad_add_fusion.place_ref, f32[31]{0:T(128)S(1)} %copy-done.3), custom_call_target="tpu_custom_call" | custom-call | tf_op jit(solution)/shard_map/pallas_call | solution.py:256
  8.3 8.6 %shard_map.78 = (bf16[3,1,32,2560]{3,2,1,0:T(8,128)(2,1)S(1)}, bf16[3,1,32,2560]{3,2,1,0:T(8,128)(2,1)}, bf16[3,1,32,2560]{3,2,1,0:T(8,128)(2,1)}, bf16[3,1,32,2560]{3,2,1,0:T(8,128)(2,1)}) custom-call(s32[2]{0:T(128)S(1)} %pad_add_fusion.place_ref, bf16[12,32,2560]{2,1,0:T(8,128)(2,1)} %raw_ref.1, bf16[14,16,2560]{2,1,0:T(8,128)(2,1)S(1)} %collective-permute-done.near_ref, ...), custom_call_target="tpu_custom_call" | custom-call | flops 2949120000 | bytes 5898240 | tf_op jit(solution)/shard_map/pallas_call | solution.py:132
  16.9 0.1 collective-permute-start.4
  17.0 18.3 %collective-permute-start.3 = (bf16[3,1,32,2560]{3,2,0,1:T(8,128)(2,1)}, bf16[3,1,32,2560]{3,2,0,1:T(8,128)(2,1)S(1)}, u32[]{:S(2)}, u32[]{:S(2)}) collective-permute-start(bf16[3,1,32,2560]{3,2,0,1:T(8,128)(2,1)} %bitcast.9), channel_id=1, source_target_pairs={{0,2},{1,3},{2,0},{3,1},{4,6},{5,7},{6,4},{7,5},{8,10},{9,11},{10,... | collective-permute-start | bytes 1474568 | tf_op jit(solution)/shard_map/ppermute | solution.py:275
  35.3 0.4 collective-permute-start.2
  35.6 16.6 %collective-permute-done.3 = bf16[3,1,32,2560]{3,2,0,1:T(8,128)(2,1)S(1)} collective-permute-done((bf16[3,1,32,2560]{3,2,0,1:T(8,128)(2,1)}, bf16[3,1,32,2560]{3,2,0,1:T(8,128)(2,1)S(1)}, u32[]{:S(2)}, u32[]{:S(2)}) %collective-permute-start.3) | collective-permute-done | bytes 491552 | tf_op jit(solution)/shard_map/ppermute | solution.py:275
  52.2 0.2 pad_maximum_fusion
  52.5 1.3 %copy-done.4 = bf16[4,3,1,32,2560]{4,3,1,2,0:T(8,128)(2,1)} copy-done((bf16[4,3,1,32,2560]{4,3,1,2,0:T(8,128)(2,1)}, bf16[4,3,1,32,2560]{4,3,1,2,0:T(8,128)(2,1)S(1)}, u32[]{:S(2)}) %copy-start.4) | copy-done | bytes 1966104
  53.7 1.1 %dynamic-slice_bitcast_fusion = (bf16[3,32,2560]{2,1,0:T(8,128)(2,1)}, bf16[3,32,2560]{2,1,0:T(8,128)(2,1)}, bf16[3,32,2560]{2,1,0:T(8,128)(2,1)}) fusion(bf16[4,3,1,32,2560]{4,3,1,2,0:T(8,128)(2,1)S(1)} %pad_maximum_fusion, s32[]{:T(128)S(6)} %select_n.70, s32[]{:T(128)S(6)} %select_n.68, s32[]{:T(128)S(6)} %select_n.66), kind=kLoop, calls=%fused_computation.7 | loop fusion | bytes 2949132 | tf_op jit(solution)/shard_map/reshape | solution.py:284
  54.9 1.3 %collective-permute-start.5 = (bf16[3,32,2560]{2,1,0:T(8,128)(2,1)}, bf16[3,32,2560]{2,1,0:T(8,128)(2,1)S(1)}, u32[]{:S(2)}, u32[]{:S(2)}) collective-permute-start(bf16[3,32,2560]{2,1,0:T(8,128)(2,1)} %get-tuple-element.20), channel_id=1, source_target_pairs={{0,4},{4,0},{8,12},{12,8},{1,5},{5,1},{9,13},{13,9},{2,6},{6,2},{1... | collective-permute-start | bytes 1474568 | tf_op jit(solution)/shard_map/ppermute | solution.py:286
  56.2 1.8 %shard_map.79.ramp_ref = bf16[4864,256]{1,0:T(8,128)(2,1)S(1)} custom-call(), custom_call_target="tpu_custom_call" | custom-call | tf_op jit(solution)/shard_map/pallas_call | solution.py:266
  58.0 0.1 broadcast_in_dim_tile.4.partner_ref
  58.3 1.3 %collective-permute-start.7 = (bf16[3,32,2560]{2,1,0:T(8,128)(2,1)}, bf16[3,32,2560]{2,1,0:T(8,128)(2,1)S(1)}, u32[]{:S(2)}, u32[]{:S(2)}) collective-permute-start(bf16[3,32,2560]{2,1,0:T(8,128)(2,1)} %get-tuple-element.18), channel_id=1, source_target_pairs={{0,12},{4,8},{8,4},{12,0},{1,13},{5,9},{9,5},{13,1},{2,14},{6,10},... | collective-permute-start | bytes 1474568 | tf_op jit(solution)/shard_map/ppermute | solution.py:286
  59.6 0.2 broadcast_in_dim.19
  59.8 1.1 bitcast_dynamic-update-slice_fusion.3
  60.9 13.5 %collective-permute-done.5 = bf16[3,32,2560]{2,1,0:T(8,128)(2,1)S(1)} collective-permute-done((bf16[3,32,2560]{2,1,0:T(8,128)(2,1)}, bf16[3,32,2560]{2,1,0:T(8,128)(2,1)S(1)}, u32[]{:S(2)}, u32[]{:S(2)}) %collective-permute-start.5) | collective-permute-done | bytes 491552 | tf_op jit(solution)/shard_map/ppermute | solution.py:286
  74.4 15.6 %collective-permute-done.6 = bf16[3,32,2560]{2,1,0:T(8,128)(2,1)S(1)} collective-permute-done((bf16[3,32,2560]{2,1,0:T(8,128)(2,1)}, bf16[3,32,2560]{2,1,0:T(8,128)(2,1)S(1)}, u32[]{:S(2)}, u32[]{:S(2)}) %collective-permute-start.6) | collective-permute-done | bytes 491552 | tf_op jit(solution)/shard_map/ppermute | solution.py:286
  90.0 12.4 %collective-permute-done.7 = bf16[3,32,2560]{2,1,0:T(8,128)(2,1)S(1)} collective-permute-done((bf16[3,32,2560]{2,1,0:T(8,128)(2,1)}, bf16[3,32,2560]{2,1,0:T(8,128)(2,1)S(1)}, u32[]{:S(2)}, u32[]{:S(2)}) %collective-permute-start.7) | collective-permute-done | bytes 491552 | tf_op jit(solution)/shard_map/ppermute | solution.py:286
  102.5 10.2 %shard_map.80 = (bf16[384,2560]{1,0:T(8,128)(2,1)}, f32[8,256]{1,0:T(8,128)}) custom-call(bf16[384,2560]{1,0:T(8,128)(2,1)S(1)} %bitcast.33, bf16[4864,256]{1,0:T(8,128)(2,1)S(1)} %shard_map.79.ramp_ref, s32[256,1]{1,0:T(8,128)S(1)} %broadcast_in_dim_tile.4.partner_ref, s32[1,256]{1,0:T(1,128)S(1)} %bitcast.35), custom_call_target="tpu_custom_call" | custom-call | tf_op jit(solution)/shard_map/pallas_call | solution.py:217
  (23 shorter events, 0.4 us)
Async XLA Ops:
  0.6 1.7 %copy-start = (bf16[32,2560]{1,0:T(8,128)(2,1)S(1)}, bf16[32,2560]{1,0:T(8,128)(2,1)}, u32[]{:S(2)}) copy-start(bf16[32,2560]{1,0:T(8,128)(2,1)} %flat_ref.1) | copy-start | bytes 491524
  0.7 1.7 %copy-start.1 = (bf16[32,2560]{1,0:T(8,128)(2,1)S(1)}, bf16[32,2560]{1,0:T(8,128)(2,1)}, u32[]{:S(2)}) copy-start(bf16[32,2560]{1,0:T(8,128)(2,1)} %dark_ref.1) | copy-start | bytes 491524
  2.4 3.8 %copy-start.3 = (f32[31]{0:T(128)S(1)}, f32[31]{0:T(128)}, u32[]{:S(2)}) copy-start(f32[31]{0:T(128)} %taps_ref.1) | copy-start | bytes 376
  3.6 4.7 %collective-permute-start = (bf16[14,16,2560]{2,1,0:T(8,128)(2,1)}, bf16[14,16,2560]{2,1,0:T(8,128)(2,1)S(1)}, u32[]{:S(2)}, u32[]{:S(2)}) collective-permute-start(bf16[14,16,2560]{2,1,0:T(8,128)(2,1)} %pad_maximum_fusion.1), channel_id=1, source_target_pairs={{0,1},{1,0},{2,3},{3,2},{4,5},{5,4},{6,7},{7,6},{8,9},{9,8},{10,11... | collective-permute-start | bytes 3440648 | tf_op jit(solution)/shard_map/ppermute | solution.py:250
  5.4 2.9 %collective-permute-start.1 = (bf16[14,16,2560]{2,1,0:T(8,128)(2,1)}, bf16[14,16,2560]{2,1,0:T(8,128)(2,1)S(1)}, u32[]{:S(2)}, u32[]{:S(2)}) collective-permute-start(bf16[14,16,2560]{2,1,0:T(8,128)(2,1)} %pad_maximum_fusion.2), channel_id=1, source_target_pairs={{1,2},{2,1},{5,6},{6,5},{9,10},{10,9},{13,14},{14,13},{17,18},{18,... | collective-permute-start | bytes 3440648 | tf_op jit(solution)/shard_map/ppermute | solution.py:252
  16.9 18.8 %collective-permute-start.4 = (bf16[3,1,32,2560]{3,2,1,0:T(8,128)(2,1)}, bf16[3,1,32,2560]{3,2,1,0:T(8,128)(2,1)S(1)}, u32[]{:S(2)}, u32[]{:S(2)}) collective-permute-start(bf16[3,1,32,2560]{3,2,1,0:T(8,128)(2,1)} %get-tuple-element.15), channel_id=1, source_target_pairs={{0,3},{1,2},{2,1},{3,0},{4,7},{5,6},{6,5},{7,4},{8,11},{9,10},{10,... | collective-permute-start | bytes 1474568 | tf_op jit(solution)/shard_map/ppermute | solution.py:275
  17.0 35.2 %collective-permute-start.3 = (bf16[3,1,32,2560]{3,2,0,1:T(8,128)(2,1)}, bf16[3,1,32,2560]{3,2,0,1:T(8,128)(2,1)S(1)}, u32[]{:S(2)}, u32[]{:S(2)}) collective-permute-start(bf16[3,1,32,2560]{3,2,0,1:T(8,128)(2,1)} %bitcast.9), channel_id=1, source_target_pairs={{0,2},{1,3},{2,0},{3,1},{4,6},{5,7},{6,4},{7,5},{8,10},{9,11},{10,... | collective-permute-start | bytes 1474568 | tf_op jit(solution)/shard_map/ppermute | solution.py:275
  35.3 16.9 %collective-permute-start.2 = (bf16[3,1,32,2560]{3,2,0,1:T(8,128)(2,1)}, bf16[3,1,32,2560]{3,2,0,1:T(8,128)(2,1)S(1)}, u32[]{:S(2)}, u32[]{:S(2)}) collective-permute-start(bf16[3,1,32,2560]{3,2,0,1:T(8,128)(2,1)} %bitcast.7), channel_id=1, source_target_pairs={{0,1},{1,0},{2,3},{3,2},{4,5},{5,4},{6,7},{7,6},{8,9},{9,8},{10,11... | collective-permute-start | bytes 1474568 | tf_op jit(solution)/shard_map/ppermute | solution.py:275
  52.5 1.3 %copy-start.4 = (bf16[4,3,1,32,2560]{4,3,1,2,0:T(8,128)(2,1)}, bf16[4,3,1,32,2560]{4,3,1,2,0:T(8,128)(2,1)S(1)}, u32[]{:S(2)}) copy-start(bf16[4,3,1,32,2560]{4,3,1,2,0:T(8,128)(2,1)S(1)} %pad_maximum_fusion) | copy-start | bytes 5898244
  54.9 3.1 %copy-start.5 = (s32[24]{0:T(128)S(1)}, s32[24]{0:T(128)}, u32[]{:S(2)}) copy-start(s32[24]{0:T(128)} %param.10) | copy-start | bytes 292
  54.9 19.5 %collective-permute-start.5 = (bf16[3,32,2560]{2,1,0:T(8,128)(2,1)}, bf16[3,32,2560]{2,1,0:T(8,128)(2,1)S(1)}, u32[]{:S(2)}, u32[]{:S(2)}) collective-permute-start(bf16[3,32,2560]{2,1,0:T(8,128)(2,1)} %get-tuple-element.20), channel_id=1, source_target_pairs={{0,4},{4,0},{8,12},{12,8},{1,5},{5,1},{9,13},{13,9},{2,6},{6,2},{1... | collective-permute-start | bytes 1474568 | tf_op jit(solution)/shard_map/ppermute | solution.py:286
  58.2 31.8 %collective-permute-start.6 = (bf16[3,32,2560]{2,1,0:T(8,128)(2,1)}, bf16[3,32,2560]{2,1,0:T(8,128)(2,1)S(1)}, u32[]{:S(2)}, u32[]{:S(2)}) collective-permute-start(bf16[3,32,2560]{2,1,0:T(8,128)(2,1)} %get-tuple-element.19), channel_id=1, source_target_pairs={{0,8},{4,12},{8,0},{12,4},{1,9},{5,13},{9,1},{13,5},{2,10},{6,14},... | collective-permute-start | bytes 1474568 | tf_op jit(solution)/shard_map/ppermute | solution.py:286
  58.3 44.1 %collective-permute-start.7 = (bf16[3,32,2560]{2,1,0:T(8,128)(2,1)}, bf16[3,32,2560]{2,1,0:T(8,128)(2,1)S(1)}, u32[]{:S(2)}, u32[]{:S(2)}) collective-permute-start(bf16[3,32,2560]{2,1,0:T(8,128)(2,1)} %get-tuple-element.18), channel_id=1, source_target_pairs={{0,12},{4,8},{8,4},{12,0},{1,13},{5,9},{9,5},{13,1},{2,14},{6,10},... | collective-permute-start | bytes 1474568 | tf_op jit(solution)/shard_map/ppermute | solution.py:286
  59.8 42.7 %copy-start.2 = (s32[256]{0:T(256)S(1)}, s32[256]{0:T(256)}, u32[]{:S(2)}) copy-start(s32[256]{0:T(256)} %param.11) | copy-start | bytes 3076

commit v2 on v1

v2 whole, which is shorter than its diff:
```python
import functools
import math

import jax
import jax.numpy as jnp
from jax import lax
from jax.experimental import pallas as pl
from jax.experimental.pallas import tpu as pltpu
from jax.sharding import PartitionSpec as P

SPAN = 256
HALO = 16
GROUP = 4
TILE = 256
CELL = 128
VMEM_BYTES = 24 * 1024 * 1024

F32 = jnp.float32
BF16 = jnp.bfloat16


def call_params():
    return pltpu.CompilerParams(vmem_limit_bytes=VMEM_BYTES)


def whole(count):
    return [pl.BlockSpec(memory_space=pltpu.VMEM)] * count


def anywhere(count):
    return [pl.BlockSpec(memory_space=pl.ANY)] * count


def cost(micros):
    return pl.CostEstimate(flops=int(micros * 1.15e9), bytes_accessed=1 << 16, transcendentals=0)


def skipping(kernel, at, count=1):
    return lambda *refs: kernel(*refs[:at], *refs[at + count :])


def split_hi_lo(values):
    high = values.astype(BF16)
    return high, (values - high.astype(F32)).astype(BF16)


def banded(index, taps_ref, tap_count):
    total = jnp.zeros(index.shape, F32)
    for tap in range(tap_count):
        total = jnp.where(index == tap, taps_ref[tap], total)
    return total


def pick_kernel(planes, half, pad_half, share, place_ref, partner_ref, pick_ref):
    turn = place_ref[2]
    picks, count = pick_ref.shape[0] // 2, pick_ref.shape[1]
    pick_at = lax.broadcasted_iota(jnp.int32, (picks, 1), 0)
    row, first = pick_at // pad_half, pick_at % pad_half
    lead_at = jnp.full((picks, 1), -1, jnp.int32)
    mate_at = lead_at

    def stands(plane):
        step = turn ^ (plane // planes)
        return (step * planes + plane % planes) * share

    for plane in range(half):
        here = first == plane
        lead_at = jnp.where(here, stands(plane) + row, lead_at)
        mate_at = jnp.where(here, stands(partner_ref[plane]) + row, mate_at)
    line_at = lax.broadcasted_iota(jnp.int32, (picks, count), 1)
    pick_ref[:picks] = (line_at == lead_at).astype(F32).astype(BF16)
    pick_ref[picks:] = (line_at == mate_at).astype(F32).astype(BF16)


def band_kernel(tap_count, rows, row_count, upper, share, place_ref, taps_ref, rowband_ref, colband_ref):
    me = place_ref[0]
    odd = lax.rem(me, 2)
    margin = tap_count // 2
    ext = rows + 2 * HALO
    height, depth = GROUP * rows, GROUP * ext
    out_at = lax.broadcasted_iota(jnp.int32, (height, depth), 0)
    in_at = lax.broadcasted_iota(jnp.int32, (height, depth), 1)
    line = out_at % share
    plane = (out_at // share) % GROUP
    block = out_at // (share * GROUP)
    step, up = block // upper, block % upper
    row = (up * row_count + (step ^ me)) * share + line
    place = in_at % ext
    straight = place - HALO
    crossed = jnp.where(place < HALO, rows + place, jnp.where(place >= rows + HALO, place - rows - 2 * HALO, straight))
    source = jnp.where(odd == 1, straight, crossed)
    index = jnp.where(in_at // ext == plane, source - row + margin, -1)
    high, low = split_hi_lo(banded(index, taps_ref, tap_count))
    rowband_ref[:height] = high
    rowband_ref[height:] = low
    width = TILE + 2 * CELL
    from_at = lax.broadcasted_iota(jnp.int32, (width, TILE), 0)
    lane = lax.broadcasted_iota(jnp.int32, (width, TILE), 1)
    to_at = jnp.where(lane < CELL, 2 * lane, 2 * (lane - CELL) + 1)
    high, low = split_hi_lo(banded(from_at - CELL - to_at + margin, taps_ref, tap_count))
    colband_ref[0] = high
    colband_ref[1] = low


def edge_kernel(planes, rows, crossing, place_ref, raw_ref, dark_ref, flat_ref, out_ref, sems):
    odd = lax.rem(place_ref[0], 2)
    span = pl.ds(pl.multiple_of((odd if crossing else 1 - odd) * (rows - HALO), HALO), HALO)
    copies = [
        pltpu.make_async_copy(raw_ref.at[:, span], out_ref.at[:planes], sems.at[0]),
        pltpu.make_async_copy(dark_ref.at[span], out_ref.at[planes], sems.at[1]),
        pltpu.make_async_copy(flat_ref.at[span], out_ref.at[planes + 1], sems.at[2]),
    ]
    for copy in copies:
        copy.start()
    for copy in copies:
        copy.wait()


def edge(place, raw, dark, flat, crossing, after):
    planes, rows, cols = raw.shape
    return pl.pallas_call(
        skipping(functools.partial(edge_kernel, planes, rows, crossing), 4, len(after)),
        out_shape=jax.ShapeDtypeStruct((planes + 2, HALO, cols), BF16),
        in_specs=[pl.BlockSpec(memory_space=pltpu.SMEM)] + anywhere(3 + len(after)),
        out_specs=whole(1)[0],
        scratch_shapes=[pltpu.SemaphoreType.DMA((3,))],
        cost_estimate=cost(2.0),
    )(place, raw, dark, flat, *after)


def lowpass_kernel(
    rows, row_count, upper, share, wants_inner,
    place_ref, raw_ref, near_ref, far_ref, near_field_ref, far_field_ref, dark_ref, flat_ref, rowband_ref, colband_ref, *rest
):
    out_refs, (level_ref, dark_all_ref, absorbed_ref, high_ref, low_ref, smooth_ref) = rest[:row_count], rest[row_count:]
    cols = raw_ref.shape[-1]
    ext = rows + 2 * HALO
    height = GROUP * rows
    active = place_ref[1] == wants_inner
    spans = ((0, HALO), (HALO, rows), (HALO + rows, HALO))

    @pl.when(jnp.logical_and(active, pl.program_id(0) == 0))
    def _():
        for (start, size), darkness, brightness in zip(
            spans,
            (near_field_ref[0], dark_ref[...], far_field_ref[0]),
            (near_field_ref[1], flat_ref[...], far_field_ref[1]),
        ):
            darkness = darkness.astype(F32)
            dark_all_ref[start : start + size] = darkness
            level_ref[start : start + size] = jnp.log(brightness.astype(F32) - darkness)
        for pad_ref in (high_ref, low_ref):
            pad_ref[:, :CELL] = jnp.zeros((height, CELL), BF16)
            pad_ref[:, CELL + cols :] = jnp.zeros((height, CELL), BF16)

    @pl.when(active)
    def _():
        for plane in range(GROUP):
            for (start, size), counts_ref in zip(spans, (near_ref, raw_ref, far_ref)):
                place = plane * ext + start
                if start > HALO and not wants_inner:
                    absorbed_ref[place : place + size] = jnp.zeros((size, cols), BF16)
                    continue
                counts = counts_ref[plane].astype(F32)
                absorbed = level_ref[start : start + size] - jnp.log(counts - dark_all_ref[start : start + size])
                absorbed_ref[place : place + size] = absorbed.astype(BF16)
        for at_col in range(0, cols, TILE):
            both = jnp.dot(rowband_ref[...], absorbed_ref[:, at_col : at_col + TILE], preferred_element_type=F32)
            high, low = split_hi_lo(both[:height] + both[height:])
            high_ref[:, CELL + at_col : CELL + at_col + TILE] = high
            low_ref[:, CELL + at_col : CELL + at_col + TILE] = low
        total = jnp.zeros((height, 1), F32)
        for at_col in range(0, cols, TILE):
            window = slice(at_col, at_col + TILE + 2 * CELL)
            piece = (
                jnp.dot(high_ref[:, window], colband_ref[0], preferred_element_type=F32)
                + jnp.dot(low_ref[:, window], colband_ref[0], preferred_element_type=F32)
                + jnp.dot(high_ref[:, window], colband_ref[1], preferred_element_type=F32)
            )
            at_half = at_col // 2
            smooth_ref[:, at_half : at_half + CELL] = piece[:, :CELL]
            smooth_ref[:, cols // 2 + at_half : cols // 2 + at_half + CELL] = piece[:, CELL:]
            total = total + jnp.sum(piece, axis=1, keepdims=True)
        mean = total / cols
        per_block = GROUP * share
        for step in range(row_count):
            for up in range(upper):
                start = (step * upper + up) * per_block
                centered = smooth_ref[start : start + per_block] - mean[start : start + per_block]
                out_refs[step][0, up] = centered.astype(BF16)


def lowpass(place, raw, near, far, dark, flat, rowband, colband, row_count, upper, share, wants_inner, first, groups, after):
    planes, rows, cols = raw.shape
    ext = rows + 2 * HALO
    shape = jax.ShapeDtypeStruct((groups, upper, GROUP * share, cols), BF16)
    height = GROUP * rows
    taken = lambda size: pl.BlockSpec((GROUP, size, cols), lambda group: (group + first, 0, 0))
    fields = pl.BlockSpec((2, HALO, cols), lambda group: (planes // 2, 0, 0))
    return pl.pallas_call(
        skipping(functools.partial(lowpass_kernel, rows, row_count, upper, share, wants_inner), 10, len(after)),
        grid=(groups,),
        out_shape=[shape] * row_count,
        in_specs=[pl.BlockSpec(memory_space=pltpu.SMEM), taken(rows), taken(HALO), taken(HALO), fields, fields] + whole(4) + anywhere(len(after)),
        out_specs=[pl.BlockSpec((1, upper, GROUP * share, cols), lambda group: (group, 0, 0, 0))] * row_count,
        scratch_shapes=[
            pltpu.VMEM((ext, cols), F32),
            pltpu.VMEM((ext, cols), F32),
            pltpu.VMEM((GROUP * ext, cols), BF16),
            pltpu.VMEM((height, cols + 2 * CELL), BF16),
            pltpu.VMEM((height, cols + 2 * CELL), BF16),
            pltpu.VMEM((height, cols), F32),
        ],
        compiler_params=call_params(),
        cost_estimate=cost(2.7 * groups),
    )(place, raw, near, far, near, far, dark, flat, rowband, colband, *after)


def route_kernel(row_count, ang_count, upper, place_ref, *rest):
    slots, targets, sems = rest[:row_count], rest[row_count:-1], rest[-1]
    me, turn = place_ref[0], place_ref[2]
    for step in range(1, ang_count):
        target = turn ^ step
        slot = me ^ (target // upper)
        for number in range(row_count):

            @pl.when(slot == number)
            def _():
                pltpu.make_async_copy(slots[number].at[:, target % upper], targets[step - 1], sems.at[step]).start()

    for step in range(1, ang_count):
        pltpu.make_async_copy(slots[0].at[:, 0], targets[step - 1], sems.at[step]).wait()


def route(place, slots, ang_count, after):
    groups, upper, lines, cols = slots[0].shape
    return pl.pallas_call(
        skipping(functools.partial(route_kernel, len(slots), ang_count, upper), 1 + len(slots)),
        out_shape=[jax.ShapeDtypeStruct((groups, lines, cols), BF16)] * (ang_count - 1),
        in_specs=[pl.BlockSpec(memory_space=pltpu.SMEM)] + anywhere(len(slots) + 1),
        out_specs=whole(ang_count - 1),
        scratch_shapes=[pltpu.SemaphoreType.DMA((ang_count,))],
        cost_estimate=cost(2.0),
    )(place, *slots, after)


def ramp_kernel(cols, to_even_ref, to_odd_ref, weave_ref):
    steps = cols // (2 * TILE)
    for out_ref, parity in ((to_even_ref, 1), (to_odd_ref, -1)):
        for block in range(2 * steps - 1):
            source = lax.broadcasted_iota(jnp.int32, (TILE, TILE), 0) + (block - (steps - 1)) * TILE
            distance = 2 * (source - lax.broadcasted_iota(jnp.int32, (TILE, TILE), 1)) + parity
            spacing = distance.astype(F32)
            falloff = -4.0 / (math.pi * math.pi * (spacing * spacing))
            out_ref[block * TILE : (block + 1) * TILE] = falloff.astype(BF16)
    source = lax.broadcasted_iota(jnp.int32, (TILE, TILE), 0)
    target = lax.broadcasted_iota(jnp.int32, (TILE, TILE), 1)
    place = jnp.where(source < CELL, 2 * source, 2 * (source - CELL) + 1)
    weave_ref[...] = (place == target).astype(F32).astype(BF16)


def ramp_lines(lines, to_even_ref, to_odd_ref, weave_ref, store):
    half = lines.shape[1] // 2
    steps = half // TILE
    for block in range(steps):
        rows = slice((steps - 1 - block) * TILE, (steps - 1 - block) * TILE + half)
        here = slice(block * TILE, (block + 1) * TILE)
        even = lines[:, here].astype(F32) + jnp.dot(
            lines[:, half:], to_even_ref[rows], preferred_element_type=F32
        )
        odd = lines[:, half + block * TILE : half + (block + 1) * TILE].astype(F32) + jnp.dot(
            lines[:, :half], to_odd_ref[rows], preferred_element_type=F32
        )
        even, odd = even.astype(BF16), odd.astype(BF16)
        for part in range(TILE // CELL):
            span = slice(part * CELL, (part + 1) * CELL)
            both = jnp.concatenate([even[:, span], odd[:, span]], axis=1)
            store(
                (TILE // CELL) * block + part, jnp.dot(both, weave_ref[...], preferred_element_type=F32).astype(BF16)
            )


def correlate(share, pad_half, scale, lines, pick_ref, shifts_ref, corr_ref, lead_ref, mate_ref, ls_ref, ms_ref, prof_ref):
    count, cols = lines.shape
    half, reach = cols // 2, SPAN // 2
    padded, width = half + 2 * reach, CELL + 2 * reach
    picks = share * pad_half
    for parity in range(2):
        start = parity * padded
        mate_ref[:, start : start + reach] = jnp.zeros((picks, reach), BF16)
        mate_ref[:, start + reach + half : start + padded] = jnp.zeros((picks, reach), BF16)
        for at_col in range(0, half, TILE):
            here = parity * half + at_col
            picked = jnp.dot(pick_ref[...], lines[:, here : here + TILE], preferred_element_type=F32).astype(BF16)
            lead_ref[:, here : here + TILE] = picked[:picks]
            place = start + reach + at_col
            mate_ref[:, place : place + TILE] = picked[picks:]
    cells = half // CELL
    for row in range(share):
        span = slice(row * pad_half, (row + 1) * pad_half)
        for cell in range(cells):
            stack = slice(cell * pad_half, (cell + 1) * pad_half)
            back = (cells - 1 - cell) * CELL
            for parity in range(2):
                at = parity * half + cell * CELL
                ls_ref[stack, parity * CELL : (parity + 1) * CELL] = lead_ref[span, at : at + CELL]
                at = parity * padded + back
                ms_ref[stack, parity * width : (parity + 1) * width] = mate_ref[span, at : at + width]
        products = lax.dot_general(ls_ref[...], ms_ref[...], (((0,), (0,)), ((), ())), preferred_element_type=F32)
        tables = (
            products[:CELL, :width],
            products[CELL:, width:],
            products[:CELL, width:] + products[CELL:, :width],
        )
        for number, table in enumerate(tables):
            skewed = pltpu.roll(table, 0, 1, stride=1, stride_axis=0)
            prof_ref[row : row + 1, number * width : (number + 1) * width] = jnp.sum(skewed, axis=0, keepdims=True)
    shifts = shifts_ref[...]
    middle = CELL + reach - 1 - lax.shift_right_arithmetic(shifts, 1)
    odd = (shifts & 1) == 1
    wanted = (jnp.where(odd, middle, -1), jnp.where(odd, middle - 1, -1), jnp.where(odd, -1, middle))
    at = lax.broadcasted_iota(jnp.int32, (width, shifts.shape[1]), 0)
    total = jnp.zeros(corr_ref.shape, F32)
    for number, place in enumerate(wanted):
        selector = (at == place).astype(F32).astype(BF16)
        rest = prof_ref[:, number * width : (number + 1) * width]
        for _ in range(3):
            high = rest.astype(BF16)
            total = total + jnp.dot(high, selector, preferred_element_type=F32)
            rest = rest - high.astype(F32)
    corr_ref[...] = total * scale


def finish_kernel(upper, slot_count, ang_count, wants_inner, has_out, has_corr, share, pad_half, scale, *refs):
    refs = list(refs)
    take = lambda count: [refs.pop(0) for _ in range(count)]
    place_ref, *ramp_refs = take(4)
    slots, pieces, (pick_ref, shifts_ref) = take(slot_count), take(ang_count - 1), take(2)
    take(1 if has_out else 0)
    (old_corr_ref,) = take(1) if has_corr else (None,)
    out_ref, corr_ref, x_ref, y_ref, in_sems, out_sems = take(6)
    me, turn = place_ref[0], place_ref[2]
    active = place_ref[3] == wants_inner
    groups = x_ref.shape[0] // ang_count

    @pl.when(active)
    def _():
        for number, slot in enumerate(slots):

            @pl.when(me ^ (turn // upper) == number)
            def _():
                pltpu.make_async_copy(slot.at[:, turn % upper], x_ref.at[:groups], in_sems.at[0]).start()

        copies = [pltpu.make_async_copy(slots[0].at[:, 0], x_ref.at[:groups], in_sems.at[0])]
        for step in range(1, ang_count):
            target = x_ref.at[step * groups : (step + 1) * groups]
            copies.append(pltpu.make_async_copy(pieces[step - 1], target, in_sems.at[step]))
            copies[-1].start()
        for copy in copies:
            copy.wait()
        stands, lines_each, cols = x_ref.shape
        lines = x_ref[...].reshape(stands * lines_each, cols)

        def store(block, values):
            y_ref[:, :, block * TILE : (block + 1) * TILE] = values.reshape(stands, lines_each, TILE)

        ramp_lines(lines, *ramp_refs, store)
        outs = []
        for step in range(ang_count):
            target = out_ref.at[pl.ds((turn ^ step) * groups, groups)]
            outs.append(
                pltpu.make_async_copy(y_ref.at[step * groups : (step + 1) * groups], target, out_sems.at[step])
            )
            outs[-1].start()
        correlate(share, pad_half, scale, lines, pick_ref, shifts_ref, corr_ref, *refs)
        for copy in outs:
            copy.wait()

    @pl.when(jnp.logical_not(active))
    def _():
        corr_ref[...] = old_corr_ref[...] if has_corr else jnp.zeros(corr_ref.shape, F32)


def finish(place, ramp, slots, pieces, picks, out, corr, wants_inner, upper, share, half, after):
    ang_count = len(pieces) + 1
    groups, lines_each, cols = pieces[0].shape
    pad_half = padded_half(half)
    args = [place, *ramp, *slots, *pieces, *picks]
    specs = [pl.BlockSpec(memory_space=pltpu.SMEM)] + whole(3) + anywhere(len(slots) + len(pieces)) + whole(2)
    cells, width = cols // (2 * CELL), CELL + SPAN
    aliases = {}
    if out is not None:
        aliases[len(args)] = 0
        args, specs = args + [out], specs + anywhere(1)
    if corr is not None:
        args, specs = args + [corr], specs + whole(1)
    args, specs = args + [after], specs + anywhere(1)
    kernel = functools.partial(
        finish_kernel, upper, len(slots), ang_count, wants_inner, out is not None, corr is not None, share, pad_half,
        (half * cols) ** (-0.5),
    )
    return pl.pallas_call(
        skipping(kernel, len(args) - 1),
        out_shape=[
            jax.ShapeDtypeStruct((ang_count * groups, lines_each, cols), BF16),
            jax.ShapeDtypeStruct((share, picks[1].shape[1]), F32),
        ],
        in_specs=specs,
        out_specs=anywhere(1) + whole(1),
        scratch_shapes=[
            pltpu.VMEM((groups * ang_count, lines_each, cols), BF16),
            pltpu.VMEM((groups * ang_count, lines_each, cols), BF16),
            pltpu.SemaphoreType.DMA((ang_count,)),
            pltpu.SemaphoreType.DMA((ang_count,)),
            pltpu.VMEM((share * pad_half, cols), BF16),
            pltpu.VMEM((share * pad_half, cols + 2 * SPAN), BF16),
            pltpu.VMEM((cells * pad_half, 2 * CELL), BF16),
            pltpu.VMEM((cells * pad_half, 2 * width), BF16),
            pltpu.VMEM((share, 3 * width), F32),
        ],
        input_output_aliases=aliases,
        compiler_params=call_params(),
        cost_estimate=cost(8.0),
    )(*args)


def padded_half(half):
    return -(-half // 16) * 16


def shards(raw_frames, dark_field, flat_field, kernel_taps, partner, shifts):
    planes, rows, cols = raw_frames.shape
    tap_count = kernel_taps.shape[0]
    half = partner.shape[0]
    row_count, ang_count = lax.axis_size("row"), lax.axis_size("ang")
    upper, share = ang_count // row_count, rows // ang_count
    me, turn = lax.axis_index("row"), lax.axis_index("ang")
    is_inner = lambda at: jnp.logical_and(at > 0, at < row_count - 1).astype(jnp.int32)
    place = jnp.stack([me, is_inner(me), turn, is_inner(turn // upper)]).astype(jnp.int32)

    cross = [(i, i + 1) for i in range(1, row_count - 1, 2)]
    far = edge(place, raw_frames, dark_field, flat_field, True, [])
    near = edge(place, raw_frames, dark_field, flat_field, False, [far])
    far = lax.ppermute(far, "row", cross + [(j, i) for i, j in cross])
    near = lax.ppermute(near, "row", [(i, i ^ 1) for i in range(row_count)])
    ext = rows + 2 * HALO
    rowband, colband = pl.pallas_call(
        functools.partial(band_kernel, tap_count, rows, row_count, upper, share),
        out_shape=[
            jax.ShapeDtypeStruct((2 * GROUP * rows, GROUP * ext), BF16),
            jax.ShapeDtypeStruct((2, TILE + 2 * CELL, TILE), BF16),
        ],
        in_specs=[pl.BlockSpec(memory_space=pltpu.SMEM)] * 2,
        out_specs=whole(2),
        compiler_params=call_params(),
        cost_estimate=cost(2.0),
    )(place, kernel_taps)
    ramp = pl.pallas_call(
        functools.partial(ramp_kernel, cols),
        out_shape=[jax.ShapeDtypeStruct((cols - TILE, TILE), BF16)] * 2 + [jax.ShapeDtypeStruct((TILE, TILE), BF16)],
        out_specs=whole(3),
        compiler_params=call_params(),
        cost_estimate=cost(1.8),
    )()

    total = planes // GROUP
    pad_half = padded_half(half)

    pick = pl.pallas_call(
        functools.partial(pick_kernel, planes, half, pad_half, share),
        out_shape=jax.ShapeDtypeStruct((2 * share * pad_half, ang_count * planes * share), BF16),
        in_specs=[pl.BlockSpec(memory_space=pltpu.SMEM)] * 2,
        out_specs=whole(1)[0],
        compiler_params=call_params(),
        cost_estimate=cost(1.5),
    )(place, partner)
    picks = (pick, shifts[None, :])

    ends = (0, row_count - 1)
    mine = lambda inner, source: (source in ends) != bool(inner)

    def filter_rows(inner, after):
        sent = lowpass(
            place, raw_frames, near, far if inner else near, dark_field, flat_field, rowband, colband,
            row_count, upper, share, inner, 0, total, after,
        )
        slots = [sent[0]]
        for step in range(1, row_count):
            pairs = [(i, i ^ step) for i in range(row_count) if mine(inner, i)]
            slots.append(lax.ppermute(sent[step], "row", pairs))
        return slots

    def regroup(inner, slots, after):
        pieces = list(route(place, slots, ang_count, after))
        for step in range(1, ang_count):
            pairs = [(i, i ^ step) for i in range(ang_count) if mine(inner, (i ^ step) // upper)]
            pieces[step - 1] = lax.ppermute(pieces[step - 1], "ang", pairs)
        return pieces

    outer = filter_rows(0, [])
    inner = filter_rows(1, [outer[0], ramp[0], pick])
    outer_lines = regroup(0, outer, inner[0])
    inner_lines = regroup(1, inner, inner[0])
    out, corr = finish(place, ramp, outer, outer_lines, picks, None, None, 0, upper, share, half, inner[0])
    filtered, correlation = finish(place, ramp, inner, inner_lines, picks, out, corr, 1, upper, share, half, corr)
    return filtered.reshape(-1, share, cols), correlation


def solution(mesh):
    in_specs = (
        P(("scan", "ang"), "row", None),
        P("row", None),
        P("row", None),
        P(),
        P("scan"),
        P(),
    )
    out_specs = (P("scan", ("ang", "row"), None), P(("scan", "ang", "row"), None))
    return jax.shard_map(shards, mesh=mesh, in_specs=in_specs, out_specs=out_specs, check_vma=False)
```

time: 113 us -> 104 us (0.920); the launches traced: 113 us -> 102 us
  waiting for transfers between devices: 58.1 us -> 31.7 us
  Pallas kernels: 22.6 us -> 37 us
  local copies, waits for them, and re-layouts: 5.63 us -> 10.8 us
  other arithmetic: 2.65 us -> 0.56 us
  starting transfers between devices: 22.9 us -> 20.9 us
    ppermute x8 -> x14, waiting for transfers between devices: 58.1 us -> 31.7 us  [the longest x6 29.1 us: regroup(): pieces[step - 1] = lax.ppermute(pieces[step - 1], 'ang', pairs)]
    pallas_call x3 -> x10, Pallas kernels: 20.5 us -> 34.9 us  [the longest x2 12 us: finish(): pl.pallas_call(skipping(kernel, len(args) - 1), out_shape=[jax.ShapeDtype...]
    unnamed x12 -> x64, local copies, waits for them, and re-layouts: 1.29 us -> 10.8 us
    concatenate x2 -> x0, other arithmetic: 2.33 us -> none  [edge(): jnp.concatenate([lax.dynamic_slice_in_dim(part, start, HALO, 1) for part...]
    ppermute x8 -> x14, starting transfers between devices: 22.9 us -> 20.9 us  [the longest x6 11.4 us: regroup(): pieces[step - 1] = lax.ppermute(pieces[step - 1], 'ang', pairs)]
    dynamic_slice x2 -> x0, local copies, waits for them, and re-layouts: 1.71 us -> none  [edge(): lax.dynamic_slice_in_dim(part, start, HALO, 1)]
    dynamic_update_slice x4 -> x0, local copies, waits for them, and re-layouts: 1.18 us -> none  [shards(): lines = lax.dynamic_update_slice_in_dim(lines, piece[None], turn ^ step, 0)]
    reshape x1 -> x0, local copies, waits for them, and re-layouts: 1.14 us -> none  [shards(): piece = lax.dynamic_slice(held, (me ^ target // upper, 0, target % upper,...]
  transfers between devices with their start and end apart: 8 -> 14, of which waited for: 4 -> 3; matrix products, arithmetic and copies ran while one was open for 2% -> 0% of each run, Pallas kernels for 3% -> 20%
where the time goes in v2:
time: 104 us; the launch traced here: 102 us
  Pallas kernels  37 us (36%)
  waiting for transfers between devices  31.7 us (30%)
  starting transfers between devices  20.9 us (20%)
  local copies, waits for them, and re-layouts  10.8 us (10%)
  between operations  1.3 us (1%)
    ppermute x6, waiting for transfers between devices, regroup(): pieces[step - 1] = lax.ppermute(pieces[step - 1], 'ang', pairs)  29.1 us
    pallas_call x2, Pallas kernels, finish(): pl.pallas_call(skipping(kernel, len(args) - 1), out_shape=[jax.ShapeDtype...  12 us
    ppermute x6, starting transfers between devices, regroup(): pieces[step - 1] = lax.ppermute(pieces[step - 1], 'ang', pairs)  11.4 us
    unnamed x64, local copies, waits for them, and re-layouts  10.8 us
    pallas_call x2, Pallas kernels, lowpass(): pl.pallas_call(skipping(functools.partial(lowpass_kernel, rows, row_count...  8.61 us
    ppermute x6, starting transfers between devices, filter_rows(): slots.append(lax.ppermute(sent[step], 'row', pairs))  7.98 us
    pallas_call x2, Pallas kernels, route(): pl.pallas_call(skipping(functools.partial(route_kernel, len(slots), ang_c...  6.4 us
    pallas_call x2, Pallas kernels, edge(): pl.pallas_call(skipping(functools.partial(edge_kernel, planes, rows, cros...  5.83 us
  transfers between devices with their start and end apart: 14, of which 3 were waited for; matrix products, arithmetic and copies ran while one was open for 0% of the time, Pallas kernels for 20%

profile of v2, /device:TPU:19, one launch (start us, length us, event | category | flops | bytes accessed | tf_op | source)
XLA Modules:
  0.0 102.2 jit_solution(8575321188638297760)
XLA Ops:
  1.2 2.9 %shard_map.78.refs_4_ = bf16[14,16,2560]{2,1,0:T(8,128)(2,1)} custom-call(s32[4]{0:T(128)} %pad_add_fusion.refs_0_.place_ref, bf16[12,32,2560]{2,1,0:T(8,128)(2,1)} %refs_1_.7, bf16[32,2560]{1,0:T(8,128)(2,1)} %refs_6_.3, bf16[32,2560]{1,0:T(8,128)(2,1)} %refs_7_.3), custom_call_target="tpu_custom_call" | custom-call | flops 2300000000 | bytes 65536 | tf_op jit(solution)/shard_map/pallas_call | solution.py:121
  4.1 2.9 %shard_map.79 = bf16[14,16,2560]{2,1,0:T(8,128)(2,1)} custom-call(s32[4]{0:T(128)} %pad_add_fusion.refs_0_.place_ref, bf16[12,32,2560]{2,1,0:T(8,128)(2,1)} %refs_1_.7, bf16[32,2560]{1,0:T(8,128)(2,1)} %refs_6_.3, bf16[32,2560]{1,0:T(8,128)(2,1)} %refs_7_.3, bf16[14,16,2560]{2,1,0:T(8,128)(2,1)} %shard_map.78.refs_4_), custom_call_target="tpu_custom_call" | custom-call | flops 2300000000 | bytes 65536 | tf_op jit(solution)/shard_map/pallas_call | solution.py:121
  8.5 1.3 %shard_map.77 = (bf16[2304,256]{1,0:T(8,128)(2,1)S(1)}, bf16[2304,256]{1,0:T(8,128)(2,1)S(1)}, bf16[256,256]{1,0:T(8,128)(2,1)S(1)}) custom-call(), custom_call_target="tpu_custom_call" | custom-call | flops 2070000000 | bytes 65536 | tf_op jit(solution)/shard_map/pallas_call | solution.py:458
  11.8 2.1 %shard_map.80 = (bf16[256,256]{1,0:T(8,128)(2,1)S(1)}, bf16[2,512,256]{2,1,0:T(8,128)(2,1)S(1)}) custom-call(s32[4]{0:T(128)S(1)} %copy-done, f32[31]{0:T(128)S(1)} %copy-done.19), custom_call_target="tpu_custom_call" | custom-call | flops 2300000000 | bytes 65536 | tf_op jit(solution)/shard_map/pallas_call | solution.py:447
  13.9 6.4 %shard_map.81 = (bf16[3,1,32,2560]{3,2,1,0:T(8,128)(2,1)S(1)}, bf16[3,1,32,2560]{3,2,1,0:T(8,128)(2,1)S(1)}, bf16[3,1,32,2560]{3,2,1,0:T(8,128)(2,1)S(1)}, bf16[3,1,32,2560]{3,2,1,0:T(8,128)(2,1)S(1)}) custom-call(s32[4]{0:T(128)S(1)} %copy-done, bf16[12,32,2560]{2,1,0:T(8,128)(2,1)S(1)} %copy-done.2, ...), custom_call_target="tpu_custom_call" | custom-call | flops 9315000320 | bytes 65536 | tf_op jit(solution)/shard_map/pallas_call | solution.py:200
  20.3 2.1 %collective-permute-start.10 = (bf16[3,1,32,2560]{3,2,1,0:T(8,128)(2,1)S(1)}, bf16[3,1,32,2560]{3,2,1,0:T(8,128)(2,1)S(1)}, u32[]{:S(2)}, u32[]{:S(2)}) collective-permute-start(bf16[3,1,32,2560]{3,2,1,0:T(8,128)(2,1)S(1)} %get-tuple-element.40), channel_id=1, source_target_pairs={{0,3},{3,0},{4,7},{7,4},{8,11},{11,8},{12,15},{15,12},{16,19},{19,... | collective-permute-start | bytes 1474568 | tf_op jit(solution)/shard_map/ppermute | solution.py:490
  22.4 1.3 %collective-permute-start.8 = (bf16[3,1,32,2560]{3,2,1,0:T(8,128)(2,1)S(1)}, bf16[3,1,32,2560]{3,2,1,0:T(8,128)(2,1)S(1)}, u32[]{:S(2)}, u32[]{:S(2)}) collective-permute-start(bf16[3,1,32,2560]{3,2,1,0:T(8,128)(2,1)S(1)} %get-tuple-element.38), channel_id=1, source_target_pairs={{0,1},{3,2},{4,5},{7,6},{8,9},{11,10},{12,13},{15,14},{16,17},{19,... | collective-permute-start | bytes 1474568 | tf_op jit(solution)/shard_map/ppermute | solution.py:490
  23.7 1.3 %collective-permute-start.9 = (bf16[3,1,32,2560]{3,2,1,0:T(8,128)(2,1)S(1)}, bf16[3,1,32,2560]{3,2,1,0:T(8,128)(2,1)S(1)}, u32[]{:S(2)}, u32[]{:S(2)}) collective-permute-start(bf16[3,1,32,2560]{3,2,1,0:T(8,128)(2,1)S(1)} %get-tuple-element.39), channel_id=1, source_target_pairs={{0,2},{3,1},{4,6},{7,5},{8,10},{11,9},{12,14},{15,13},{16,18},{19,... | collective-permute-start | bytes 1474568 | tf_op jit(solution)/shard_map/ppermute | solution.py:490
  25.1 2.2 %shard_map.83 = (bf16[3,1,32,2560]{3,2,1,0:T(8,128)(2,1)S(1)}, bf16[3,1,32,2560]{3,2,1,0:T(8,128)(2,1)}, bf16[3,1,32,2560]{3,2,1,0:T(8,128)(2,1)}, bf16[3,1,32,2560]{3,2,1,0:T(8,128)(2,1)}) custom-call(s32[4]{0:T(128)S(1)} %copy-done, bf16[12,32,2560]{2,1,0:T(8,128)(2,1)S(1)} %copy-done.2, ...), custom_call_target="tpu_custom_call" | custom-call | flops 9315000320 | bytes 65536 | tf_op jit(solution)/shard_map/pallas_call | solution.py:200
  28.1 1.3 %collective-permute-start.2 = (bf16[3,1,32,2560]{3,2,1,0:T(8,128)(2,1)}, bf16[3,1,32,2560]{3,2,1,0:T(8,128)(2,1)S(1)}, u32[]{:S(2)}, u32[]{:S(2)}) collective-permute-start(bf16[3,1,32,2560]{3,2,1,0:T(8,128)(2,1)} %get-tuple-element.32), channel_id=1, source_target_pairs={{1,0},{2,3},{5,4},{6,7},{9,8},{10,11},{13,12},{14,15},{17,16},{18,... | collective-permute-start | bytes 1474568 | tf_op jit(solution)/shard_map/ppermute | solution.py:490
  29.4 1.3 %collective-permute-start.3 = (bf16[3,1,32,2560]{3,2,1,0:T(8,128)(2,1)}, bf16[3,1,32,2560]{3,2,1,0:T(8,128)(2,1)S(1)}, u32[]{:S(2)}, u32[]{:S(2)}) collective-permute-start(bf16[3,1,32,2560]{3,2,1,0:T(8,128)(2,1)} %get-tuple-element.33), channel_id=1, source_target_pairs={{1,3},{2,0},{5,7},{6,4},{9,11},{10,8},{13,15},{14,12},{17,19},{18,... | collective-permute-start | bytes 1474568 | tf_op jit(solution)/shard_map/ppermute | solution.py:490
  31.4 2.6 %collective-permute-done.9.refs_3_.refs_6_ = bf16[3,1,32,2560]{3,2,1,0:T(8,128)(2,1)S(1)} collective-permute-done((bf16[3,1,32,2560]{3,2,1,0:T(8,128)(2,1)S(1)}, bf16[3,1,32,2560]{3,2,1,0:T(8,128)(2,1)S(1)}, u32[]{:S(2)}, u32[]{:S(2)}) %collective-permute-start.9) | collective-permute-done | bytes 491552 | tf_op jit(solution)/shard_map/ppermute | solution.py:490
  34.9 3.2 %shard_map.85 = (bf16[3,32,2560]{2,1,0:T(8,128)(2,1)}, bf16[3,32,2560]{2,1,0:T(8,128)(2,1)}, bf16[3,32,2560]{2,1,0:T(8,128)(2,1)}) custom-call(s32[4]{0:T(128)} %pad_add_fusion.refs_0_.place_ref, bf16[3,1,32,2560]{3,2,1,0:T(8,128)(2,1)} %copy-done.26, bf16[3,1,32,2560]{3,2,1,0:T(8,128)(2,1)} %copy-done.9, bf16[3,1,32,2560]{3,2,1,0:T(8,128)(2,1)} %copy-done.11, ...), custom_call_target="tpu_custom_call" | custom-call | flops 2300000000 | bytes 65536 | tf_op jit(solution)/shard_map/pallas_call | solution.py:237
  38.1 3.2 %collective-permute-start.11 = (bf16[3,32,2560]{2,1,0:T(8,128)(2,1)}, bf16[3,32,2560]{2,1,0:T(8,128)(2,1)S(1)}, u32[]{:S(2)}, u32[]{:S(2)}) collective-permute-start(bf16[3,32,2560]{2,1,0:T(8,128)(2,1)} %get-tuple-element.41), channel_id=1, source_target_pairs={{4,0},{8,12},{5,1},{9,13},{6,2},{10,14},{7,3},{11,15},{20,16},{24,... | collective-permute-start | bytes 1474568 | tf_op jit(solution)/shard_map/ppermute | solution.py:497
  41.3 2.1 %collective-permute-start.12 = (bf16[3,32,2560]{2,1,0:T(8,128)(2,1)}, bf16[3,32,2560]{2,1,0:T(8,128)(2,1)}, u32[]{:S(2)}, u32[]{:S(2)}) collective-permute-start(bf16[3,32,2560]{2,1,0:T(8,128)(2,1)} %get-tuple-element.42), channel_id=1, source_target_pairs={{4,12},{8,0},{5,13},{9,1},{6,14},{10,2},{7,15},{11,3},{20,28},{24,... | collective-permute-start | bytes 1474568 | tf_op jit(solution)/shard_map/ppermute | solution.py:497
  43.4 1.6 %collective-permute-start.13 = (bf16[3,32,2560]{2,1,0:T(8,128)(2,1)}, bf16[3,32,2560]{2,1,0:T(8,128)(2,1)}, u32[]{:S(2)}, u32[]{:S(2)}) collective-permute-start(bf16[3,32,2560]{2,1,0:T(8,128)(2,1)} %get-tuple-element.43), channel_id=1, source_target_pairs={{0,12},{12,0},{1,13},{13,1},{2,14},{14,2},{3,15},{15,3},{16,28},{2... | collective-permute-start | bytes 1474568 | tf_op jit(solution)/shard_map/ppermute | solution.py:497
  46.6 3.2 %shard_map.84 = (bf16[3,32,2560]{2,1,0:T(8,128)(2,1)}, bf16[3,32,2560]{2,1,0:T(8,128)(2,1)}, bf16[3,32,2560]{2,1,0:T(8,128)(2,1)}) custom-call(s32[4]{0:T(128)} %pad_add_fusion.refs_0_.place_ref, bf16[3,1,32,2560]{3,2,1,0:T(8,128)(2,1)} %copy-done.24, bf16[3,1,32,2560]{3,2,1,0:T(8,128)(2,1)} %copy-done.3, bf16[3,1,32,2560]{3,2,1,0:T(8,128)(2,1)} %copy-done.7, ...), custom_call_target="tpu_custom_call" | custom-call | flops 2300000000 | bytes 65536 | tf_op jit(solution)/shard_map/pallas_call | solution.py:237
  49.8 1.3 %collective-permute-start.5 = (bf16[3,32,2560]{2,1,0:T(8,128)(2,1)}, bf16[3,32,2560]{2,1,0:T(8,128)(2,1)S(1)}, u32[]{:S(2)}, u32[]{:S(2)}) collective-permute-start(bf16[3,32,2560]{2,1,0:T(8,128)(2,1)} %get-tuple-element.35), channel_id=1, source_target_pairs={{0,4},{12,8},{1,5},{13,9},{2,6},{14,10},{3,7},{15,11},{16,20},{28,... | collective-permute-start | bytes 1474568 | tf_op jit(solution)/shard_map/ppermute | solution.py:497
  51.1 1.3 %collective-permute-start.6 = (bf16[3,32,2560]{2,1,0:T(8,128)(2,1)}, bf16[3,32,2560]{2,1,0:T(8,128)(2,1)S(1)}, u32[]{:S(2)}, u32[]{:S(2)}) collective-permute-start(bf16[3,32,2560]{2,1,0:T(8,128)(2,1)} %get-tuple-element.36), channel_id=1, source_target_pairs={{0,8},{12,4},{1,9},{13,5},{2,10},{14,6},{3,11},{15,7},{16,24},{28,... | collective-permute-start | bytes 1474568 | tf_op jit(solution)/shard_map/ppermute | solution.py:497
  52.4 18.9 %collective-permute-done.11.refs_8_ = bf16[3,32,2560]{2,1,0:T(8,128)(2,1)S(1)} collective-permute-done((bf16[3,32,2560]{2,1,0:T(8,128)(2,1)}, bf16[3,32,2560]{2,1,0:T(8,128)(2,1)S(1)}, u32[]{:S(2)}, u32[]{:S(2)}) %collective-permute-start.11) | collective-permute-done | bytes 491552 | tf_op jit(solution)/shard_map/ppermute | solution.py:497
  71.3 1.9 %collective-permute-start.7 = (bf16[3,32,2560]{2,1,0:T(8,128)(2,1)}, bf16[3,32,2560]{2,1,0:T(8,128)(2,1)S(1)}, u32[]{:S(2)}, u32[]{:S(2)}) collective-permute-start(bf16[3,32,2560]{2,1,0:T(8,128)(2,1)} %get-tuple-element.37), channel_id=1, source_target_pairs={{4,8},{8,4},{5,9},{9,5},{6,10},{10,6},{7,11},{11,7},{20,24},{24,20... | collective-permute-start | bytes 1474568 | tf_op jit(solution)/shard_map/ppermute | solution.py:497
  74.6 1.3 %copy-done.23 = bf16[2304,256]{1,0:T(8,128)(2,1)S(1)} copy-done((bf16[2304,256]{1,0:T(8,128)(2,1)S(1)}, bf16[2304,256]{1,0:T(8,128)(2,1)}, u32[]{:S(2)}) %copy-start.23) | copy-done | bytes 1179672
  80.7 10.2 %collective-permute-done.7.refs_10_ = bf16[3,32,2560]{2,1,0:T(8,128)(2,1)S(1)} collective-permute-done((bf16[3,32,2560]{2,1,0:T(8,128)(2,1)}, bf16[3,32,2560]{2,1,0:T(8,128)(2,1)S(1)}, u32[]{:S(2)}, u32[]{:S(2)}) %collective-permute-start.7) | collective-permute-done | bytes 491552 | tf_op jit(solution)/shard_map/ppermute | solution.py:497
  90.9 11.1 %shard_map.87 = (bf16[12,32,2560]{2,1,0:T(8,128)(2,1)}, f32[8,256]{1,0:T(8,128)}) custom-call(s32[4]{0:T(128)S(1)} %copy-done.1, bf16[2304,256]{1,0:T(8,128)(2,1)S(1)} %copy-done.21, bf16[2304,256]{1,0:T(8,128)(2,1)S(1)} %copy-done.23, bf16[256,256]{1,0:T(8,128)(2,1)S(1)} %copy-done.31, ...), custom_call_target="tpu_custom_call", output_to_operand_aliasing={{0}: (13, {})} | custom-call | flops 9200000000 | bytes 65536 | tf_op jit(solution)/shard_map/pallas_call | solution.py:402
  (80 shorter events, 13.9 us)
Async XLA Ops:
  7.1 6.8 %collective-permute-start = (bf16[14,16,2560]{2,1,0:T(8,128)(2,1)}, bf16[14,16,2560]{2,1,0:T(8,128)(2,1)S(1)}, u32[]{:S(2)}, u32[]{:S(2)}) collective-permute-start(bf16[14,16,2560]{2,1,0:T(8,128)(2,1)} %shard_map.79), channel_id=1, source_target_pairs={{0,1},{1,0},{2,3},{3,2},{4,5},{5,4},{6,7},{7,6},{8,9},{9,8},{10,11... | collective-permute-start | bytes 3440648 | tf_op jit(solution)/shard_map/ppermute | solution.py:445
  7.8 17.3 %collective-permute-start.1 = (bf16[14,16,2560]{2,1,0:T(8,128)(2,1)}, bf16[14,16,2560]{2,1,0:T(8,128)(2,1)S(1)}, u32[]{:S(2)}, u32[]{:S(2)}) collective-permute-start(bf16[14,16,2560]{2,1,0:T(8,128)(2,1)} %shard_map.78.refs_4_), channel_id=1, source_target_pairs={{1,2},{2,1},{5,6},{6,5},{9,10},{10,9},{13,14},{14,13},{17,18},{18,... | collective-permute-start | bytes 3440648 | tf_op jit(solution)/shard_map/ppermute | solution.py:444
  10.9 14.2 %copy-start.20 = (bf16[2304,256]{1,0:T(8,128)(2,1)}, bf16[2304,256]{1,0:T(8,128)(2,1)S(1)}, u32[]{:S(2)}) copy-start(bf16[2304,256]{1,0:T(8,128)(2,1)S(1)} %get-tuple-element.25.refs_11_.refs_1_) | copy-start | bytes 3538948
  11.8 13.3 %copy-start.28 = (bf16[512,384]{1,0:T(8,128)(2,1)}, bf16[512,384]{1,0:T(8,128)(2,1)S(1)}, u32[]{:S(2)}) copy-start(bf16[512,384]{1,0:T(8,128)(2,1)S(1)} %shard_map.82.refs_12_.refs_11_) | copy-start | bytes 1179652
  20.3 10.4 %collective-permute-start.10 = (bf16[3,1,32,2560]{3,2,1,0:T(8,128)(2,1)S(1)}, bf16[3,1,32,2560]{3,2,1,0:T(8,128)(2,1)S(1)}, u32[]{:S(2)}, u32[]{:S(2)}) collective-permute-start(bf16[3,1,32,2560]{3,2,1,0:T(8,128)(2,1)S(1)} %get-tuple-element.40), channel_id=1, source_target_pairs={{0,3},{3,0},{4,7},{7,4},{8,11},{11,8},{12,15},{15,12},{16,19},{19,... | collective-permute-start | bytes 1474568 | tf_op jit(solution)/shard_map/ppermute | solution.py:490
  22.4 9.0 %collective-permute-start.8 = (bf16[3,1,32,2560]{3,2,1,0:T(8,128)(2,1)S(1)}, bf16[3,1,32,2560]{3,2,1,0:T(8,128)(2,1)S(1)}, u32[]{:S(2)}, u32[]{:S(2)}) collective-permute-start(bf16[3,1,32,2560]{3,2,1,0:T(8,128)(2,1)S(1)} %get-tuple-element.38), channel_id=1, source_target_pairs={{0,1},{3,2},{4,5},{7,6},{8,9},{11,10},{12,13},{15,14},{16,17},{19,... | collective-permute-start | bytes 1474568 | tf_op jit(solution)/shard_map/ppermute | solution.py:490
  23.7 10.3 %collective-permute-start.9 = (bf16[3,1,32,2560]{3,2,1,0:T(8,128)(2,1)S(1)}, bf16[3,1,32,2560]{3,2,1,0:T(8,128)(2,1)S(1)}, u32[]{:S(2)}, u32[]{:S(2)}) collective-permute-start(bf16[3,1,32,2560]{3,2,1,0:T(8,128)(2,1)S(1)} %get-tuple-element.39), channel_id=1, source_target_pairs={{0,2},{3,1},{4,6},{7,5},{8,10},{11,9},{12,14},{15,13},{16,18},{19,... | collective-permute-start | bytes 1474568 | tf_op jit(solution)/shard_map/ppermute | solution.py:490
  28.1 15.3 %collective-permute-start.2 = (bf16[3,1,32,2560]{3,2,1,0:T(8,128)(2,1)}, bf16[3,1,32,2560]{3,2,1,0:T(8,128)(2,1)S(1)}, u32[]{:S(2)}, u32[]{:S(2)}) collective-permute-start(bf16[3,1,32,2560]{3,2,1,0:T(8,128)(2,1)} %get-tuple-element.32), channel_id=1, source_target_pairs={{1,0},{2,3},{5,4},{6,7},{9,8},{10,11},{13,12},{14,15},{17,16},{18,... | collective-permute-start | bytes 1474568 | tf_op jit(solution)/shard_map/ppermute | solution.py:490
  29.4 15.6 %collective-permute-start.3 = (bf16[3,1,32,2560]{3,2,1,0:T(8,128)(2,1)}, bf16[3,1,32,2560]{3,2,1,0:T(8,128)(2,1)S(1)}, u32[]{:S(2)}, u32[]{:S(2)}) collective-permute-start(bf16[3,1,32,2560]{3,2,1,0:T(8,128)(2,1)} %get-tuple-element.33), channel_id=1, source_target_pairs={{1,3},{2,0},{5,7},{6,4},{9,11},{10,8},{13,15},{14,12},{17,19},{18,... | collective-permute-start | bytes 1474568 | tf_op jit(solution)/shard_map/ppermute | solution.py:490
  30.7 14.3 %collective-permute-start.4 = (bf16[3,1,32,2560]{3,2,1,0:T(8,128)(2,1)}, bf16[3,1,32,2560]{3,2,1,0:T(8,128)(2,1)S(1)}, u32[]{:S(2)}, u32[]{:S(2)}) collective-permute-start(bf16[3,1,32,2560]{3,2,1,0:T(8,128)(2,1)} %get-tuple-element.34), channel_id=1, source_target_pairs={{1,2},{2,1},{5,6},{6,5},{9,10},{10,9},{13,14},{14,13},{17,18},{18,... | collective-permute-start | bytes 1474568 | tf_op jit(solution)/shard_map/ppermute | solution.py:490
  38.1 33.2 %collective-permute-start.11 = (bf16[3,32,2560]{2,1,0:T(8,128)(2,1)}, bf16[3,32,2560]{2,1,0:T(8,128)(2,1)S(1)}, u32[]{:S(2)}, u32[]{:S(2)}) collective-permute-start(bf16[3,32,2560]{2,1,0:T(8,128)(2,1)} %get-tuple-element.41), channel_id=1, source_target_pairs={{4,0},{8,12},{5,1},{9,13},{6,2},{10,14},{7,3},{11,15},{20,16},{24,... | collective-permute-start | bytes 1474568 | tf_op jit(solution)/shard_map/ppermute | solution.py:497
  41.3 31.9 %collective-permute-start.12 = (bf16[3,32,2560]{2,1,0:T(8,128)(2,1)}, bf16[3,32,2560]{2,1,0:T(8,128)(2,1)}, u32[]{:S(2)}, u32[]{:S(2)}) collective-permute-start(bf16[3,32,2560]{2,1,0:T(8,128)(2,1)} %get-tuple-element.42), channel_id=1, source_target_pairs={{4,12},{8,0},{5,13},{9,1},{6,14},{10,2},{7,15},{11,3},{20,28},{24,... | collective-permute-start | bytes 1474568 | tf_op jit(solution)/shard_map/ppermute | solution.py:497
  43.4 29.8 %copy-start.1 = (s32[4]{0:T(128)S(1)}, s32[4]{0:T(128)}, u32[]{:S(2)}) copy-start(s32[4]{0:T(128)} %pad_add_fusion.refs_0_.place_ref) | copy-start | bytes 52
  43.4 29.8 %copy-start.6 = (bf16[3,1,32,2560]{3,2,1,0:T(8,128)(2,1)S(1)}, bf16[3,1,32,2560]{3,2,1,0:T(8,128)(2,1)}, u32[]{:S(2)}) copy-start(bf16[3,1,32,2560]{3,2,1,0:T(8,128)(2,1)} %copy-done.5) | copy-start | bytes 1474564
  43.4 29.9 %copy-start.10 = (bf16[3,1,32,2560]{3,2,1,0:T(8,128)(2,1)S(1)}, bf16[3,1,32,2560]{3,2,1,0:T(8,128)(2,1)}, u32[]{:S(2)}) copy-start(bf16[3,1,32,2560]{3,2,1,0:T(8,128)(2,1)} %copy-done.9) | copy-start | bytes 1474564
  43.4 29.9 %copy-start.12 = (bf16[3,1,32,2560]{3,2,1,0:T(8,128)(2,1)S(1)}, bf16[3,1,32,2560]{3,2,1,0:T(8,128)(2,1)}, u32[]{:S(2)}) copy-start(bf16[3,1,32,2560]{3,2,1,0:T(8,128)(2,1)} %copy-done.11) | copy-start | bytes 1474564
  43.4 29.9 %copy-start.17 = (s32[256]{0:T(256)S(1)}, s32[256]{0:T(256)}, u32[]{:S(2)}) copy-start(s32[256]{0:T(256)} %param.11) | copy-start | bytes 3076
  43.4 29.8 %collective-permute-start.13 = (bf16[3,32,2560]{2,1,0:T(8,128)(2,1)}, bf16[3,32,2560]{2,1,0:T(8,128)(2,1)}, u32[]{:S(2)}, u32[]{:S(2)}) collective-permute-start(bf16[3,32,2560]{2,1,0:T(8,128)(2,1)} %get-tuple-element.43), channel_id=1, source_target_pairs={{0,12},{12,0},{1,13},{13,1},{2,14},{14,2},{3,15},{15,3},{16,28},{2... | collective-permute-start | bytes 1474568 | tf_op jit(solution)/shard_map/ppermute | solution.py:497
  49.8 30.8 %collective-permute-start.5 = (bf16[3,32,2560]{2,1,0:T(8,128)(2,1)}, bf16[3,32,2560]{2,1,0:T(8,128)(2,1)S(1)}, u32[]{:S(2)}, u32[]{:S(2)}) collective-permute-start(bf16[3,32,2560]{2,1,0:T(8,128)(2,1)} %get-tuple-element.35), channel_id=1, source_target_pairs={{0,4},{12,8},{1,5},{13,9},{2,6},{14,10},{3,7},{15,11},{16,20},{28,... | collective-permute-start | bytes 1474568 | tf_op jit(solution)/shard_map/ppermute | solution.py:497
  51.1 29.5 %collective-permute-start.6 = (bf16[3,32,2560]{2,1,0:T(8,128)(2,1)}, bf16[3,32,2560]{2,1,0:T(8,128)(2,1)S(1)}, u32[]{:S(2)}, u32[]{:S(2)}) collective-permute-start(bf16[3,32,2560]{2,1,0:T(8,128)(2,1)} %get-tuple-element.36), channel_id=1, source_target_pairs={{0,8},{12,4},{1,9},{13,5},{2,10},{14,6},{3,11},{15,7},{16,24},{28,... | collective-permute-start | bytes 1474568 | tf_op jit(solution)/shard_map/ppermute | solution.py:497
  71.3 19.6 %collective-permute-start.7 = (bf16[3,32,2560]{2,1,0:T(8,128)(2,1)}, bf16[3,32,2560]{2,1,0:T(8,128)(2,1)S(1)}, u32[]{:S(2)}, u32[]{:S(2)}) collective-permute-start(bf16[3,32,2560]{2,1,0:T(8,128)(2,1)} %get-tuple-element.37), channel_id=1, source_target_pairs={{4,8},{8,4},{5,9},{9,5},{6,10},{10,6},{7,11},{11,7},{20,24},{24,20... | collective-permute-start | bytes 1474568 | tf_op jit(solution)/shard_map/ppermute | solution.py:497
  79.8 11.1 %copy-start.4 = (bf16[3,1,32,2560]{3,2,1,0:T(8,128)(2,1)S(1)}, bf16[3,1,32,2560]{3,2,1,0:T(8,128)(2,1)}, u32[]{:S(2)}) copy-start(bf16[3,1,32,2560]{3,2,1,0:T(8,128)(2,1)} %copy-done.3) | copy-start | bytes 1474564
  79.8 11.1 %copy-start.8 = (bf16[3,1,32,2560]{3,2,1,0:T(8,128)(2,1)S(1)}, bf16[3,1,32,2560]{3,2,1,0:T(8,128)(2,1)}, u32[]{:S(2)}) copy-start(bf16[3,1,32,2560]{3,2,1,0:T(8,128)(2,1)} %copy-done.7) | copy-start | bytes 1474564
  79.8 11.1 %copy-start.14 = (bf16[3,1,32,2560]{3,2,1,0:T(8,128)(2,1)S(1)}, bf16[3,1,32,2560]{3,2,1,0:T(8,128)(2,1)}, u32[]{:S(2)}) copy-start(bf16[3,1,32,2560]{3,2,1,0:T(8,128)(2,1)} %copy-done.13) | copy-start | bytes 1474564
  (22 other events, 41.1 us)

commit v3 on v2

v3 whole, which is shorter than its diff:
```python
import functools
import math

import jax
import jax.numpy as jnp
from jax import lax
from jax.experimental import pallas as pl
from jax.experimental.pallas import tpu as pltpu
from jax.sharding import PartitionSpec as P

SPAN = 256
HALO = 16
GROUP = 4
TILE = 256
CELL = 128
UNROLL = 2

F32 = jnp.float32
BF16 = jnp.bfloat16


def call_params(mebibytes=16):
    return pltpu.CompilerParams(vmem_limit_bytes=mebibytes << 20)


def whole(count):
    return [pl.BlockSpec(memory_space=pltpu.VMEM)] * count


def anywhere(count):
    return [pl.BlockSpec(memory_space=pl.ANY)] * count


def cost(micros):
    return pl.CostEstimate(flops=int(micros * 1.15e9), bytes_accessed=1 << 16, transcendentals=0)


def skipping(kernel, at, count=1):
    return lambda *refs: kernel(*refs[:at], *refs[at + count :])


def split_hi_lo(values):
    high = values.astype(BF16)
    return high, (values - high.astype(F32)).astype(BF16)


def banded(index, taps_ref, tap_count):
    total = jnp.zeros(index.shape, F32)
    for tap in range(tap_count):
        total = jnp.where(index == tap, taps_ref[tap], total)
    return total


def late_lanes(ang_count):
    return max(1, ang_count // 4)


def lane_width(lines):
    return -(-lines // CELL) * CELL


def pair_slots(half):
    return -(-(half // 2 + 1) // 16) * 16


def pick_kernel(planes, half, slots, share, place_ref, partner_ref, *pick_refs):
    turn = place_ref[2]
    picks = share * slots
    pick_at = lax.broadcasted_iota(jnp.int32, (picks, 1), 0)
    row, first = pick_at // slots, pick_at % slots
    lanes_early = pick_refs[0].shape[1]
    leads = [jnp.full((picks, 1), -1, jnp.int32) for _ in pick_refs]
    mates = list(leads)
    counts = [jnp.int32(0) for _ in pick_refs]

    def stands(plane):
        return (turn ^ (plane // planes)) * lane_width(planes * share) + plane % planes * share

    for plane in range(half):
        lead, mate = stands(plane), stands(partner_ref[plane])
        late = jnp.maximum(lead, mate) >= lanes_early
        for part, mine in enumerate((jnp.logical_not(late), late)):
            here = first == jnp.where(mine, counts[part], -1)
            leads[part] = jnp.where(here, lead + row, leads[part])
            mates[part] = jnp.where(here, mate + row, mates[part])
            counts[part] = counts[part] + jnp.where(mine, 1, 0)
    for part, pick_ref in enumerate(pick_refs):
        line_at = lax.broadcasted_iota(jnp.int32, (picks, pick_ref.shape[1]), 1)
        pick_ref[:picks] = (line_at == leads[part]).astype(F32).astype(BF16)
        pick_ref[picks:] = (line_at == mates[part]).astype(F32).astype(BF16)


def band_kernel(tap_count, rows, row_count, upper, share, place_ref, taps_ref, rowband_ref, colband_ref):
    me = place_ref[0]
    odd = lax.rem(me, 2)
    margin = tap_count // 2
    ext = rows + 2 * HALO
    height, depth = GROUP * rows, GROUP * ext
    out_at = lax.broadcasted_iota(jnp.int32, (height, depth), 0)
    in_at = lax.broadcasted_iota(jnp.int32, (height, depth), 1)
    line = out_at % share
    plane = (out_at // share) % GROUP
    block = out_at // (share * GROUP)
    step, up = block // upper, block % upper
    row = (up * row_count + (step ^ me)) * share + line
    place = in_at % ext
    straight = place - HALO
    crossed = jnp.where(place < HALO, rows + place, jnp.where(place >= rows + HALO, place - rows - 2 * HALO, straight))
    source = jnp.where(odd == 1, straight, crossed)
    index = jnp.where(in_at // ext == plane, source - row + margin, -1)
    high, low = split_hi_lo(banded(index, taps_ref, tap_count))
    rowband_ref[:height] = high
    rowband_ref[height:] = low
    width = TILE + 2 * CELL
    from_at = lax.broadcasted_iota(jnp.int32, (width, TILE), 0)
    lane = lax.broadcasted_iota(jnp.int32, (width, TILE), 1)
    to_at = jnp.where(lane < CELL, 2 * lane, 2 * (lane - CELL) + 1)
    high, low = split_hi_lo(banded(from_at - CELL - to_at + margin, taps_ref, tap_count))
    colband_ref[0] = high
    colband_ref[1] = low


def edge_kernel(planes, rows, place_ref, raw_ref, dark_ref, flat_ref, near_ref, far_ref, held_ref, in_sems, out_sems):
    odd = lax.rem(place_ref[0], 2)
    near_at = pl.multiple_of((1 - odd) * (rows - HALO), HALO)
    far_at = pl.multiple_of(odd * (rows - HALO), HALO)
    loads, stores = [], []
    for side, (out_ref, start) in enumerate(((far_ref, far_at), (near_ref, near_at))):
        span, held = pl.ds(start, HALO), held_ref.at[side]
        loads.append(
            [
                pltpu.make_async_copy(raw_ref.at[:, span], held.at[:planes], in_sems.at[side, 0]),
                pltpu.make_async_copy(dark_ref.at[span], held.at[planes], in_sems.at[side, 1]),
                pltpu.make_async_copy(flat_ref.at[span], held.at[planes + 1], in_sems.at[side, 2]),
            ]
        )
        stores.append(pltpu.make_async_copy(held, out_ref, out_sems.at[side]))
    for side in loads:
        for copy in side:
            copy.start()
    for side, store in zip(loads, stores):
        for copy in side:
            copy.wait()
        store.start()
    for store in stores:
        store.wait()


def edges(place, raw, dark, flat):
    planes, rows, cols = raw.shape
    return pl.pallas_call(
        functools.partial(edge_kernel, planes, rows),
        out_shape=[jax.ShapeDtypeStruct((planes + 2, HALO, cols), BF16)] * 2,
        in_specs=[pl.BlockSpec(memory_space=pltpu.SMEM)] + anywhere(3),
        out_specs=anywhere(2),
        scratch_shapes=[
            pltpu.VMEM((2, planes + 2, HALO, cols), BF16),
            pltpu.SemaphoreType.DMA((2, 3)),
            pltpu.SemaphoreType.DMA((2,)),
        ],
        compiler_params=call_params(60),
        cost_estimate=cost(2.0),
    )(place, raw, dark, flat)


def lowpass_kernel(
    groups, row_count, upper, share, wants_inner,
    place_ref, raw_ref, near_ref, far_ref, dark_ref, flat_ref, rowband_ref, colband_ref, *rest
):
    out_refs, (level_ref, dark_all_ref, absorbed_ref, held_ref, smooth_ref) = rest[:row_count], rest[row_count:]
    planes, rows, cols = raw_ref.shape
    ext = rows + 2 * HALO
    height = GROUP * rows
    per_block = GROUP * share
    spans = ((0, HALO), (HALO, rows), (HALO + rows, HALO))

    @pl.when(place_ref[1] == wants_inner)
    def _():
        fields = (
            (near_ref[planes], near_ref[planes + 1]),
            (dark_ref[...], flat_ref[...]),
            (far_ref[planes], far_ref[planes + 1]),
        )
        for (start, size), (darkness, brightness) in zip(spans, fields):
            darkness = darkness.astype(F32)
            dark_all_ref[start : start + size] = darkness
            level_ref[start : start + size] = jnp.log(brightness.astype(F32) - darkness)
        for group in range(groups):
            sums = []
            for inner in range(GROUP):
                for (start, size), counts_ref in zip(spans, (near_ref, raw_ref, far_ref)):
                    place = inner * ext + start
                    if start > HALO and not wants_inner:
                        absorbed_ref[place : place + size] = jnp.zeros((size, cols), BF16)
                        sums.append(jnp.zeros((size, 1), F32))
                        continue
                    counts = counts_ref[group * GROUP + inner].astype(F32)
                    absorbed = level_ref[start : start + size] - jnp.log(counts - dark_all_ref[start : start + size])
                    absorbed_ref[place : place + size] = absorbed.astype(BF16)
                    sums.append(jnp.sum(absorbed, axis=1, keepdims=True))
            means = jnp.broadcast_to(jnp.concatenate(sums, axis=0) / cols, (GROUP * ext, CELL)).astype(BF16)
            both = jnp.dot(rowband_ref[...], means, preferred_element_type=F32)
            level = (both[:height] + both[height:]).astype(BF16)
            here = slice(group * height, (group + 1) * height)
            held_ref[here, :CELL] = -level
            held_ref[here, CELL + cols :] = -level
            level = jnp.concatenate([level.astype(F32)] * (TILE // CELL), axis=1)
            for at_col in range(0, cols, TILE):
                both = jnp.dot(rowband_ref[...], absorbed_ref[:, at_col : at_col + TILE], preferred_element_type=F32)
                less = both[:height] + both[height:] - level
                held_ref[here, CELL + at_col : CELL + at_col + TILE] = less.astype(BF16)
        total = jnp.zeros((groups * height, 1), F32)
        for at_col in range(0, cols, TILE):
            window = held_ref[:, at_col : at_col + TILE + 2 * CELL]
            piece = jnp.dot(window, colband_ref[0], preferred_element_type=F32) + jnp.dot(
                window, colband_ref[1], preferred_element_type=F32
            )
            at_half = at_col // 2
            smooth_ref[:, at_half : at_half + CELL] = piece[:, :CELL]
            smooth_ref[:, cols // 2 + at_half : cols // 2 + at_half + CELL] = piece[:, CELL:]
            total = total + jnp.sum(piece, axis=1, keepdims=True)
        mean = total / cols
        for group in range(groups):
            for step in range(row_count):
                for up in range(upper):
                    start = group * height + (step * upper + up) * per_block
                    centered = smooth_ref[start : start + per_block] - mean[start : start + per_block]
                    out_refs[step][group, up] = centered.astype(BF16)


def lowpass(place, raw, near, far, dark, flat, rowband, colband, row_count, upper, share, wants_inner, after):
    planes, rows, cols = raw.shape
    ext = rows + 2 * HALO
    groups = planes // GROUP
    shape = jax.ShapeDtypeStruct((groups, upper, GROUP * share, cols), BF16)
    return pl.pallas_call(
        skipping(functools.partial(lowpass_kernel, groups, row_count, upper, share, wants_inner), 8, len(after)),
        out_shape=[shape] * row_count,
        in_specs=[pl.BlockSpec(memory_space=pltpu.SMEM)] + whole(7) + anywhere(len(after)),
        out_specs=whole(row_count),
        scratch_shapes=[
            pltpu.VMEM((ext, cols), F32),
            pltpu.VMEM((ext, cols), F32),
            pltpu.VMEM((GROUP * ext, cols), BF16),
            pltpu.VMEM((planes * rows, cols + 2 * CELL), BF16),
            pltpu.VMEM((planes * rows, cols), F32),
        ],
        compiler_params=call_params(24),
        cost_estimate=cost(6.5),
    )(place, raw, near, far, dark, flat, rowband, colband, *after)


def route_kernel(row_count, ang_count, upper, place_ref, *rest):
    slots, targets, sems = rest[:row_count], rest[row_count:-1], rest[-1]
    me, turn = place_ref[0], place_ref[2]
    for step in range(1, ang_count):
        target = turn ^ step
        slot = me ^ (target // upper)
        for number in range(row_count):

            @pl.when(slot == number)
            def _():
                pltpu.make_async_copy(slots[number].at[:, target % upper], targets[step - 1], sems.at[step]).start()

    for step in range(1, ang_count):
        pltpu.make_async_copy(slots[0].at[:, 0], targets[step - 1], sems.at[step]).wait()


def route(place, slots, ang_count, after):
    groups, upper, lines, cols = slots[0].shape
    return pl.pallas_call(
        skipping(functools.partial(route_kernel, len(slots), ang_count, upper), 1 + len(slots)),
        out_shape=[jax.ShapeDtypeStruct((groups, lines, cols), BF16)] * (ang_count - 1),
        in_specs=[pl.BlockSpec(memory_space=pltpu.SMEM)] + anywhere(len(slots) + 1),
        out_specs=whole(ang_count - 1),
        scratch_shapes=[pltpu.SemaphoreType.DMA((ang_count,))],
        compiler_params=call_params(8),
        cost_estimate=cost(2.0),
    )(place, *slots, after)


def ramp_kernel(cols, to_even_ref, to_odd_ref, weave_ref):
    steps = cols // (2 * TILE)
    for out_ref, parity in ((to_even_ref, 1), (to_odd_ref, -1)):
        for block in range(2 * steps - 1):
            source = lax.broadcasted_iota(jnp.int32, (TILE, TILE), 0) + (block - (steps - 1)) * TILE
            distance = 2 * (source - lax.broadcasted_iota(jnp.int32, (TILE, TILE), 1)) + parity
            spacing = distance.astype(F32)
            falloff = -4.0 / (math.pi * math.pi * (spacing * spacing))
            out_ref[block * TILE : (block + 1) * TILE] = falloff.astype(BF16)
    source = lax.broadcasted_iota(jnp.int32, (TILE, TILE), 0)
    target = lax.broadcasted_iota(jnp.int32, (TILE, TILE), 1)
    place = jnp.where(source < CELL, 2 * source, 2 * (source - CELL) + 1)
    weave_ref[...] = (place == target).astype(F32).astype(BF16)


def ramp_lines(lines, half, to_even_ref, to_odd_ref, weave_ref, store):
    steps = half // TILE
    for block in range(steps):
        rows = slice((steps - 1 - block) * TILE, (steps - 1 - block) * TILE + half)
        here = slice(block * TILE, (block + 1) * TILE)
        there = slice(half + block * TILE, half + (block + 1) * TILE)
        even = lines(here).astype(F32) + jnp.dot(
            lines(slice(half, 2 * half)), to_even_ref[rows], preferred_element_type=F32
        )
        odd = lines(there).astype(F32) + jnp.dot(lines(slice(0, half)), to_odd_ref[rows], preferred_element_type=F32)
        even, odd = even.astype(BF16), odd.astype(BF16)
        for part in range(TILE // CELL):
            span = slice(part * CELL, (part + 1) * CELL)
            both = jnp.concatenate([even[:, span], odd[:, span]], axis=1)
            store(
                (TILE // CELL) * block + part, jnp.dot(both, weave_ref[...], preferred_element_type=F32).astype(BF16)
            )


def correlate(share, slots, lanes, cols, pick_ref, add, lead_ref, mate_ref, ls_ref, ms_ref):
    half, reach = cols // 2, SPAN // 2
    padded, width = half + 2 * reach, CELL + 2 * reach
    picks = share * slots
    for parity in range(2):
        start = parity * padded
        mate_ref[:, start : start + reach] = jnp.zeros((picks, reach), BF16)
        mate_ref[:, start + reach + half : start + padded] = jnp.zeros((picks, reach), BF16)
        for at_col in range(0, half, TILE):
            here = parity * half + at_col
            picked = 0.0
            for lane, lines in enumerate(lanes):
                values = lines(slice(here, here + TILE))
                at = lane * lane_width(values.shape[0])
                ones = pick_ref[:, at : at + values.shape[0]]
                picked = picked + jnp.dot(ones, values, preferred_element_type=F32)
            picked = picked.astype(BF16)
            lead_ref[:, here : here + TILE] = picked[:picks]
            place = start + reach + at_col
            mate_ref[:, place : place + TILE] = picked[picks:]
    cells = half // CELL

    def one_row(row, _):
        span = pl.ds(pl.multiple_of(row * slots, slots), slots)
        for cell in range(cells):
            stack = slice(cell * slots, (cell + 1) * slots)
            back = (cells - 1 - cell) * CELL
            for parity in range(2):
                at = parity * half + cell * CELL
                ls_ref[stack, parity * CELL : (parity + 1) * CELL] = lead_ref[span, at : at + CELL]
                at = parity * padded + back
                ms_ref[stack, parity * width : (parity + 1) * width] = mate_ref[span, at : at + width]
        products = lax.dot_general(ls_ref[...], ms_ref[...], (((0,), (0,)), ((), ())), preferred_element_type=F32)
        tables = (
            products[:CELL, :width],
            products[CELL:, width:],
            products[:CELL, width:] + products[CELL:, :width],
        )
        for number, table in enumerate(tables):
            skewed = pltpu.roll(table, 0, 1, stride=1, stride_axis=0)
            add(row, number, jnp.sum(skewed, axis=0, keepdims=True))
        return 0

    lax.fori_loop(0, share, one_row, 0, unroll=UNROLL)


def select_shifts(profile_ref, shifts, scale, width):
    reach = SPAN // 2
    middle = CELL + reach - 1 - lax.shift_right_arithmetic(shifts, 1)
    odd = (shifts & 1) == 1
    wanted = (jnp.where(odd, middle, -1), jnp.where(odd, middle - 1, -1), jnp.where(odd, -1, middle))
    at = lax.broadcasted_iota(jnp.int32, (width, shifts.shape[1]), 0)
    total = jnp.zeros((profile_ref.shape[0], shifts.shape[1]), F32)
    for number, place in enumerate(wanted):
        selector = (at == place).astype(F32).astype(BF16)
        rest = profile_ref[:, number * width : (number + 1) * width]
        for _ in range(3):
            high = rest.astype(BF16)
            total = total + jnp.dot(high, selector, preferred_element_type=F32)
            rest = rest - high.astype(F32)
    return total * scale


def flat(ref, span, first=None, count=None):
    part = ref[:, :, span] if first is None else ref[first : first + count, :, span]
    return part.reshape(part.shape[0] * part.shape[1], part.shape[2])


def finish_kernel(
    upper, slot_count, ang_count, wants_inner, parts, has_out, has_old, has_other, share, slots, scale, *refs
):
    refs = list(refs)
    take = lambda count: [refs.pop(0) for _ in range(count)]
    late = ang_count - late_lanes(ang_count)
    lanes = ang_count if 1 in parts else late
    last, loads, gives_own = 1 in parts, 0 in parts, parts == (0,)
    place_ref, *ramp_refs = take(4)
    slot_refs, pieces, picks = take(slot_count), take(lanes - 1 if loads else lanes), take(len(parts))
    (shifts_ref,) = take(1) if last else (None,)
    take(1 if has_out else 0)
    (old_ref,) = take(1) if has_old else (None,)
    (other_ref,) = take(1) if has_other else (None,)
    out_ref, result_ref = take(2)
    (own_ref,) = take(1) if gives_own else (None,)
    (x_ref,) = take(1) if loads else (None,)
    y_ref, in_sems, out_sems, profile_ref = take(4)
    me, turn = place_ref[0], place_ref[2]
    active = place_ref[3] == wants_inner
    groups, lines_each, cols = pieces[0].shape

    @pl.when(active)
    def _():
        if loads:
            targets = [x_ref.at[:groups]] + ([own_ref] if gives_own else [])
            sems = (in_sems.at[0], in_sems.at[ang_count])
            for number, slot in enumerate(slot_refs):

                @pl.when(me ^ (turn // upper) == number)
                def _():
                    for target, sem in zip(targets, sems):
                        pltpu.make_async_copy(slot.at[:, turn % upper], target, sem).start()

            copies = [pltpu.make_async_copy(slot_refs[0].at[:, 0], target, sem) for target, sem in zip(targets, sems)]
            for lane in range(1, lanes):
                target = x_ref.at[lane * groups : (lane + 1) * groups]
                copies.append(pltpu.make_async_copy(pieces[lane - 1], target, in_sems.at[lane]))
                copies[-1].start()
            for copy in copies:
                copy.wait()
            known = [lambda span, at=lane * groups: flat(x_ref, span, at, groups) for lane in range(lanes)]
        else:
            known = [lambda span, ref=piece: flat(ref, span) for piece in pieces]
        width = CELL + SPAN
        started = []
        for number, part in enumerate(parts):
            low, high = (0, late) if part == 0 else (late, ang_count)

            def lines(span, low=low, high=high):
                if loads:
                    return flat(x_ref, span, low * groups, (high - low) * groups)
                values = [read(span) for read in known[low:high]]
                return values[0] if len(values) == 1 else jnp.concatenate(values, axis=0)

            base = 0 if loads else late

            def store(block, values, low=low - base, high=high - base):
                here = slice(block * TILE, (block + 1) * TILE)
                y_ref[low * groups : high * groups, :, here] = values.reshape((high - low) * groups, lines_each, TILE)

            ramp_lines(lines, cols // 2, *ramp_refs, store)
            for lane in range(low, high):
                target = out_ref.at[pl.ds((turn ^ lane) * groups, groups)]
                source = y_ref.at[(lane - base) * groups : (lane - base + 1) * groups]
                started.append(pltpu.make_async_copy(source, target, out_sems.at[lane]))
                started[-1].start()

            def add(row, table, values, number=number, part=part):
                at = (pl.ds(row, 1), slice(table * width, (table + 1) * width))
                if number:
                    values = values + profile_ref[at]
                elif part:
                    values = values + old_ref[at]
                profile_ref[at] = values

            correlate(share, slots, known[:high], cols, picks[number], add, *refs)
        result_ref[...] = select_shifts(profile_ref, shifts_ref[...], scale, width) if last else profile_ref[...]
        for copy in started:
            copy.wait()

    @pl.when(jnp.logical_not(active))
    def _():
        result_ref[...] = other_ref[...] if has_other else jnp.zeros(result_ref.shape, F32)


def finish(place, ramp, slots, pieces, picks, shifts, out, old, other, wants_inner, parts, upper, share, half, after):
    loads, last, gives_own = 0 in parts, 1 in parts, parts == (0,)
    ang_count = len(pieces) + (1 if loads else 0)
    groups, lines_each, cols = pieces[0].shape
    lanes = ang_count if last else ang_count - late_lanes(ang_count)
    number = pair_slots(half)
    pieces = pieces[: lanes - 1] if loads else pieces
    args = [place, *ramp, *slots, *pieces, *(picks[part] for part in parts)]
    specs = [pl.BlockSpec(memory_space=pltpu.SMEM)] + whole(3)
    specs = specs + (anywhere if loads else whole)(len(slots) + len(pieces)) + whole(len(parts))
    cells, width = cols // (2 * CELL), CELL + SPAN
    if last:
        args, specs = args + [shifts], specs + whole(1)
    aliases = {}
    if out is not None:
        aliases[len(args)] = 0
        args, specs = args + [out], specs + anywhere(1)
    if old is not None:
        args, specs = args + [old], specs + whole(1)
    if other is not None:
        args, specs = args + [other], specs + whole(1)
    args, specs = args + [after], specs + anywhere(1)
    kernel = functools.partial(
        finish_kernel, upper, len(slots), ang_count, wants_inner, parts, out is not None, old is not None,
        other is not None, share, number, (half * cols) ** (-0.5),
    )
    lines = lambda count: (groups * count, lines_each, cols)
    return pl.pallas_call(
        skipping(kernel, len(args) - 1),
        out_shape=[
            jax.ShapeDtypeStruct(lines(ang_count), BF16),
            jax.ShapeDtypeStruct((share, shifts.shape[1] if last else 3 * width), F32),
        ]
        + [jax.ShapeDtypeStruct(lines(1), BF16)] * gives_own,
        in_specs=specs,
        out_specs=anywhere(1) + whole(1 + gives_own),
        scratch_shapes=[pltpu.VMEM(lines(lanes), BF16)] * loads
        + [
            pltpu.VMEM(lines(lanes if loads else late_lanes(ang_count)), BF16),
            pltpu.SemaphoreType.DMA((ang_count + 1,)),
            pltpu.SemaphoreType.DMA((ang_count,)),
            pltpu.VMEM((share, 3 * width), F32),
            pltpu.VMEM((share * number, cols), BF16),
            pltpu.VMEM((share * number, cols + 2 * SPAN), BF16),
            pltpu.VMEM((cells * number, 2 * CELL), BF16),
            pltpu.VMEM((cells * number, 2 * width), BF16),
        ],
        input_output_aliases=aliases,
        compiler_params=call_params(),
        cost_estimate=cost(5.0 * len(parts)),
    )(*args)


def shards(raw_frames, dark_field, flat_field, kernel_taps, partner, shifts):
    planes, rows, cols = raw_frames.shape
    tap_count = kernel_taps.shape[0]
    half = partner.shape[0]
    row_count, ang_count = lax.axis_size("row"), lax.axis_size("ang")
    upper, share = ang_count // row_count, rows // ang_count
    me, turn = lax.axis_index("row"), lax.axis_index("ang")
    is_inner = lambda at: jnp.logical_and(at > 0, at < row_count - 1).astype(jnp.int32)
    place = jnp.stack([me, is_inner(me), turn, is_inner(turn // upper)]).astype(jnp.int32)

    cross = [(i, i + 1) for i in range(1, row_count - 1, 2)]
    near, far = edges(place, raw_frames, dark_field, flat_field)
    far = lax.ppermute(far, "row", cross + [(j, i) for i, j in cross])
    near = lax.ppermute(near, "row", [(i, i ^ 1) for i in range(row_count)])
    ext = rows + 2 * HALO
    rowband, colband = pl.pallas_call(
        functools.partial(band_kernel, tap_count, rows, row_count, upper, share),
        out_shape=[
            jax.ShapeDtypeStruct((2 * GROUP * rows, GROUP * ext), BF16),
            jax.ShapeDtypeStruct((2, TILE + 2 * CELL, TILE), BF16),
        ],
        in_specs=[pl.BlockSpec(memory_space=pltpu.SMEM)] * 2,
        out_specs=whole(2),
        compiler_params=call_params(),
        cost_estimate=cost(2.0),
    )(place, kernel_taps)
    ramp = pl.pallas_call(
        functools.partial(ramp_kernel, cols),
        out_shape=[jax.ShapeDtypeStruct((cols - TILE, TILE), BF16)] * 2 + [jax.ShapeDtypeStruct((TILE, TILE), BF16)],
        out_specs=whole(3),
        compiler_params=call_params(),
        cost_estimate=cost(1.8),
    )()

    number, late = pair_slots(half), late_lanes(ang_count)

    per_lane = lane_width(planes * share)
    picks = pl.pallas_call(
        functools.partial(pick_kernel, planes, half, number, share),
        out_shape=[
            jax.ShapeDtypeStruct((2 * share * number, lanes * per_lane), BF16) for lanes in (ang_count - late, ang_count)
        ],
        in_specs=[pl.BlockSpec(memory_space=pltpu.SMEM)] * 2,
        out_specs=whole(2),
        compiler_params=call_params(),
        cost_estimate=cost(1.5),
    )(place, partner)
    shifts = shifts[None, :]

    ends = (0, row_count - 1)
    mine = lambda inner, source: (source in ends) != bool(inner)

    def filter_rows(inner, after):
        sent = lowpass(
            place, raw_frames, near, far if inner else near, dark_field, flat_field, rowband, colband,
            row_count, upper, share, inner, after,
        )
        slots = [sent[0]]
        for step in range(1, row_count):
            pairs = [(i, i ^ step) for i in range(row_count) if mine(inner, i)]
            slots.append(lax.ppermute(sent[step], "row", pairs))
        return slots

    def regroup(inner, slots, after):
        pieces = list(route(place, slots, ang_count, after))
        for step in range(1, ang_count):
            pairs = [(i, i ^ step) for i in range(ang_count) if mine(inner, (i ^ step) // upper)]
            pieces[step - 1] = lax.ppermute(pieces[step - 1], "ang", pairs)
        return pieces

    outer = filter_rows(0, [])
    inner = filter_rows(1, [outer[0], ramp[0], picks[0]])
    outer_lines = regroup(0, outer, inner[0])
    inner_lines = regroup(1, inner, inner[0])
    ending = functools.partial(finish, place, ramp)
    out, ends_corr = ending(
        outer, outer_lines, picks, shifts, None, None, None, 0, (0, 1), upper, share, half, inner[0]
    )
    out, profile, own = ending(
        inner, inner_lines, picks, shifts, out, None, None, 1, (0,), upper, share, half, ends_corr
    )
    filtered, correlation = ending(
        [], [own, *inner_lines], picks, shifts, out, profile, ends_corr, 1, (1,), upper, share, half, profile
    )
    return filtered.reshape(-1, share, cols), correlation


def solution(mesh):
    in_specs = (
        P(("scan", "ang"), "row", None),
        P("row", None),
        P("row", None),
        P(),
        P("scan"),
        P(),
    )
    out_specs = (P("scan", ("ang", "row"), None), P(("scan", "ang", "row"), None))
    return jax.shard_map(shards, mesh=mesh, in_specs=in_specs, out_specs=out_specs, check_vma=False)
```

time: 104 us -> 95.1 us (0.914)
  the two profiles are of different devices: /device:TPU:19 before, /device:TPU:21 now
where the time goes in v3:
time: 95.1 us; the launch traced here: 94.7 us
  waiting for transfers between devices  35.9 us (38%)
  Pallas kernels  34.5 us (36%)
  starting transfers between devices  22.5 us (24%)
  between operations  1.17 us (1%)
    ppermute x6, waiting for transfers between devices, regroup(): pieces[step - 1] = lax.ppermute(pieces[step - 1], 'ang', pairs)  26.1 us
    pallas_call x3, Pallas kernels, finish(): pl.pallas_call(skipping(kernel, len(args) - 1), out_shape=[jax.ShapeDtype...  16.3 us
    ppermute x6, starting transfers between devices, regroup(): pieces[step - 1] = lax.ppermute(pieces[step - 1], 'ang', pairs)  9.74 us
    ppermute x6, starting transfers between devices, filter_rows(): slots.append(lax.ppermute(sent[step], 'row', pairs))  9.03 us
    ppermute x1, waiting for transfers between devices, shards(): far = lax.ppermute(far, 'row', cross + [(j, i) for i, j in cross])  6.88 us
    pallas_call x2, Pallas kernels, lowpass(): pl.pallas_call(skipping(functools.partial(lowpass_kernel, groups, row_cou...  6.81 us
    pallas_call x1, Pallas kernels, edges(): pl.pallas_call(functools.partial(edge_kernel, planes, rows), out_shape=[j...  3.45 us
    pallas_call x2, Pallas kernels, route(): pl.pallas_call(skipping(functools.partial(route_kernel, len(slots), ang_c...  3.16 us
  transfers between devices with their start and end apart: 14, of which 5 were waited for; matrix products, arithmetic and copies ran while one was open for 0% of the time, Pallas kernels for 25%

profile of v3, /device:TPU:21, one launch (start us, length us, event | category | flops | bytes accessed | tf_op | source)
XLA Modules:
  0.0 94.7 jit_solution(11959509489348751227)
XLA Ops:
  1.3 3.5 %shard_map.78 = (bf16[14,16,2560]{2,1,0:T(8,128)(2,1)}, bf16[14,16,2560]{2,1,0:T(8,128)(2,1)}) custom-call(s32[4]{0:T(128)} %pad_add_fusion.place_ref.refs_0_, bf16[12,32,2560]{2,1,0:T(8,128)(2,1)} %refs_1_.3, bf16[32,2560]{1,0:T(8,128)(2,1)} %refs_4_.3, bf16[32,2560]{1,0:T(8,128)(2,1)} %refs_5_.3), custom_call_target="tpu_custom_call" | custom-call | flops 2300000000 | bytes 65536 | tf_op jit(solution)/shard_map/pallas_call | solution.py:151
  5.5 3.0 %collective-permute-start.1 = (bf16[14,16,2560]{2,1,0:T(8,128)(2,1)}, bf16[14,16,2560]{2,1,0:T(8,128)(2,1)S(1)}, u32[]{:S(2)}, u32[]{:S(2)}) collective-permute-start(bf16[14,16,2560]{2,1,0:T(8,128)(2,1)} %get-tuple-element.36), channel_id=1, source_target_pairs={{1,2},{2,1},{5,6},{6,5},{9,10},{10,9},{13,14},{14,13},{17,18},{18,... | collective-permute-start | bytes 3440648 | tf_op jit(solution)/shard_map/ppermute | solution.py:535
  8.5 1.4 %shard_map.81 = (bf16[256,384]{1,0:T(8,128)(2,1)S(1)}, bf16[256,512]{1,0:T(8,128)(2,1)S(1)}) custom-call(s32[4]{0:T(128)S(1)} %copy-done, s32[24]{0:T(128)S(1)} %copy-done.5), custom_call_target="tpu_custom_call" | custom-call | flops 1724999936 | bytes 65536 | tf_op jit(solution)/shard_map/pallas_call | solution.py:560
  9.9 1.3 %shard_map.77 = (bf16[2304,256]{1,0:T(8,128)(2,1)S(1)}, bf16[2304,256]{1,0:T(8,128)(2,1)S(1)}, bf16[256,256]{1,0:T(8,128)(2,1)S(1)}) custom-call(), custom_call_target="tpu_custom_call" | custom-call | flops 2070000000 | bytes 65536 | tf_op jit(solution)/shard_map/pallas_call | solution.py:549
  11.3 2.1 %shard_map.79 = (bf16[256,256]{1,0:T(8,128)(2,1)S(1)}, bf16[2,512,256]{2,1,0:T(8,128)(2,1)S(1)}) custom-call(s32[4]{0:T(128)S(1)} %copy-done, f32[31]{0:T(128)S(1)} %copy-done.6), custom_call_target="tpu_custom_call" | custom-call | flops 2300000000 | bytes 65536 | tf_op jit(solution)/shard_map/pallas_call | solution.py:538
  14.0 1.3 %collective-permute-start.7 = (bf16[3,1,32,2560]{3,2,1,0:T(8,128)(2,1)S(1)}, bf16[3,1,32,2560]{3,2,1,0:T(8,128)(2,1)S(1)}, u32[]{:S(2)}, u32[]{:S(2)}) collective-permute-start(bf16[3,1,32,2560]{3,2,1,0:T(8,128)(2,1)S(1)} %get-tuple-element.47), channel_id=1, source_target_pairs={{0,1},{3,2},{4,5},{7,6},{8,9},{11,10},{12,13},{15,14},{16,17},{19,... | collective-permute-start | bytes 1474568 | tf_op jit(solution)/shard_map/ppermute | solution.py:583
  15.3 1.3 %collective-permute-start.8 = (bf16[3,1,32,2560]{3,2,1,0:T(8,128)(2,1)S(1)}, bf16[3,1,32,2560]{3,2,1,0:T(8,128)(2,1)S(1)}, u32[]{:S(2)}, u32[]{:S(2)}) collective-permute-start(bf16[3,1,32,2560]{3,2,1,0:T(8,128)(2,1)S(1)} %get-tuple-element.48), channel_id=1, source_target_pairs={{0,2},{3,1},{4,6},{7,5},{8,10},{11,9},{12,14},{15,13},{16,18},{19,... | collective-permute-start | bytes 1474568 | tf_op jit(solution)/shard_map/ppermute | solution.py:583
  17.3 6.9 %collective-permute-done.1.refs_3_ = bf16[14,16,2560]{2,1,0:T(8,128)(2,1)S(1)} collective-permute-done((bf16[14,16,2560]{2,1,0:T(8,128)(2,1)}, bf16[14,16,2560]{2,1,0:T(8,128)(2,1)S(1)}, u32[]{:S(2)}, u32[]{:S(2)}) %collective-permute-start.1) | collective-permute-done | bytes 1146912 | tf_op jit(solution)/shard_map/ppermute | solution.py:535
  24.1 6.3 %shard_map.82 = (bf16[3,1,32,2560]{3,2,1,0:T(8,128)(2,1)S(1)}, bf16[3,1,32,2560]{3,2,1,0:T(8,128)(2,1)S(1)}, bf16[3,1,32,2560]{3,2,1,0:T(8,128)(2,1)S(1)}, bf16[3,1,32,2560]{3,2,1,0:T(8,128)(2,1)S(1)}) custom-call(s32[4]{0:T(128)S(1)} %copy-done, bf16[12,32,2560]{2,1,0:T(8,128)(2,1)S(1)} %copy-done.1, ...), custom_call_target="tpu_custom_call" | custom-call | flops 7474999808 | bytes 65536 | tf_op jit(solution)/shard_map/pallas_call | solution.py:236
  30.4 1.3 %collective-permute-start.2 = (bf16[3,1,32,2560]{3,2,1,0:T(8,128)(2,1)S(1)}, bf16[3,1,32,2560]{3,2,1,0:T(8,128)(2,1)S(1)}, u32[]{:S(2)}, u32[]{:S(2)}) collective-permute-start(bf16[3,1,32,2560]{3,2,1,0:T(8,128)(2,1)S(1)} %get-tuple-element.42), channel_id=1, source_target_pairs={{1,0},{2,3},{5,4},{6,7},{9,8},{10,11},{13,12},{14,15},{17,16},{18,... | collective-permute-start | bytes 1474568 | tf_op jit(solution)/shard_map/ppermute | solution.py:583
  31.7 1.3 %collective-permute-start.3 = (bf16[3,1,32,2560]{3,2,1,0:T(8,128)(2,1)S(1)}, bf16[3,1,32,2560]{3,2,1,0:T(8,128)(2,1)S(1)}, u32[]{:S(2)}, u32[]{:S(2)}) collective-permute-start(bf16[3,1,32,2560]{3,2,1,0:T(8,128)(2,1)S(1)} %get-tuple-element.43), channel_id=1, source_target_pairs={{1,3},{2,0},{5,7},{6,4},{9,11},{10,8},{13,15},{14,12},{17,19},{18,... | collective-permute-start | bytes 1474568 | tf_op jit(solution)/shard_map/ppermute | solution.py:583
  33.1 3.1 %collective-permute-start.4 = (bf16[3,1,32,2560]{3,2,1,0:T(8,128)(2,1)S(1)}, bf16[3,1,32,2560]{3,2,1,0:T(8,128)(2,1)S(1)}, u32[]{:S(2)}, u32[]{:S(2)}) collective-permute-start(bf16[3,1,32,2560]{3,2,1,0:T(8,128)(2,1)S(1)} %get-tuple-element.44), channel_id=1, source_target_pairs={{1,2},{2,1},{5,6},{6,5},{9,10},{10,9},{13,14},{14,13},{17,18},{18,... | collective-permute-start | bytes 1474568 | tf_op jit(solution)/shard_map/ppermute | solution.py:583
  36.2 1.6 %shard_map.84 = (bf16[3,32,2560]{2,1,0:T(8,128)(2,1)S(1)}, bf16[3,32,2560]{2,1,0:T(8,128)(2,1)S(1)}, bf16[3,32,2560]{2,1,0:T(8,128)(2,1)S(1)}) custom-call(s32[4]{0:T(128)S(1)} %copy-done, bf16[3,1,32,2560]{3,2,1,0:T(8,128)(2,1)S(1)} %get-tuple-element.39.refs_8_.refs_1_.refs_4_, bf16[3,1,32,2560]{3,2,1,0:T(8,128)(2,1)S(1)} %collective-permute-done.7.refs_2_.refs_5_, ...), custom_call_target="tpu_custom_call" | custom-call | flops 2300000000 | bytes 65536 | tf_op jit(solution)/shard_map/pallas_call | solution.py:271
  37.8 3.2 %collective-permute-start.10 = (bf16[3,32,2560]{2,1,0:T(8,128)(2,1)S(1)}, bf16[3,32,2560]{2,1,0:T(8,128)(2,1)S(1)}, u32[]{:S(2)}, u32[]{:S(2)}) collective-permute-start(bf16[3,32,2560]{2,1,0:T(8,128)(2,1)S(1)} %get-tuple-element.50), channel_id=1, source_target_pairs={{4,0},{8,12},{5,1},{9,13},{6,2},{10,14},{7,3},{11,15},{20,16},{24,... | collective-permute-start | bytes 1474568 | tf_op jit(solution)/shard_map/ppermute | solution.py:590
  41.0 1.3 %collective-permute-start.11 = (bf16[3,32,2560]{2,1,0:T(8,128)(2,1)S(1)}, bf16[3,32,2560]{2,1,0:T(8,128)(2,1)S(1)}, u32[]{:S(2)}, u32[]{:S(2)}) collective-permute-start(bf16[3,32,2560]{2,1,0:T(8,128)(2,1)S(1)} %get-tuple-element.51), channel_id=1, source_target_pairs={{4,12},{8,0},{5,13},{9,1},{6,14},{10,2},{7,15},{11,3},{20,28},{24,... | collective-permute-start | bytes 1474568 | tf_op jit(solution)/shard_map/ppermute | solution.py:590
  43.1 2.9 %collective-permute-done.4.refs_4_.refs_7_ = bf16[3,1,32,2560]{3,2,1,0:T(8,128)(2,1)S(1)} collective-permute-done((bf16[3,1,32,2560]{3,2,1,0:T(8,128)(2,1)S(1)}, bf16[3,1,32,2560]{3,2,1,0:T(8,128)(2,1)S(1)}, u32[]{:S(2)}, u32[]{:S(2)}) %collective-permute-start.4) | collective-permute-done | bytes 491552 | tf_op jit(solution)/shard_map/ppermute | solution.py:583
  46.0 1.6 %shard_map.83 = (bf16[3,32,2560]{2,1,0:T(8,128)(2,1)S(1)}, bf16[3,32,2560]{2,1,0:T(8,128)(2,1)S(1)}, bf16[3,32,2560]{2,1,0:T(8,128)(2,1)S(1)}) custom-call(s32[4]{0:T(128)S(1)} %copy-done, bf16[3,1,32,2560]{3,2,1,0:T(8,128)(2,1)S(1)} %get-tuple-element.41.refs_1_.refs_5_.refs_14_.refs_4_, ...), custom_call_target="tpu_custom_call" | custom-call | flops 2300000000 | bytes 65536 | tf_op jit(solution)/shard_map/pallas_call | solution.py:271
  47.6 1.3 %collective-permute-start.5 = (bf16[3,32,2560]{2,1,0:T(8,128)(2,1)S(1)}, bf16[3,32,2560]{2,1,0:T(8,128)(2,1)S(1)}, u32[]{:S(2)}, u32[]{:S(2)}) collective-permute-start(bf16[3,32,2560]{2,1,0:T(8,128)(2,1)S(1)} %get-tuple-element.45), channel_id=1, source_target_pairs={{0,4},{12,8},{1,5},{13,9},{2,6},{14,10},{3,7},{15,11},{16,20},{28,... | collective-permute-start | bytes 1474568 | tf_op jit(solution)/shard_map/ppermute | solution.py:590
  50.2 21.2 %collective-permute-done.10.refs_8_ = bf16[3,32,2560]{2,1,0:T(8,128)(2,1)S(1)} collective-permute-done((bf16[3,32,2560]{2,1,0:T(8,128)(2,1)S(1)}, bf16[3,32,2560]{2,1,0:T(8,128)(2,1)S(1)}, u32[]{:S(2)}, u32[]{:S(2)}) %collective-permute-start.10) | collective-permute-done | bytes 491552 | tf_op jit(solution)/shard_map/ppermute | solution.py:590
  71.4 1.9 %collective-permute-start.13 = (bf16[3,32,2560]{2,1,0:T(8,128)(2,1)S(1)}, bf16[3,32,2560]{2,1,0:T(8,128)(2,1)S(1)}, u32[]{:S(2)}, u32[]{:S(2)}) collective-permute-start(bf16[3,32,2560]{2,1,0:T(8,128)(2,1)S(1)} %get-tuple-element.57), channel_id=1, source_target_pairs={{4,8},{8,4},{5,9},{9,5},{6,10},{10,6},{7,11},{11,7},{20,24},{24,20... | collective-permute-start | bytes 1474568 | tf_op jit(solution)/shard_map/ppermute | solution.py:590
  74.2 2.5 %collective-permute-done.6.refs_9_.refs_6_ = bf16[3,32,2560]{2,1,0:T(8,128)(2,1)S(1)} collective-permute-done((bf16[3,32,2560]{2,1,0:T(8,128)(2,1)S(1)}, bf16[3,32,2560]{2,1,0:T(8,128)(2,1)S(1)}, u32[]{:S(2)}, u32[]{:S(2)}) %collective-permute-start.6) | collective-permute-done | bytes 491552 | tf_op jit(solution)/shard_map/ppermute | solution.py:590
  76.7 8.2 %shard_map.86 = (bf16[12,32,2560]{2,1,0:T(8,128)(2,1)}, f32[8,1152]{1,0:T(8,128)S(1)}, bf16[3,32,2560]{2,1,0:T(8,128)(2,1)S(1)}) custom-call(s32[4]{0:T(128)S(1)} %copy-done, bf16[2304,256]{1,0:T(8,128)(2,1)S(1)} %get-tuple-element.32.refs_9_.refs_1_, bf16[2304,256]{1,0:T(8,128)(2,1)S(1)} %get-tuple-element.33.refs_2_, ...), custom_call_target="tpu_custom_call", output_to_operand_aliasing={{0}: (11, {})} | custom-call | flops 5750000128 | bytes 65536 | tf_op jit(solution)/shard_map/pallas_call | solution.py:497
  84.9 2.4 %collective-permute-done.13.refs_7_ = bf16[3,32,2560]{2,1,0:T(8,128)(2,1)S(1)} collective-permute-done((bf16[3,32,2560]{2,1,0:T(8,128)(2,1)S(1)}, bf16[3,32,2560]{2,1,0:T(8,128)(2,1)S(1)}, u32[]{:S(2)}, u32[]{:S(2)}) %collective-permute-start.13) | collective-permute-done | bytes 491552 | tf_op jit(solution)/shard_map/ppermute | solution.py:590
  87.3 7.2 %shard_map.87 = (bf16[12,32,2560]{2,1,0:T(8,128)(2,1)}, f32[8,256]{1,0:T(8,128)}) custom-call(s32[4]{0:T(128)S(1)} %copy-done, bf16[2304,256]{1,0:T(8,128)(2,1)S(1)} %get-tuple-element.32.refs_9_.refs_1_, bf16[2304,256]{1,0:T(8,128)(2,1)S(1)} %get-tuple-element.33.refs_2_, ...), custom_call_target="tpu_custom_call", output_to_operand_aliasing={{0}: (10, {})} | custom-call | flops 5750000128 | bytes 65536 | tf_op jit(solution)/shard_map/pallas_call | solution.py:497
  (30 shorter events, 5.5 us)
Async XLA Ops:
  1.2 7.2 %copy-start = (s32[4]{0:T(128)S(1)}, s32[4]{0:T(128)}, u32[]{:S(2)}) copy-start(s32[4]{0:T(128)} %pad_add_fusion.place_ref.refs_0_) | copy-start | bytes 52
  1.3 7.2 %copy-start.5 = (s32[24]{0:T(128)S(1)}, s32[24]{0:T(128)}, u32[]{:S(2)}) copy-start(s32[24]{0:T(128)} %partner_ref.1) | copy-start | bytes 292
  4.7 8.6 %collective-permute-start = (bf16[14,16,2560]{2,1,0:T(8,128)(2,1)}, bf16[14,16,2560]{2,1,0:T(8,128)(2,1)S(1)}, u32[]{:S(2)}, u32[]{:S(2)}) collective-permute-start(bf16[14,16,2560]{2,1,0:T(8,128)(2,1)} %get-tuple-element.35), channel_id=1, source_target_pairs={{0,1},{1,0},{2,3},{3,2},{4,5},{5,4},{6,7},{7,6},{8,9},{9,8},{10,11... | collective-permute-start | bytes 3440648 | tf_op jit(solution)/shard_map/ppermute | solution.py:536
  5.5 18.7 %collective-permute-start.1 = (bf16[14,16,2560]{2,1,0:T(8,128)(2,1)}, bf16[14,16,2560]{2,1,0:T(8,128)(2,1)S(1)}, u32[]{:S(2)}, u32[]{:S(2)}) collective-permute-start(bf16[14,16,2560]{2,1,0:T(8,128)(2,1)} %get-tuple-element.36), channel_id=1, source_target_pairs={{1,2},{2,1},{5,6},{6,5},{9,10},{10,9},{13,14},{14,13},{17,18},{18,... | collective-permute-start | bytes 3440648 | tf_op jit(solution)/shard_map/ppermute | solution.py:535
  9.9 1.4 %copy-start.6 = (f32[31]{0:T(128)S(1)}, f32[31]{0:T(128)}, u32[]{:S(2)}) copy-start(f32[31]{0:T(128)} %taps_ref.1) | copy-start | bytes 376
  11.2 2.1 %copy-start.1 = (bf16[12,32,2560]{2,1,0:T(8,128)(2,1)S(1)}, bf16[12,32,2560]{2,1,0:T(8,128)(2,1)}, u32[]{:S(2)}) copy-start(bf16[12,32,2560]{2,1,0:T(8,128)(2,1)} %refs_1_.3) | copy-start | bytes 5898244
  11.3 2.1 %copy-start.2 = (bf16[32,2560]{1,0:T(8,128)(2,1)S(1)}, bf16[32,2560]{1,0:T(8,128)(2,1)}, u32[]{:S(2)}) copy-start(bf16[32,2560]{1,0:T(8,128)(2,1)} %refs_4_.3) | copy-start | bytes 491524
  11.3 2.1 %copy-start.3 = (bf16[32,2560]{1,0:T(8,128)(2,1)S(1)}, bf16[32,2560]{1,0:T(8,128)(2,1)}, u32[]{:S(2)}) copy-start(bf16[32,2560]{1,0:T(8,128)(2,1)} %refs_5_.3) | copy-start | bytes 491524
  14.0 19.1 %collective-permute-start.7 = (bf16[3,1,32,2560]{3,2,1,0:T(8,128)(2,1)S(1)}, bf16[3,1,32,2560]{3,2,1,0:T(8,128)(2,1)S(1)}, u32[]{:S(2)}, u32[]{:S(2)}) collective-permute-start(bf16[3,1,32,2560]{3,2,1,0:T(8,128)(2,1)S(1)} %get-tuple-element.47), channel_id=1, source_target_pairs={{0,1},{3,2},{4,5},{7,6},{8,9},{11,10},{12,13},{15,14},{16,17},{19,... | collective-permute-start | bytes 1474568 | tf_op jit(solution)/shard_map/ppermute | solution.py:583
  15.3 20.9 %collective-permute-start.8 = (bf16[3,1,32,2560]{3,2,1,0:T(8,128)(2,1)S(1)}, bf16[3,1,32,2560]{3,2,1,0:T(8,128)(2,1)S(1)}, u32[]{:S(2)}, u32[]{:S(2)}) collective-permute-start(bf16[3,1,32,2560]{3,2,1,0:T(8,128)(2,1)S(1)} %get-tuple-element.48), channel_id=1, source_target_pairs={{0,2},{3,1},{4,6},{7,5},{8,10},{11,9},{12,14},{15,13},{16,18},{19,... | collective-permute-start | bytes 1474568 | tf_op jit(solution)/shard_map/ppermute | solution.py:583
  16.6 19.6 %collective-permute-start.9 = (bf16[3,1,32,2560]{3,2,1,0:T(8,128)(2,1)S(1)}, bf16[3,1,32,2560]{3,2,1,0:T(8,128)(2,1)S(1)}, u32[]{:S(2)}, u32[]{:S(2)}) collective-permute-start(bf16[3,1,32,2560]{3,2,1,0:T(8,128)(2,1)S(1)} %get-tuple-element.49), channel_id=1, source_target_pairs={{0,3},{3,0},{4,7},{7,4},{8,11},{11,8},{12,15},{15,12},{16,19},{19,... | collective-permute-start | bytes 1474568 | tf_op jit(solution)/shard_map/ppermute | solution.py:583
  30.4 12.0 %collective-permute-start.2 = (bf16[3,1,32,2560]{3,2,1,0:T(8,128)(2,1)S(1)}, bf16[3,1,32,2560]{3,2,1,0:T(8,128)(2,1)S(1)}, u32[]{:S(2)}, u32[]{:S(2)}) collective-permute-start(bf16[3,1,32,2560]{3,2,1,0:T(8,128)(2,1)S(1)} %get-tuple-element.42), channel_id=1, source_target_pairs={{1,0},{2,3},{5,4},{6,7},{9,8},{10,11},{13,12},{14,15},{17,16},{18,... | collective-permute-start | bytes 1474568 | tf_op jit(solution)/shard_map/ppermute | solution.py:583
  31.7 11.4 %collective-permute-start.3 = (bf16[3,1,32,2560]{3,2,1,0:T(8,128)(2,1)S(1)}, bf16[3,1,32,2560]{3,2,1,0:T(8,128)(2,1)S(1)}, u32[]{:S(2)}, u32[]{:S(2)}) collective-permute-start(bf16[3,1,32,2560]{3,2,1,0:T(8,128)(2,1)S(1)} %get-tuple-element.43), channel_id=1, source_target_pairs={{1,3},{2,0},{5,7},{6,4},{9,11},{10,8},{13,15},{14,12},{17,19},{18,... | collective-permute-start | bytes 1474568 | tf_op jit(solution)/shard_map/ppermute | solution.py:583
  33.1 12.9 %collective-permute-start.4 = (bf16[3,1,32,2560]{3,2,1,0:T(8,128)(2,1)S(1)}, bf16[3,1,32,2560]{3,2,1,0:T(8,128)(2,1)S(1)}, u32[]{:S(2)}, u32[]{:S(2)}) collective-permute-start(bf16[3,1,32,2560]{3,2,1,0:T(8,128)(2,1)S(1)} %get-tuple-element.44), channel_id=1, source_target_pairs={{1,2},{2,1},{5,6},{6,5},{9,10},{10,9},{13,14},{14,13},{17,18},{18,... | collective-permute-start | bytes 1474568 | tf_op jit(solution)/shard_map/ppermute | solution.py:583
  37.8 33.6 %collective-permute-start.10 = (bf16[3,32,2560]{2,1,0:T(8,128)(2,1)S(1)}, bf16[3,32,2560]{2,1,0:T(8,128)(2,1)S(1)}, u32[]{:S(2)}, u32[]{:S(2)}) collective-permute-start(bf16[3,32,2560]{2,1,0:T(8,128)(2,1)S(1)} %get-tuple-element.50), channel_id=1, source_target_pairs={{4,0},{8,12},{5,1},{9,13},{6,2},{10,14},{7,3},{11,15},{20,16},{24,... | collective-permute-start | bytes 1474568 | tf_op jit(solution)/shard_map/ppermute | solution.py:590
  41.0 32.3 %collective-permute-start.11 = (bf16[3,32,2560]{2,1,0:T(8,128)(2,1)S(1)}, bf16[3,32,2560]{2,1,0:T(8,128)(2,1)S(1)}, u32[]{:S(2)}, u32[]{:S(2)}) collective-permute-start(bf16[3,32,2560]{2,1,0:T(8,128)(2,1)S(1)} %get-tuple-element.51), channel_id=1, source_target_pairs={{4,12},{8,0},{5,13},{9,1},{6,14},{10,2},{7,15},{11,3},{20,28},{24,... | collective-permute-start | bytes 1474568 | tf_op jit(solution)/shard_map/ppermute | solution.py:590
  42.4 31.0 %copy-start.4 = (s32[256]{0:T(256)S(1)}, s32[256]{0:T(256)}, u32[]{:S(2)}) copy-start(s32[256]{0:T(256)} %param.11) | copy-start | bytes 3076
  42.4 30.9 %collective-permute-start.12 = (bf16[3,32,2560]{2,1,0:T(8,128)(2,1)S(1)}, bf16[3,32,2560]{2,1,0:T(8,128)(2,1)S(1)}, u32[]{:S(2)}, u32[]{:S(2)}) collective-permute-start(bf16[3,32,2560]{2,1,0:T(8,128)(2,1)S(1)} %get-tuple-element.52), channel_id=1, source_target_pairs={{0,12},{12,0},{1,13},{13,1},{2,14},{14,2},{3,15},{15,3},{16,28},{2... | collective-permute-start | bytes 1474568 | tf_op jit(solution)/shard_map/ppermute | solution.py:590
  47.6 26.6 %collective-permute-start.5 = (bf16[3,32,2560]{2,1,0:T(8,128)(2,1)S(1)}, bf16[3,32,2560]{2,1,0:T(8,128)(2,1)S(1)}, u32[]{:S(2)}, u32[]{:S(2)}) collective-permute-start(bf16[3,32,2560]{2,1,0:T(8,128)(2,1)S(1)} %get-tuple-element.45), channel_id=1, source_target_pairs={{0,4},{12,8},{1,5},{13,9},{2,6},{14,10},{3,7},{15,11},{16,20},{28,... | collective-permute-start | bytes 1474568 | tf_op jit(solution)/shard_map/ppermute | solution.py:590
  48.9 27.8 %collective-permute-start.6 = (bf16[3,32,2560]{2,1,0:T(8,128)(2,1)S(1)}, bf16[3,32,2560]{2,1,0:T(8,128)(2,1)S(1)}, u32[]{:S(2)}, u32[]{:S(2)}) collective-permute-start(bf16[3,32,2560]{2,1,0:T(8,128)(2,1)S(1)} %get-tuple-element.46), channel_id=1, source_target_pairs={{0,8},{12,4},{1,9},{13,5},{2,10},{14,6},{3,11},{15,7},{16,24},{28,... | collective-permute-start | bytes 1474568 | tf_op jit(solution)/shard_map/ppermute | solution.py:590
  71.4 15.9 %collective-permute-start.13 = (bf16[3,32,2560]{2,1,0:T(8,128)(2,1)S(1)}, bf16[3,32,2560]{2,1,0:T(8,128)(2,1)S(1)}, u32[]{:S(2)}, u32[]{:S(2)}) collective-permute-start(bf16[3,32,2560]{2,1,0:T(8,128)(2,1)S(1)} %get-tuple-element.57), channel_id=1, source_target_pairs={{4,8},{8,4},{5,9},{9,5},{6,10},{10,6},{7,11},{11,7},{20,24},{24,20... | collective-permute-start | bytes 1474568 | tf_op jit(solution)/shard_map/ppermute | solution.py:590

commit v4 on v3

--- a/solution.py
+++ b/solution.py
@@ -90,27 +90,29 @@
         pick_ref[picks:] = (line_at == mates[part]).astype(F32).astype(BF16)
 
 
-def band_kernel(tap_count, rows, row_count, upper, share, place_ref, taps_ref, rowband_ref, colband_ref):
+def band_kernel(
+    tap_count, rows, row_count, upper, share, place_ref, taps_ref, rowband_ref, farband_ref, colband_ref
+):
     me = place_ref[0]
     odd = lax.rem(me, 2)
     margin = tap_count // 2
-    ext = rows + 2 * HALO
-    height, depth = GROUP * rows, GROUP * ext
-    out_at = lax.broadcasted_iota(jnp.int32, (height, depth), 0)
-    in_at = lax.broadcasted_iota(jnp.int32, (height, depth), 1)
-    line = out_at % share
-    plane = (out_at // share) % GROUP
-    block = out_at // (share * GROUP)
-    step, up = block // upper, block % upper
-    row = (up * row_count + (step ^ me)) * share + line
-    place = in_at % ext
-    straight = place - HALO
-    crossed = jnp.where(place < HALO, rows + place, jnp.where(place >= rows + HALO, place - rows - 2 * HALO, straight))
-    source = jnp.where(odd == 1, straight, crossed)
-    index = jnp.where(in_at // ext == plane, source - row + margin, -1)
-    high, low = split_hi_lo(banded(index, taps_ref, tap_count))
-    rowband_ref[:height] = high
-    rowband_ref[height:] = low
+    height = GROUP * rows
+    for out_ref, depth, skip in ((rowband_ref, rows + 2 * HALO, 0), (farband_ref, HALO, rows + HALO)):
+        out_at = lax.broadcasted_iota(jnp.int32, (height, GROUP * depth), 0)
+        in_at = lax.broadcasted_iota(jnp.int32, (height, GROUP * depth), 1)
+        line = out_at % share
+        plane = (out_at // share) % GROUP
+        block = out_at // (share * GROUP)
+        step, up = block // upper, block % upper
+        row = (up * row_count + (step ^ me)) * share + line
+        place = in_at % depth + skip
+        straight = place - HALO
+        crossed = jnp.where(place < HALO, rows + place, jnp.where(place >= rows + HALO, place - rows - 2 * HALO, straight))
+        source = jnp.where(odd == 1, straight, crossed)
+        index = jnp.where(in_at // depth == plane, source - row + margin, -1)
+        high, low = split_hi_lo(banded(index, taps_ref, tap_count))
+        out_ref[:height] = high
+        out_ref[height:] = low
     width = TILE + 2 * CELL
     from_at = lax.broadcasted_iota(jnp.int32, (width, TILE), 0)
     lane = lax.broadcasted_iota(jnp.int32, (width, TILE), 1)
@@ -163,91 +165,149 @@
     )(place, raw, dark, flat)
 
 
-def lowpass_kernel(
-    groups, row_count, upper, share, wants_inner,
-    place_ref, raw_ref, near_ref, far_ref, dark_ref, flat_ref, rowband_ref, colband_ref, *rest
+def free_steps(rows, row_count, upper, share, margin):
+    def reached(me, step):
+        for up in range(upper):
+            start = (up * row_count + (me ^ step)) * share
+            if start + share - 1 + margin >= rows if me % 2 else start < margin:
+                return True
+        return False
+
+    count = 0
+    while count < row_count and not any(reached(me, count) for me in range(1, row_count - 1)):
+        count += 1
+    return count
+
+
+def smooth_lines(groups, upper, share, steps, height, row_dot, colband_ref, held_ref, smooth_ref, out_refs):
+    cols = smooth_ref.shape[1]
+    per_block = GROUP * share
+    low, high = steps[0] * upper * per_block, (steps[-1] + 1) * upper * per_block
+    count = high - low
+    for group in range(groups):
+        here = slice(group * count, (group + 1) * count)
+        level = row_dot(group, None, low, high).astype(BF16)
+        held_ref[here, :CELL] = -level
+        held_ref[here, CELL + cols :] = -level
+        level = jnp.concatenate([level.astype(F32)] * (TILE // CELL), axis=1)
+        for at_col in range(0, cols, TILE):
+            less = row_dot(group, slice(at_col, at_col + TILE), low, high) - level
+            held_ref[here, CELL + at_col : CELL + at_col + TILE] = less.astype(BF16)
+    lines = slice(0, groups * count)
+    total = jnp.zeros((groups * count, 1), F32)
+    for at_col in range(0, cols, TILE):
+        window = held_ref[lines, at_col : at_col + TILE + 2 * CELL]
+        piece = jnp.dot(window, colband_ref[0], preferred_element_type=F32) + jnp.dot(
+            window, colband_ref[1], preferred_element_type=F32
+        )
+        at_half = at_col // 2
+        smooth_ref[lines, at_half : at_half + CELL] = piece[:, :CELL]
+        smooth_ref[lines, cols // 2 + at_half : cols // 2 + at_half + CELL] = piece[:, CELL:]
+        total = total + jnp.sum(piece, axis=1, keepdims=True)
+    mean = total / cols
+    for group in range(groups):
+        for number, step in enumerate(steps):
+            for up in range(upper):
+                start = group * count + (number * upper + up) * per_block
+                centered = smooth_ref[start : start + per_block] - mean[start : start + per_block]
+                out_refs[step][group, up] = centered.astype(BF16)
+
+
+def band_rows(band_ref, values, height, low, high):
+    if high - low == height:
+        both = jnp.dot(band_ref[...], values, preferred_element_type=F32)
+    else:
+        rows = jnp.concatenate([band_ref[low:high], band_ref[height + low : height + high]], axis=0)
+        both = jnp.dot(rows, values, preferred_element_type=F32)
+    return both[: high - low] + both[high - low :]
+
+
+def near_kernel(
+    groups, row_count, upper, share, free,
+    place_ref, raw_ref, near_ref, dark_ref, flat_ref, rowband_ref, colband_ref, *rest
 ):
-    out_refs, (level_ref, dark_all_ref, absorbed_ref, held_ref, smooth_ref) = rest[:row_count], rest[row_count:]
+    out_refs, (absorbed_ref, means_ref, level_ref, dark_all_ref, held_ref, smooth_ref) = rest[:row_count], rest[row_count:]
     planes, rows, cols = raw_ref.shape
-    ext = rows + 2 * HALO
-    height = GROUP * rows
-    per_block = GROUP * share
-    spans = ((0, HALO), (HALO, rows), (HALO + rows, HALO))
-
-    @pl.when(place_ref[1] == wants_inner)
+    ext, height = rows + 2 * HALO, GROUP * rows
+    spans = ((0, HALO), (HALO, rows))
+    fields = ((near_ref[planes], near_ref[planes + 1]), (dark_ref[...], flat_ref[...]))
+    for (start, size), (darkness, brightness) in zip(spans, fields):
+        darkness = darkness.astype(F32)
+        dark_all_ref[start : start + size] = darkness
+        level_ref[start : start + size] = jnp.log(brightness.astype(F32) - darkness)
+    for plane in range(planes):
+        for (start, size), counts_ref in zip(spans, (near_ref, raw_ref)):
+            place = slice(plane * ext + start, plane * ext + start + size)
+            counts = counts_ref[plane].astype(F32)
+            absorbed = level_ref[start : start + size] - jnp.log(counts - dark_all_ref[start : start + size])
+            absorbed_ref[place] = absorbed.astype(BF16)
+            mean = jnp.sum(absorbed, axis=1, keepdims=True) / cols
+            means_ref[place] = jnp.broadcast_to(mean, (size, CELL)).astype(BF16)
+        place = slice(plane * ext + HALO + rows, (plane + 1) * ext)
+        absorbed_ref[place] = jnp.zeros((HALO, cols), BF16)
+        means_ref[place] = jnp.zeros((HALO, CELL), BF16)
+
+    def row_dot(group, span, low, high):
+        here = slice(group * GROUP * ext, (group + 1) * GROUP * ext)
+        values = means_ref[here] if span is None else absorbed_ref[here, span]
+        return band_rows(rowband_ref, values, height, low, high)
+
+    for inner, steps in ((0, range(row_count)), (1, range(free))):
+        if steps:
+
+            @pl.when(place_ref[1] == inner)
+            def _():
+                smooth_lines(
+                    groups, upper, share, steps, height, row_dot, colband_ref, held_ref, smooth_ref, out_refs
+                )
+
+
+def far_kernel(
+    groups, row_count, upper, share, free,
+    place_ref, far_ref, absorbed_ref, means_ref, rowband_ref, farband_ref, colband_ref, *rest
+):
+    out_refs, (far_absorbed_ref, far_means_ref, held_ref, smooth_ref) = rest[: row_count - free], rest[row_count - free :]
+    planes, cols = far_ref.shape[0] - 2, far_ref.shape[2]
+    rows = absorbed_ref.shape[0] // planes - 2 * HALO
+    ext, height = rows + 2 * HALO, GROUP * rows
+
+    @pl.when(place_ref[1] == 1)
     def _():
-        fields = (
-            (near_ref[planes], near_ref[planes + 1]),
-            (dark_ref[...], flat_ref[...]),
-            (far_ref[planes], far_ref[planes + 1]),
+        darkness = far_ref[planes].astype(F32)
+        level = jnp.log(far_ref[planes + 1].astype(F32) - darkness)
+        for plane in range(planes):
+            absorbed = level - jnp.log(far_ref[plane].astype(F32) - darkness)
+            place = slice(plane * HALO, (plane + 1) * HALO)
+            far_absorbed_ref[place] = absorbed.astype(BF16)
+            mean = jnp.sum(absorbed, axis=1, keepdims=True) / cols
+            far_means_ref[place] = jnp.broadcast_to(mean, (HALO, CELL)).astype(BF16)
+
+        def row_dot(group, span, low, high):
+            here = slice(group * GROUP * ext, (group + 1) * GROUP * ext)
+            there = slice(group * GROUP * HALO, (group + 1) * GROUP * HALO)
+            values = means_ref[here] if span is None else absorbed_ref[here, span]
+            others = far_means_ref[there] if span is None else far_absorbed_ref[there, span]
+            return band_rows(rowband_ref, values, height, low, high) + band_rows(farband_ref, others, height, low, high)
+
+        smooth_lines(
+            groups, upper, share, range(free, row_count), height, row_dot, colband_ref, held_ref, smooth_ref,
+            [None] * free + list(out_refs),
         )
-        for (start, size), (darkness, brightness) in zip(spans, fields):
-            darkness = darkness.astype(F32)
-            dark_all_ref[start : start + size] = darkness
-            level_ref[start : start + size] = jnp.log(brightness.astype(F32) - darkness)
-        for group in range(groups):
-            sums = []
-            for inner in range(GROUP):
-                for (start, size), counts_ref in zip(spans, (near_ref, raw_ref, far_ref)):
-                    place = inner * ext + start
-                    if start > HALO and not wants_inner:
-                        absorbed_ref[place : place + size] = jnp.zeros((size, cols), BF16)
-                        sums.append(jnp.zeros((size, 1), F32))
-                        continue
-                    counts = counts_ref[group * GROUP + inner].astype(F32)
-                    absorbed = level_ref[start : start + size] - jnp.log(counts - dark_all_ref[start : start + size])
-                    absorbed_ref[place : place + size] = absorbed.astype(BF16)
-                    sums.append(jnp.sum(absorbed, axis=1, keepdims=True))
-            means = jnp.broadcast_to(jnp.concatenate(sums, axis=0) / cols, (GROUP * ext, CELL)).astype(BF16)
-            both = jnp.dot(rowband_ref[...], means, preferred_element_type=F32)
-            level = (both[:height] + both[height:]).astype(BF16)
-            here = slice(group * height, (group + 1) * height)
-            held_ref[here, :CELL] = -level
-            held_ref[here, CELL + cols :] = -level
-            level = jnp.concatenate([level.astype(F32)] * (TILE // CELL), axis=1)
-            for at_col in range(0, cols, TILE):
-                both = jnp.dot(rowband_ref[...], absorbed_ref[:, at_col : at_col + TILE], preferred_element_type=F32)
-                less = both[:height] + both[height:] - level
-                held_ref[here, CELL + at_col : CELL + at_col + TILE] = less.astype(BF16)
-        total = jnp.zeros((groups * height, 1), F32)
-        for at_col in range(0, cols, TILE):
-            window = held_ref[:, at_col : at_col + TILE + 2 * CELL]
-            piece = jnp.dot(window, colband_ref[0], preferred_element_type=F32) + jnp.dot(
-                window, colband_ref[1], preferred_element_type=F32
-            )
-            at_half = at_col // 2
-            smooth_ref[:, at_half : at_half + CELL] = piece[:, :CELL]
-            smooth_ref[:, cols // 2 + at_half : cols // 2 + at_half + CELL] = piece[:, CELL:]
-            total = total + jnp.sum(piece, axis=1, keepdims=True)
-        mean = total / cols
-        for group in range(groups):
-            for step in range(row_count):
-                for up in range(upper):
-                    start = group * height + (step * upper + up) * per_block
-                    centered = smooth_ref[start : start + per_block] - mean[start : start + per_block]
-                    out_refs[step][group, up] = centered.astype(BF16)
-
-
-def lowpass(place, raw, near, far, dark, flat, rowband, colband, row_count, upper, share, wants_inner, after):
-    planes, rows, cols = raw.shape
-    ext = rows + 2 * HALO
+
+
+def lowpass_call(kernel, free, place, inputs, planes, rows, cols, row_count, upper, share, outs, extra, scratch, micros, after):
     groups = planes // GROUP
     shape = jax.ShapeDtypeStruct((groups, upper, GROUP * share, cols), BF16)
     return pl.pallas_call(
-        skipping(functools.partial(lowpass_kernel, groups, row_count, upper, share, wants_inner), 8, len(after)),
-        out_shape=[shape] * row_count,
-        in_specs=[pl.BlockSpec(memory_space=pltpu.SMEM)] + whole(7) + anywhere(len(after)),
-        out_specs=whole(row_count),
-        scratch_shapes=[
-            pltpu.VMEM((ext, cols), F32),
-            pltpu.VMEM((ext, cols), F32),
-            pltpu.VMEM((GROUP * ext, cols), BF16),
-            pltpu.VMEM((planes * rows, cols + 2 * CELL), BF16),
-            pltpu.VMEM((planes * rows, cols), F32),
-        ],
+        skipping(functools.partial(kernel, groups, row_count, upper, share, free), 1 + len(inputs), len(after)),
+        out_shape=[shape] * outs + extra,
+        in_specs=[pl.BlockSpec(memory_space=pltpu.SMEM)] + whole(len(inputs)) + anywhere(len(after)),
+        out_specs=whole(outs + len(extra)),
+        scratch_shapes=scratch
+        + [pltpu.VMEM((planes * rows, cols + 2 * CELL), BF16), pltpu.VMEM((planes * rows, cols), F32)],
         compiler_params=call_params(24),
-        cost_estimate=cost(6.5),
-    )(place, raw, near, far, dark, flat, rowband, colband, *after)
+        cost_estimate=cost(micros),
+    )(place, *inputs, *after)
 
 
 def route_kernel(row_count, ang_count, upper, place_ref, *rest):
@@ -313,10 +373,9 @@
             )
 
 
-def correlate(share, slots, lanes, cols, pick_ref, add, lead_ref, mate_ref, ls_ref, ms_ref):
+def pick_lines(lanes, cols, pick_ref, lead_ref, mate_ref):
     half, reach = cols // 2, SPAN // 2
-    padded, width = half + 2 * reach, CELL + 2 * reach
-    picks = share * slots
+    padded, picks = half + 2 * reach, lead_ref.shape[0]
     for parity in range(2):
         start = parity * padded
         mate_ref[:, start : start + reach] = jnp.zeros((picks, reach), BF16)
@@ -333,6 +392,32 @@
             lead_ref[:, here : here + TILE] = picked[:picks]
             place = start + reach + at_col
             mate_ref[:, place : place + TILE] = picked[picks:]
+
+
+def add_lines(lanes, first, are_leads, cols, pick_ref, some_leads_ref, some_mates_ref, lead_ref, mate_ref):
+    half, reach = cols // 2, SPAN // 2
+    padded, picks = half + 2 * reach, lead_ref.shape[0]
+    to_leads = are_leads.astype(F32)
+    rows = pl.ds(pl.multiple_of(jnp.where(are_leads, 0, picks), picks), picks)
+    mate_ref[...] = some_mates_ref[...]
+    for parity in range(2):
+        for at_col in range(0, half, TILE):
+            here = parity * half + at_col
+            picked = 0.0
+            for lane, lines in enumerate(lanes):
+                values = lines(slice(here, here + TILE))
+                at = (first + lane) * lane_width(values.shape[0])
+                picked = picked + jnp.dot(pick_ref[rows, at : at + values.shape[0]], values, preferred_element_type=F32)
+            span = slice(here, here + TILE)
+            lead_ref[:, span] = (some_leads_ref[:, span].astype(F32) + picked * to_leads).astype(BF16)
+            place = parity * padded + reach + at_col
+            span = slice(place, place + TILE)
+            mate_ref[:, span] = (some_mates_ref[:, span].astype(F32) + picked * (1.0 - to_leads)).astype(BF16)
+
+
+def correlate(share, slots, cols, add, lead_ref, mate_ref, ls_ref, ms_ref):
+    half, reach = cols // 2, SPAN // 2
+    padded, width = half + 2 * reach, CELL + 2 * reach
     cells = half // CELL
 
     def one_row(row, _):
@@ -390,13 +475,15 @@
     lanes = ang_count if 1 in parts else late
     last, loads, gives_own = 1 in parts, 0 in parts, parts == (0,)
     place_ref, *ramp_refs = take(4)
-    slot_refs, pieces, picks = take(slot_count), take(lanes - 1 if loads else lanes), take(len(parts))
+    slot_refs, pieces = take(slot_count), take(lanes - 1 if loads else lanes)
+    picks = dict(zip((0, 1) if loads else (1,), take(2 if loads else 1)))
+    some_leads_ref, some_mates_ref = take(2) if not loads else (None, None)
     (shifts_ref,) = take(1) if last else (None,)
     take(1 if has_out else 0)
     (old_ref,) = take(1) if has_old else (None,)
     (other_ref,) = take(1) if has_other else (None,)
     out_ref, result_ref = take(2)
-    (own_ref,) = take(1) if gives_own else (None,)
+    own_ref, leads_out_ref, mates_out_ref = take(3) if gives_own else (None,) * 3
     (x_ref,) = take(1) if loads else (None,)
     y_ref, in_sems, out_sems, profile_ref = take(4)
     me, turn = place_ref[0], place_ref[2]
@@ -457,7 +544,17 @@
                     values = values + old_ref[at]
                 profile_ref[at] = values
 
-            correlate(share, slots, known[:high], cols, picks[number], add, *refs)
+            lead_ref, mate_ref, *stacks = refs
+            if loads:
+                pick_lines(known[:high], cols, picks[part], lead_ref, mate_ref)
+            else:
+                are_leads = (turn ^ late) < ang_count // 2
+                add_lines(
+                    known[late:], late, are_leads, cols, picks[1], some_leads_ref, some_mates_ref, lead_ref, mate_ref
+                )
+            correlate(share, slots, cols, add, lead_ref, mate_ref, *stacks)
+        if gives_own:
+            pick_lines(known, cols, picks[1], leads_out_ref, mates_out_ref)
         result_ref[...] = select_shifts(profile_ref, shifts_ref[...], scale, width) if last else profile_ref[...]
         for copy in started:
             copy.wait()
@@ -467,16 +564,16 @@
         result_ref[...] = other_ref[...] if has_other else jnp.zeros(result_ref.shape, F32)
 
 
-def finish(place, ramp, slots, pieces, picks, shifts, out, old, other, wants_inner, parts, upper, share, half, after):
+def finish(place, ramp, slots, pieces, picks, some, shifts, out, old, other, wants_inner, parts, upper, share, half, after):
     loads, last, gives_own = 0 in parts, 1 in parts, parts == (0,)
     ang_count = len(pieces) + (1 if loads else 0)
     groups, lines_each, cols = pieces[0].shape
     lanes = ang_count if last else ang_count - late_lanes(ang_count)
     number = pair_slots(half)
     pieces = pieces[: lanes - 1] if loads else pieces
-    args = [place, *ramp, *slots, *pieces, *(picks[part] for part in parts)]
+    args = [place, *ramp, *slots, *pieces, *(picks if loads else picks[1:]), *some]
     specs = [pl.BlockSpec(memory_space=pltpu.SMEM)] + whole(3)
-    specs = specs + (anywhere if loads else whole)(len(slots) + len(pieces)) + whole(len(parts))
+    specs = specs + (anywhere if loads else whole)(len(slots) + len(pieces)) + whole(2 if loads else 1 + len(some))
     cells, width = cols // (2 * CELL), CELL + SPAN
     if last:
         args, specs = args + [shifts], specs + whole(1)
@@ -500,9 +597,14 @@
             jax.ShapeDtypeStruct(lines(ang_count), BF16),
             jax.ShapeDtypeStruct((share, shifts.shape[1] if last else 3 * width), F32),
         ]
-        + [jax.ShapeDtypeStruct(lines(1), BF16)] * gives_own,
+        + [
+            jax.ShapeDtypeStruct(lines(1), BF16),
+            jax.ShapeDtypeStruct((share * number, cols), BF16),
+            jax.ShapeDtypeStruct((share * number, cols + 2 * SPAN), BF16),
+        ]
+        * gives_own,
         in_specs=specs,
-        out_specs=anywhere(1) + whole(1 + gives_own),
+        out_specs=anywhere(1) + whole(1 + 3 * gives_own),
         scratch_shapes=[pltpu.VMEM(lines(lanes), BF16)] * loads
         + [
             pltpu.VMEM(lines(lanes if loads else late_lanes(ang_count)), BF16),
@@ -535,14 +637,15 @@
     far = lax.ppermute(far, "row", cross + [(j, i) for i, j in cross])
     near = lax.ppermute(near, "row", [(i, i ^ 1) for i in range(row_count)])
     ext = rows + 2 * HALO
-    rowband, colband = pl.pallas_call(
+    rowband, farband, colband = pl.pallas_call(
         functools.partial(band_kernel, tap_count, rows, row_count, upper, share),
         out_shape=[
             jax.ShapeDtypeStruct((2 * GROUP * rows, GROUP * ext), BF16),
+            jax.ShapeDtypeStruct((2 * GROUP * rows, GROUP * HALO), BF16),
             jax.ShapeDtypeStruct((2, TILE + 2 * CELL, TILE), BF16),
         ],
         in_specs=[pl.BlockSpec(memory_space=pltpu.SMEM)] * 2,
-        out_specs=whole(2),
+        out_specs=whole(3),
         compiler_params=call_params(),
         cost_estimate=cost(2.0),
     )(place, kernel_taps)
@@ -572,16 +675,28 @@
     ends = (0, row_count - 1)
     mine = lambda inner, source: (source in ends) != bool(inner)
 
-    def filter_rows(inner, after):
-        sent = lowpass(
-            place, raw_frames, near, far if inner else near, dark_field, flat_field, rowband, colband,
-            row_count, upper, share, inner, after,
-        )
-        slots = [sent[0]]
-        for step in range(1, row_count):
-            pairs = [(i, i ^ step) for i in range(row_count) if mine(inner, i)]
-            slots.append(lax.ppermute(sent[step], "row", pairs))
-        return slots
+    free = free_steps(rows, row_count, upper, share, tap_count // 2)
+    sizes = (planes, rows, cols, row_count, upper, share)
+    *begun, absorbed, means = lowpass_call(
+        near_kernel, free, place, [raw_frames, near, dark_field, flat_field, rowband, colband], *sizes, row_count,
+        [jax.ShapeDtypeStruct((planes * ext, cols), BF16), jax.ShapeDtypeStruct((planes * ext, CELL), BF16)],
+        [pltpu.VMEM((rows + HALO, cols), F32)] * 2, 6.5, [],
+    )
+    ended = lowpass_call(
+        far_kernel, free, place, [far, absorbed, means, rowband, farband, colband], *sizes, row_count - free, [],
+        [pltpu.VMEM((planes * HALO, cols), BF16), pltpu.VMEM((planes * HALO, CELL), BF16)], 3.5,
+        [begun[0], ramp[0], picks[0]],
+    )
+
+    def exchange(step, sent, wanted):
+        return lax.ppermute(sent, "row", [(i, i ^ step) for i in range(row_count) if wanted(i)])
+
+    any_row = lambda source: True
+    common = [begun[0] if step == 0 else exchange(step, begun[step], any_row) for step in range(free)]
+    outer = common + [exchange(step, begun[step], functools.partial(mine, 0)) for step in range(free, row_count)]
+    inner = common + [exchange(step, ended[step - free], functools.partial(mine, 1)) for step in range(free, row_count)]
+    if not free:
+        outer[0], inner[0] = begun[0], ended[0]
 
     def regroup(inner, slots, after):
         pieces = list(route(place, slots, ang_count, after))
@@ -590,19 +705,17 @@
             pieces[step - 1] = lax.ppermute(pieces[step - 1], "ang", pairs)
         return pieces
 
-    outer = filter_rows(0, [])
-    inner = filter_rows(1, [outer[0], ramp[0], picks[0]])
-    outer_lines = regroup(0, outer, inner[0])
-    inner_lines = regroup(1, inner, inner[0])
+    outer_lines = regroup(0, outer, ended[0])
+    inner_lines = regroup(1, inner, ended[0])
     ending = functools.partial(finish, place, ramp)
     out, ends_corr = ending(
-        outer, outer_lines, picks, shifts, None, None, None, 0, (0, 1), upper, share, half, inner[0]
+        outer, outer_lines, picks, [], shifts, None, None, None, 0, (0, 1), upper, share, half, ended[0]
     )
-    out, profile, own = ending(
-        inner, inner_lines, picks, shifts, out, None, None, 1, (0,), upper, share, half, ends_corr
+    out, profile, own, *some = ending(
+        inner, inner_lines, picks, [], shifts, out, None, None, 1, (0,), upper, share, half, ends_corr
     )
     filtered, correlation = ending(
-        [], [own, *inner_lines], picks, shifts, out, profile, ends_corr, 1, (1,), upper, share, half, profile
+        [], [own, *inner_lines], picks, some, shifts, out, profile, ends_corr, 1, (1,), upper, share, half, profile
     )
     return filtered.reshape(-1, share, cols), correlation
 

time: 95.1 us -> 92.6 us (0.974)
  the two profiles are of different devices: /device:TPU:21 before, /device:TPU:19 now
where the time goes in v4:
time: 92.6 us; the launch traced here: 92.2 us
  waiting for transfers between devices  36.7 us (40%)
  Pallas kernels  34.4 us (37%)
  starting transfers between devices  19.4 us (21%)
  between operations  1.12 us (1%)
    ppermute x6, waiting for transfers between devices, regroup(): pieces[step - 1] = lax.ppermute(pieces[step - 1], 'ang', pairs)  26.5 us
    pallas_call x3, Pallas kernels, finish(): pl.pallas_call(skipping(kernel, len(args) - 1), out_shape=[jax.ShapeDtype...  16.2 us
    ppermute x5, waiting for transfers between devices, exchange(): lax.ppermute(sent, 'row', [(i, i ^ step) for i in range(row_count) if wan...  10.2 us
    ppermute x6, starting transfers between devices, regroup(): pieces[step - 1] = lax.ppermute(pieces[step - 1], 'ang', pairs)  9.74 us
    ppermute x5, starting transfers between devices, exchange(): lax.ppermute(sent, 'row', [(i, i ^ step) for i in range(row_count) if wan...  8.02 us
    pallas_call x2, Pallas kernels, lowpass_call(): pl.pallas_call(skipping(functools.partial(kernel, groups, row_count, uppe...  6.73 us
    pallas_call x1, Pallas kernels, edges(): pl.pallas_call(functools.partial(edge_kernel, planes, rows), out_shape=[j...  3.32 us
    pallas_call x2, Pallas kernels, route(): pl.pallas_call(skipping(functools.partial(route_kernel, len(slots), ang_c...  3.16 us
  transfers between devices with their start and end apart: 13, of which 6 were waited for; matrix products, arithmetic and copies ran while one was open for 0% of the time, Pallas kernels for 27%

profile of v4, /device:TPU:19, one launch (start us, length us, event | category | flops | bytes accessed | tf_op | source)
XLA Modules:
  0.0 92.2 jit_solution(12036770469375693847)
XLA Ops:
  1.3 3.3 %shard_map.78 = (bf16[14,16,2560]{2,1,0:T(8,128)(2,1)}, bf16[14,16,2560]{2,1,0:T(8,128)(2,1)}) custom-call(s32[4]{0:T(128)} %pad_add_fusion.place_ref.refs_0_, bf16[12,32,2560]{2,1,0:T(8,128)(2,1)} %refs_1_.1, bf16[32,2560]{1,0:T(8,128)(2,1)} %refs_3_.1, bf16[32,2560]{1,0:T(8,128)(2,1)} %refs_4_.1), custom_call_target="tpu_custom_call" | custom-call | flops 2300000000 | bytes 65536 | tf_op jit(solution)/shard_map/pallas_call | solution.py:153
  4.6 0.7 collective-permute-start
  5.4 0.9 collective-permute-start.2
  6.3 1.3 %shard_map.77 = (bf16[2304,256]{1,0:T(8,128)(2,1)S(1)}, bf16[2304,256]{1,0:T(8,128)(2,1)S(1)}, bf16[256,256]{1,0:T(8,128)(2,1)S(1)}) custom-call(), custom_call_target="tpu_custom_call" | custom-call | flops 2070000000 | bytes 65536 | tf_op jit(solution)/shard_map/pallas_call | solution.py:652
  7.7 2.2 %shard_map.79 = (bf16[256,256]{1,0:T(8,128)(2,1)S(1)}, bf16[256,64]{1,0:T(8,128)(2,1)S(1)}, bf16[2,512,256]{2,1,0:T(8,128)(2,1)S(1)}) custom-call(s32[4]{0:T(128)S(1)} %copy-done, f32[31]{0:T(128)S(1)} %copy-done.5), custom_call_target="tpu_custom_call" | custom-call | flops 2300000000 | bytes 65536 | tf_op jit(solution)/shard_map/pallas_call | solution.py:640
  9.9 6.0 %shard_map.80 = (bf16[3,1,32,2560]{3,2,1,0:T(8,128)(2,1)S(1)}, bf16[3,1,32,2560]{3,2,1,0:T(8,128)(2,1)S(1)}, bf16[3,1,32,2560]{3,2,1,0:T(8,128)(2,1)S(1)}, bf16[...) custom-call(s32[4]{0:T(128)S(1)} %copy-done, ...), custom_call_target="tpu_custom_call" | custom-call | flops 7474999808 | bytes 65536 | tf_op jit(solution)/shard_map/pallas_call | solution.py:301
  16.1 2.6 %collective-permute-start.7 = (bf16[3,1,32,2560]{3,2,1,0:T(8,128)(2,1)S(1)}, bf16[3,1,32,2560]{3,2,1,0:T(8,128)(2,1)S(1)}, u32[]{:S(2)}, u32[]{:S(2)}) collective-permute-start(bf16[3,1,32,2560]{3,2,1,0:T(8,128)(2,1)S(1)} %get-tuple-element.53), channel_id=1, source_target_pairs={{0,2},{3,1},{4,6},{7,5},{8,10},{11,9},{12,14},{15,13},{16,18},{19,... | collective-permute-start | bytes 1474568 | tf_op jit(solution)/shard_map/ppermute | solution.py:692
  18.7 3.3 %collective-permute-start.8 = (bf16[3,1,32,2560]{3,2,1,0:T(8,128)(2,1)S(1)}, bf16[3,1,32,2560]{3,2,1,0:T(8,128)(2,1)S(1)}, u32[]{:S(2)}, u32[]{:S(2)}) collective-permute-start(bf16[3,1,32,2560]{3,2,1,0:T(8,128)(2,1)S(1)} %get-tuple-element.54), channel_id=1, source_target_pairs={{0,3},{3,0},{4,7},{7,4},{8,11},{11,8},{12,15},{15,12},{16,19},{19,... | collective-permute-start | bytes 1474568 | tf_op jit(solution)/shard_map/ppermute | solution.py:692
  22.0 1.4 %shard_map.81 = (bf16[256,384]{1,0:T(8,128)(2,1)S(1)}, bf16[256,512]{1,0:T(8,128)(2,1)S(1)}) custom-call(s32[4]{0:T(128)S(1)} %copy-done, s32[24]{0:T(128)S(1)} %copy-done.6), custom_call_target="tpu_custom_call" | custom-call | flops 1724999936 | bytes 65536 | tf_op jit(solution)/shard_map/pallas_call | solution.py:663
  24.8 1.3 %collective-permute-start.3 = (bf16[3,1,32,2560]{3,2,1,0:T(8,128)(2,1)S(1)}, bf16[3,1,32,2560]{3,2,1,0:T(8,128)(2,1)S(1)}, u32[]{:S(2)}, u32[]{:S(2)}) collective-permute-start(bf16[3,1,32,2560]{3,2,1,0:T(8,128)(2,1)S(1)} %get-tuple-element.48.refs_5_.refs_14_), channel_id=1, source_target_pairs={{1,3},{2,0},{5,7},{6,4},{9,11},{10,8},{13,15},{14,12},{17,19},{18,... | collective-permute-start | bytes 1474568 | tf_op jit(solution)/shard_map/ppermute | solution.py:692
  26.5 7.3 %collective-permute-done.8.refs_4_.refs_7_ = bf16[3,1,32,2560]{3,2,1,0:T(8,128)(2,1)S(1)} collective-permute-done((bf16[3,1,32,2560]{3,2,1,0:T(8,128)(2,1)S(1)}, bf16[3,1,32,2560]{3,2,1,0:T(8,128)(2,1)S(1)}, u32[]{:S(2)}, u32[]{:S(2)}) %collective-permute-start.8) | collective-permute-done | bytes 491552 | tf_op jit(solution)/shard_map/ppermute | solution.py:692
  33.8 1.6 %shard_map.84 = (bf16[3,32,2560]{2,1,0:T(8,128)(2,1)S(1)}, bf16[3,32,2560]{2,1,0:T(8,128)(2,1)S(1)}, bf16[3,32,2560]{2,1,0:T(8,128)(2,1)S(1)}) custom-call(s32[4]{0:T(128)S(1)} %copy-done, bf16[3,1,32,2560]{3,2,1,0:T(8,128)(2,1)S(1)} %get-tuple-element.41.refs_7_.refs_1_.refs_4_, bf16[3,1,32,2560]{3,2,1,0:T(8,128)(2,1)S(1)} %collective-permute-done.1.refs_2_.refs_5_, ...), custom_call_target="tpu_custom_call" | custom-call | flops 2300000000 | bytes 65536 | tf_op jit(solution)/shard_map/pallas_call | solution.py:331
  35.4 3.2 %collective-permute-start.9 = (bf16[3,32,2560]{2,1,0:T(8,128)(2,1)S(1)}, bf16[3,32,2560]{2,1,0:T(8,128)(2,1)S(1)}, u32[]{:S(2)}, u32[]{:S(2)}) collective-permute-start(bf16[3,32,2560]{2,1,0:T(8,128)(2,1)S(1)} %get-tuple-element.55), channel_id=1, source_target_pairs={{4,0},{8,12},{5,1},{9,13},{6,2},{10,14},{7,3},{11,15},{20,16},{24,... | collective-permute-start | bytes 1474568 | tf_op jit(solution)/shard_map/ppermute | solution.py:705
  38.7 1.3 %collective-permute-start.10 = (bf16[3,32,2560]{2,1,0:T(8,128)(2,1)S(1)}, bf16[3,32,2560]{2,1,0:T(8,128)(2,1)S(1)}, u32[]{:S(2)}, u32[]{:S(2)}) collective-permute-start(bf16[3,32,2560]{2,1,0:T(8,128)(2,1)S(1)} %get-tuple-element.56), channel_id=1, source_target_pairs={{4,12},{8,0},{5,13},{9,1},{6,14},{10,2},{7,15},{11,3},{20,28},{24,... | collective-permute-start | bytes 1474568 | tf_op jit(solution)/shard_map/ppermute | solution.py:705
  40.7 2.5 %collective-permute-done.3.refs_3_.refs_6_ = bf16[3,1,32,2560]{3,2,1,0:T(8,128)(2,1)S(1)} collective-permute-done((bf16[3,1,32,2560]{3,2,1,0:T(8,128)(2,1)S(1)}, bf16[3,1,32,2560]{3,2,1,0:T(8,128)(2,1)S(1)}, u32[]{:S(2)}, u32[]{:S(2)}) %collective-permute-start.3) | collective-permute-done | bytes 491552 | tf_op jit(solution)/shard_map/ppermute | solution.py:692
  43.2 1.6 %shard_map.83 = (bf16[3,32,2560]{2,1,0:T(8,128)(2,1)S(1)}, bf16[3,32,2560]{2,1,0:T(8,128)(2,1)S(1)}, bf16[3,32,2560]{2,1,0:T(8,128)(2,1)S(1)}) custom-call(s32[4]{0:T(128)S(1)} %copy-done, bf16[3,1,32,2560]{3,2,1,0:T(8,128)(2,1)S(1)} %get-tuple-element.41.refs_7_.refs_1_.refs_4_, bf16[3,1,32,2560]{3,2,1,0:T(8,128)(2,1)S(1)} %collective-permute-done.1.refs_2_.refs_5_, ...), custom_call_target="tpu_custom_call" | custom-call | flops 2300000000 | bytes 65536 | tf_op jit(solution)/shard_map/pallas_call | solution.py:331
  44.8 1.3 %collective-permute-start.5 = (bf16[3,32,2560]{2,1,0:T(8,128)(2,1)S(1)}, bf16[3,32,2560]{2,1,0:T(8,128)(2,1)S(1)}, u32[]{:S(2)}, u32[]{:S(2)}) collective-permute-start(bf16[3,32,2560]{2,1,0:T(8,128)(2,1)S(1)} %get-tuple-element.50), channel_id=1, source_target_pairs={{0,4},{12,8},{1,5},{13,9},{2,6},{14,10},{3,7},{15,11},{16,20},{28,... | collective-permute-start | bytes 1474568 | tf_op jit(solution)/shard_map/ppermute | solution.py:705
  46.1 1.3 %collective-permute-start.6 = (bf16[3,32,2560]{2,1,0:T(8,128)(2,1)S(1)}, bf16[3,32,2560]{2,1,0:T(8,128)(2,1)S(1)}, u32[]{:S(2)}, u32[]{:S(2)}) collective-permute-start(bf16[3,32,2560]{2,1,0:T(8,128)(2,1)S(1)} %get-tuple-element.51), channel_id=1, source_target_pairs={{0,8},{12,4},{1,9},{13,5},{2,10},{14,6},{3,11},{15,7},{16,24},{28,... | collective-permute-start | bytes 1474568 | tf_op jit(solution)/shard_map/ppermute | solution.py:705
  47.4 22.5 %collective-permute-done.9.refs_8_ = bf16[3,32,2560]{2,1,0:T(8,128)(2,1)S(1)} collective-permute-done((bf16[3,32,2560]{2,1,0:T(8,128)(2,1)S(1)}, bf16[3,32,2560]{2,1,0:T(8,128)(2,1)S(1)}, u32[]{:S(2)}, u32[]{:S(2)}) %collective-permute-start.9) | collective-permute-done | bytes 491552 | tf_op jit(solution)/shard_map/ppermute | solution.py:705
  69.9 1.9 %collective-permute-start.12 = (bf16[3,32,2560]{2,1,0:T(8,128)(2,1)S(1)}, bf16[3,32,2560]{2,1,0:T(8,128)(2,1)S(1)}, u32[]{:S(2)}, u32[]{:S(2)}) collective-permute-start(bf16[3,32,2560]{2,1,0:T(8,128)(2,1)S(1)} %get-tuple-element.61), channel_id=1, source_target_pairs={{4,8},{8,4},{5,9},{9,5},{6,10},{10,6},{7,11},{11,7},{20,24},{24,20... | collective-permute-start | bytes 1474568 | tf_op jit(solution)/shard_map/ppermute | solution.py:705
  72.5 2.7 %collective-permute-done.6.refs_9_.refs_6_ = bf16[3,32,2560]{2,1,0:T(8,128)(2,1)S(1)} collective-permute-done((bf16[3,32,2560]{2,1,0:T(8,128)(2,1)S(1)}, bf16[3,32,2560]{2,1,0:T(8,128)(2,1)S(1)}, u32[]{:S(2)}, u32[]{:S(2)}) %collective-permute-start.6) | collective-permute-done | bytes 491552 | tf_op jit(solution)/shard_map/ppermute | solution.py:705
  75.1 9.4 %shard_map.86 = (bf16[12,32,2560]{2,1,0:T(8,128)(2,1)}, f32[8,1152]{1,0:T(8,128)S(1)}, bf16[3,32,2560]{2,1,0:T(8,128)(2,1)S(1)}, bf16[128,2560]{1,0:T(8,128)(2,1)S(1)}, bf16[128,3072]{1,0:T(8,128)(2,1)S(1)}) custom-call(s32[4]{0:T(128)S(1)} %copy-done, bf16[2304,256]{1,0:T(8,128)(2,1)S(1)} %get-tuple-element.35.refs_8_.refs_1_, ...), custom_call_target="tpu_custom_call", output_to_operand_aliasing={{0}: (12, {})} | custom-call | flops 5750000128 | bytes 65536 | tf_op jit(solution)/shard_map/pallas_call | solution.py:594
  84.5 1.3 %collective-permute-done.12.refs_7_ = bf16[3,32,2560]{2,1,0:T(8,128)(2,1)S(1)} collective-permute-done((bf16[3,32,2560]{2,1,0:T(8,128)(2,1)S(1)}, bf16[3,32,2560]{2,1,0:T(8,128)(2,1)S(1)}, u32[]{:S(2)}, u32[]{:S(2)}) %collective-permute-start.12) | collective-permute-done | bytes 491552 | tf_op jit(solution)/shard_map/ppermute | solution.py:705
  85.8 6.2 %shard_map.87 = (bf16[12,32,2560]{2,1,0:T(8,128)(2,1)}, f32[8,256]{1,0:T(8,128)}) custom-call(s32[4]{0:T(128)S(1)} %copy-done, bf16[2304,256]{1,0:T(8,128)(2,1)S(1)} %get-tuple-element.35.refs_8_.refs_1_, bf16[2304,256]{1,0:T(8,128)(2,1)S(1)} %get-tuple-element.36.refs_2_, ...), custom_call_target="tpu_custom_call", output_to_operand_aliasing={{0}: (12, {})} | custom-call | flops 5750000128 | bytes 65536 | tf_op jit(solution)/shard_map/pallas_call | solution.py:594
  (28 shorter events, 4.1 us)
Async XLA Ops:
  4.6 5.2 %collective-permute-start = (bf16[14,16,2560]{2,1,0:T(8,128)(2,1)}, bf16[14,16,2560]{2,1,0:T(8,128)(2,1)S(1)}, u32[]{:S(2)}, u32[]{:S(2)}) collective-permute-start(bf16[14,16,2560]{2,1,0:T(8,128)(2,1)} %get-tuple-element.38), channel_id=1, source_target_pairs={{0,1},{1,0},{2,3},{3,2},{4,5},{5,4},{6,7},{7,6},{8,9},{9,8},{10,11... | collective-permute-start | bytes 3440648 | tf_op jit(solution)/shard_map/ppermute | solution.py:638
  5.4 2.2 %copy-start = (s32[4]{0:T(128)S(1)}, s32[4]{0:T(128)}, u32[]{:S(2)}) copy-start(s32[4]{0:T(128)} %pad_add_fusion.place_ref.refs_0_) | copy-start | bytes 52
  5.4 2.2 %copy-start.5 = (f32[31]{0:T(128)S(1)}, f32[31]{0:T(128)}, u32[]{:S(2)}) copy-start(f32[31]{0:T(128)} %taps_ref.1) | copy-start | bytes 376
  5.4 18.0 %collective-permute-start.2 = (bf16[14,16,2560]{2,1,0:T(8,128)(2,1)}, bf16[14,16,2560]{2,1,0:T(8,128)(2,1)S(1)}, u32[]{:S(2)}, u32[]{:S(2)}) collective-permute-start(bf16[14,16,2560]{2,1,0:T(8,128)(2,1)} %get-tuple-element.43), channel_id=1, source_target_pairs={{1,2},{2,1},{5,6},{6,5},{9,10},{10,9},{13,14},{14,13},{17,18},{18,... | collective-permute-start | bytes 3440648 | tf_op jit(solution)/shard_map/ppermute | solution.py:637
  7.6 2.3 %copy-start.1 = (bf16[12,32,2560]{2,1,0:T(8,128)(2,1)S(1)}, bf16[12,32,2560]{2,1,0:T(8,128)(2,1)}, u32[]{:S(2)}) copy-start(bf16[12,32,2560]{2,1,0:T(8,128)(2,1)} %refs_1_.1) | copy-start | bytes 5898244
  7.6 2.3 %copy-start.2 = (bf16[32,2560]{1,0:T(8,128)(2,1)S(1)}, bf16[32,2560]{1,0:T(8,128)(2,1)}, u32[]{:S(2)}) copy-start(bf16[32,2560]{1,0:T(8,128)(2,1)} %refs_3_.1) | copy-start | bytes 491524
  7.6 2.3 %copy-start.3 = (bf16[32,2560]{1,0:T(8,128)(2,1)S(1)}, bf16[32,2560]{1,0:T(8,128)(2,1)}, u32[]{:S(2)}) copy-start(bf16[32,2560]{1,0:T(8,128)(2,1)} %refs_4_.1) | copy-start | bytes 491524
  9.9 12.1 %copy-start.6 = (s32[24]{0:T(128)S(1)}, s32[24]{0:T(128)}, u32[]{:S(2)}) copy-start(s32[24]{0:T(128)} %partner_ref.1) | copy-start | bytes 292
  15.9 10.2 %collective-permute-start.1 = (bf16[3,1,32,2560]{3,2,1,0:T(8,128)(2,1)S(1)}, bf16[3,1,32,2560]{3,2,1,0:T(8,128)(2,1)S(1)}, u32[]{:S(2)}, u32[]{:S(2)}) collective-permute-start(bf16[3,1,32,2560]{3,2,1,0:T(8,128)(2,1)S(1)} %get-tuple-element.42), channel_id=1, source_target_pairs={{0,1},{1,0},{2,3},{3,2},{4,5},{5,4},{6,7},{7,6},{8,9},{9,8},{10,11... | collective-permute-start | bytes 1474568 | tf_op jit(solution)/shard_map/ppermute | solution.py:692
  16.1 10.4 %collective-permute-start.7 = (bf16[3,1,32,2560]{3,2,1,0:T(8,128)(2,1)S(1)}, bf16[3,1,32,2560]{3,2,1,0:T(8,128)(2,1)S(1)}, u32[]{:S(2)}, u32[]{:S(2)}) collective-permute-start(bf16[3,1,32,2560]{3,2,1,0:T(8,128)(2,1)S(1)} %get-tuple-element.53), channel_id=1, source_target_pairs={{0,2},{3,1},{4,6},{7,5},{8,10},{11,9},{12,14},{15,13},{16,18},{19,... | collective-permute-start | bytes 1474568 | tf_op jit(solution)/shard_map/ppermute | solution.py:692
  18.7 15.1 %collective-permute-start.8 = (bf16[3,1,32,2560]{3,2,1,0:T(8,128)(2,1)S(1)}, bf16[3,1,32,2560]{3,2,1,0:T(8,128)(2,1)S(1)}, u32[]{:S(2)}, u32[]{:S(2)}) collective-permute-start(bf16[3,1,32,2560]{3,2,1,0:T(8,128)(2,1)S(1)} %get-tuple-element.54), channel_id=1, source_target_pairs={{0,3},{3,0},{4,7},{7,4},{8,11},{11,8},{12,15},{15,12},{16,19},{19,... | collective-permute-start | bytes 1474568 | tf_op jit(solution)/shard_map/ppermute | solution.py:692
  24.1 16.6 %collective-permute-start.4 = (bf16[3,1,32,2560]{3,2,1,0:T(8,128)(2,1)S(1)}, bf16[3,1,32,2560]{3,2,1,0:T(8,128)(2,1)S(1)}, u32[]{:S(2)}, u32[]{:S(2)}) collective-permute-start(bf16[3,1,32,2560]{3,2,1,0:T(8,128)(2,1)S(1)} %get-tuple-element.49), channel_id=1, source_target_pairs={{1,2},{2,1},{5,6},{6,5},{9,10},{10,9},{13,14},{14,13},{17,18},{18,... | collective-permute-start | bytes 1474568 | tf_op jit(solution)/shard_map/ppermute | solution.py:692
  24.8 18.4 %collective-permute-start.3 = (bf16[3,1,32,2560]{3,2,1,0:T(8,128)(2,1)S(1)}, bf16[3,1,32,2560]{3,2,1,0:T(8,128)(2,1)S(1)}, u32[]{:S(2)}, u32[]{:S(2)}) collective-permute-start(bf16[3,1,32,2560]{3,2,1,0:T(8,128)(2,1)S(1)} %get-tuple-element.48.refs_5_.refs_14_), channel_id=1, source_target_pairs={{1,3},{2,0},{5,7},{6,4},{9,11},{10,8},{13,15},{14,12},{17,19},{18,... | collective-permute-start | bytes 1474568 | tf_op jit(solution)/shard_map/ppermute | solution.py:692
  35.4 34.4 %collective-permute-start.9 = (bf16[3,32,2560]{2,1,0:T(8,128)(2,1)S(1)}, bf16[3,32,2560]{2,1,0:T(8,128)(2,1)S(1)}, u32[]{:S(2)}, u32[]{:S(2)}) collective-permute-start(bf16[3,32,2560]{2,1,0:T(8,128)(2,1)S(1)} %get-tuple-element.55), channel_id=1, source_target_pairs={{4,0},{8,12},{5,1},{9,13},{6,2},{10,14},{7,3},{11,15},{20,16},{24,... | collective-permute-start | bytes 1474568 | tf_op jit(solution)/shard_map/ppermute | solution.py:705
  38.7 33.1 %collective-permute-start.10 = (bf16[3,32,2560]{2,1,0:T(8,128)(2,1)S(1)}, bf16[3,32,2560]{2,1,0:T(8,128)(2,1)S(1)}, u32[]{:S(2)}, u32[]{:S(2)}) collective-permute-start(bf16[3,32,2560]{2,1,0:T(8,128)(2,1)S(1)} %get-tuple-element.56), channel_id=1, source_target_pairs={{4,12},{8,0},{5,13},{9,1},{6,14},{10,2},{7,15},{11,3},{20,28},{24,... | collective-permute-start | bytes 1474568 | tf_op jit(solution)/shard_map/ppermute | solution.py:705
  40.0 31.8 %copy-start.4 = (s32[256]{0:T(256)S(1)}, s32[256]{0:T(256)}, u32[]{:S(2)}) copy-start(s32[256]{0:T(256)} %param.11) | copy-start | bytes 3076
  40.0 31.8 %collective-permute-start.11 = (bf16[3,32,2560]{2,1,0:T(8,128)(2,1)S(1)}, bf16[3,32,2560]{2,1,0:T(8,128)(2,1)S(1)}, u32[]{:S(2)}, u32[]{:S(2)}) collective-permute-start(bf16[3,32,2560]{2,1,0:T(8,128)(2,1)S(1)} %get-tuple-element.57), channel_id=1, source_target_pairs={{0,12},{12,0},{1,13},{13,1},{2,14},{14,2},{3,15},{15,3},{16,28},{2... | collective-permute-start | bytes 1474568 | tf_op jit(solution)/shard_map/ppermute | solution.py:705
  44.8 27.7 %collective-permute-start.5 = (bf16[3,32,2560]{2,1,0:T(8,128)(2,1)S(1)}, bf16[3,32,2560]{2,1,0:T(8,128)(2,1)S(1)}, u32[]{:S(2)}, u32[]{:S(2)}) collective-permute-start(bf16[3,32,2560]{2,1,0:T(8,128)(2,1)S(1)} %get-tuple-element.50), channel_id=1, source_target_pairs={{0,4},{12,8},{1,5},{13,9},{2,6},{14,10},{3,7},{15,11},{16,20},{28,... | collective-permute-start | bytes 1474568 | tf_op jit(solution)/shard_map/ppermute | solution.py:705
  46.1 29.1 %collective-permute-start.6 = (bf16[3,32,2560]{2,1,0:T(8,128)(2,1)S(1)}, bf16[3,32,2560]{2,1,0:T(8,128)(2,1)S(1)}, u32[]{:S(2)}, u32[]{:S(2)}) collective-permute-start(bf16[3,32,2560]{2,1,0:T(8,128)(2,1)S(1)} %get-tuple-element.51), channel_id=1, source_target_pairs={{0,8},{12,4},{1,9},{13,5},{2,10},{14,6},{3,11},{15,7},{16,24},{28,... | collective-permute-start | bytes 1474568 | tf_op jit(solution)/shard_map/ppermute | solution.py:705
  69.9 16.0 %collective-permute-start.12 = (bf16[3,32,2560]{2,1,0:T(8,128)(2,1)S(1)}, bf16[3,32,2560]{2,1,0:T(8,128)(2,1)S(1)}, u32[]{:S(2)}, u32[]{:S(2)}) collective-permute-start(bf16[3,32,2560]{2,1,0:T(8,128)(2,1)S(1)} %get-tuple-element.61), channel_id=1, source_target_pairs={{4,8},{8,4},{5,9},{9,5},{6,10},{10,6},{7,11},{11,7},{20,24},{24,20... | collective-permute-start | bytes 1474568 | tf_op jit(solution)/shard_map/ppermute | solution.py:705

commit v5 on v4

--- a/solution.py
+++ b/solution.py
@@ -310,30 +310,34 @@
     )(place, *inputs, *after)
 
 
-def route_kernel(row_count, ang_count, upper, place_ref, *rest):
-    slots, targets, sems = rest[:row_count], rest[row_count:-1], rest[-1]
+def route_kernel(row_count, upper, steps, sets, place_ref, *rest):
+    held, (targets, sems) = rest[: sets * row_count], (rest[sets * row_count : -1], rest[-1])
     me, turn = place_ref[0], place_ref[2]
-    for step in range(1, ang_count):
+    for at, (step, wanted) in enumerate(steps):
         target = turn ^ step
-        slot = me ^ (target // upper)
-        for number in range(row_count):
-
-            @pl.when(slot == number)
+        owner = target // upper
+        inner = jnp.logical_and(owner > 0, owner < row_count - 1).astype(jnp.int32)
+        first = inner * row_count if wanted is None else wanted * row_count
+        for number, slot_ref in enumerate(held):
+
+            @pl.when(first + (me ^ owner) == number)
             def _():
-                pltpu.make_async_copy(slots[number].at[:, target % upper], targets[step - 1], sems.at[step]).start()
-
-    for step in range(1, ang_count):
-        pltpu.make_async_copy(slots[0].at[:, 0], targets[step - 1], sems.at[step]).wait()
-
-
-def route(place, slots, ang_count, after):
-    groups, upper, lines, cols = slots[0].shape
+                pltpu.make_async_copy(slot_ref.at[:, target % upper], targets[at], sems.at[at]).start()
+
+    for at in range(len(steps)):
+        pltpu.make_async_copy(held[0].at[:, 0], targets[at], sems.at[at]).wait()
+
+
+def route(place, sets, steps, upper, after):
+    row_count = len(sets[0])
+    groups, _, lines, cols = sets[0][0].shape
+    slots = [slot for held in sets for slot in held]
     return pl.pallas_call(
-        skipping(functools.partial(route_kernel, len(slots), ang_count, upper), 1 + len(slots)),
-        out_shape=[jax.ShapeDtypeStruct((groups, lines, cols), BF16)] * (ang_count - 1),
+        skipping(functools.partial(route_kernel, row_count, upper, steps, len(sets)), 1 + len(slots)),
+        out_shape=[jax.ShapeDtypeStruct((groups, lines, cols), BF16)] * len(steps),
         in_specs=[pl.BlockSpec(memory_space=pltpu.SMEM)] + anywhere(len(slots) + 1),
-        out_specs=whole(ang_count - 1),
-        scratch_shapes=[pltpu.SemaphoreType.DMA((ang_count,))],
+        out_specs=whole(len(steps)),
+        scratch_shapes=[pltpu.SemaphoreType.DMA((len(steps),))],
         compiler_params=call_params(8),
         cost_estimate=cost(2.0),
     )(place, *slots, after)
@@ -698,15 +702,18 @@
     if not free:
         outer[0], inner[0] = begun[0], ended[0]
 
-    def regroup(inner, slots, after):
-        pieces = list(route(place, slots, ang_count, after))
-        for step in range(1, ang_count):
-            pairs = [(i, i ^ step) for i in range(ang_count) if mine(inner, (i ^ step) // upper)]
-            pieces[step - 1] = lax.ppermute(pieces[step - 1], "ang", pairs)
-        return pieces
-
-    outer_lines = regroup(0, outer, ended[0])
-    inner_lines = regroup(1, inner, ended[0])
+    def send(step, lines, wanted):
+        pairs = [(i, i ^ step) for i in range(ang_count) if wanted((i ^ step) // upper)]
+        return lax.ppermute(lines, "ang", pairs)
+
+    short, long = range(1, ang_count // 2), range(max(1, ang_count // 2), ang_count)
+    routed = route(place, [outer], [(step, 0) for step in long], upper, ended[0])
+    outer_long = [send(step, lines, functools.partial(mine, 0)) for step, lines in zip(long, routed)]
+    steps = [(step, 1) for step in long] + [(step, None) for step in short]
+    routed = route(place, [outer, inner], steps, upper, ended[0])
+    shared = [send(step, lines, any_row) for step, lines in zip(short, routed[len(long) :])]
+    inner_long = [send(step, lines, functools.partial(mine, 1)) for step, lines in zip(long, routed)]
+    outer_lines, inner_lines = shared + outer_long, shared + inner_long
     ending = functools.partial(finish, place, ramp)
     out, ends_corr = ending(
         outer, outer_lines, picks, [], shifts, None, None, None, 0, (0, 1), upper, share, half, ended[0]

time: 92.6 us -> 89.5 us (0.967)
  the two profiles are of different devices: /device:TPU:19 before, /device:TPU:0 now
where the time goes in v5:
time: 89.5 us; the launch traced here: 89.2 us
  Pallas kernels  34.1 us (38%)
  waiting for transfers between devices  28.6 us (32%)
  starting transfers between devices  24.9 us (28%)
  between operations  1.1 us (1%)
    ppermute x5, waiting for transfers between devices, send(): return lax.ppermute(lines, 'ang', pairs)  19.1 us
    pallas_call x3, Pallas kernels, finish(): pl.pallas_call(skipping(kernel, len(args) - 1), out_shape=[jax.ShapeDtype...  16.1 us
    ppermute x5, starting transfers between devices, send(): return lax.ppermute(lines, 'ang', pairs)  14.3 us
    ppermute x5, waiting for transfers between devices, exchange(): lax.ppermute(sent, 'row', [(i, i ^ step) for i in range(row_count) if wan...  9.48 us
    ppermute x5, starting transfers between devices, exchange(): lax.ppermute(sent, 'row', [(i, i ^ step) for i in range(row_count) if wan...  9.39 us
    pallas_call x2, Pallas kernels, lowpass_call(): pl.pallas_call(skipping(functools.partial(kernel, groups, row_count, uppe...  6.73 us
    pallas_call x1, Pallas kernels, edges(): pl.pallas_call(functools.partial(edge_kernel, planes, rows), out_shape=[j...  3.45 us
    pallas_call x2, Pallas kernels, route(): pl.pallas_call(skipping(functools.partial(route_kernel, row_count, upper,...  2.87 us
  transfers between devices with their start and end apart: 12, of which 4 were waited for; matrix products, arithmetic and copies ran while one was open for 0% of the time, Pallas kernels for 33%

profile of v5, /device:TPU:0, one launch (start us, length us, event | category | flops | bytes accessed | tf_op | source)
XLA Modules:
  0.0 89.2 jit_solution(12103337370381713140)
XLA Ops:
  1.2 3.5 %shard_map.78 = (bf16[14,16,2560]{2,1,0:T(8,128)(2,1)}, bf16[14,16,2560]{2,1,0:T(8,128)(2,1)}) custom-call(s32[4]{0:T(128)} %pad_add_fusion.place_ref.refs_0_, bf16[12,32,2560]{2,1,0:T(8,128)(2,1)} %refs_1_.1, bf16[32,2560]{1,0:T(8,128)(2,1)} %refs_3_.1, bf16[32,2560]{1,0:T(8,128)(2,1)} %refs_4_.1), custom_call_target="tpu_custom_call" | custom-call | flops 2300000000 | bytes 65536 | tf_op jit(solution)/shard_map/pallas_call | solution.py:153
  5.2 0.7 collective-permute-start.2
  5.9 1.4 %shard_map.81 = (bf16[256,384]{1,0:T(8,128)(2,1)S(1)}, bf16[256,512]{1,0:T(8,128)(2,1)S(1)}) custom-call(s32[4]{0:T(128)S(1)} %copy-done, s32[24]{0:T(128)S(1)} %copy-done.5), custom_call_target="tpu_custom_call" | custom-call | flops 1724999936 | bytes 65536 | tf_op jit(solution)/shard_map/pallas_call | solution.py:667
  7.3 1.3 %shard_map.77 = (bf16[2304,256]{1,0:T(8,128)(2,1)S(1)}, bf16[2304,256]{1,0:T(8,128)(2,1)S(1)}, bf16[256,256]{1,0:T(8,128)(2,1)S(1)}) custom-call(), custom_call_target="tpu_custom_call" | custom-call | flops 2070000000 | bytes 65536 | tf_op jit(solution)/shard_map/pallas_call | solution.py:656
  8.7 2.2 %shard_map.79 = (bf16[256,256]{1,0:T(8,128)(2,1)S(1)}, bf16[256,64]{1,0:T(8,128)(2,1)S(1)}, bf16[2,512,256]{2,1,0:T(8,128)(2,1)S(1)}) custom-call(s32[4]{0:T(128)S(1)} %copy-done, f32[31]{0:T(128)S(1)} %copy-done.6), custom_call_target="tpu_custom_call" | custom-call | flops 2300000000 | bytes 65536 | tf_op jit(solution)/shard_map/pallas_call | solution.py:644
  11.0 6.0 %shard_map.80 = (bf16[3,1,32,2560]{3,2,1,0:T(8,128)(2,1)S(1)}, bf16[3,1,32,2560]{3,2,1,0:T(8,128)(2,1)S(1)}, bf16[3,1,32,2560]{3,2,1,0:T(8,128)(2,1)S(1)}, bf16[...) custom-call(s32[4]{0:T(128)S(1)} %copy-done, ...), custom_call_target="tpu_custom_call" | custom-call | flops 7474999808 | bytes 65536 | tf_op jit(solution)/shard_map/pallas_call | solution.py:301
  17.0 2.2 %collective-permute-start.1 = (bf16[3,1,32,2560]{3,2,1,0:T(8,128)(2,1)S(1)}, bf16[3,1,32,2560]{3,2,1,0:T(8,128)(2,1)S(1)}, u32[]{:S(2)}, u32[]{:S(2)}) collective-permute-start(bf16[3,1,32,2560]{3,2,1,0:T(8,128)(2,1)S(1)} %get-tuple-element.41), channel_id=1, source_target_pairs={{0,1},{1,0},{2,3},{3,2},{4,5},{5,4},{6,7},{7,6},{8,9},{9,8},{10,11... | collective-permute-start | bytes 1474568 | tf_op jit(solution)/shard_map/ppermute | solution.py:696
  19.2 2.8 %collective-permute-start.5 = (bf16[3,1,32,2560]{3,2,1,0:T(8,128)(2,1)S(1)}, bf16[3,1,32,2560]{3,2,1,0:T(8,128)(2,1)S(1)}, u32[]{:S(2)}, u32[]{:S(2)}) collective-permute-start(bf16[3,1,32,2560]{3,2,1,0:T(8,128)(2,1)S(1)} %get-tuple-element.49), channel_id=1, source_target_pairs={{0,2},{3,1},{4,6},{7,5},{8,10},{11,9},{12,14},{15,13},{16,18},{19,... | collective-permute-start | bytes 1474568 | tf_op jit(solution)/shard_map/ppermute | solution.py:696
  22.0 2.4 %collective-permute-start.6 = (bf16[3,1,32,2560]{3,2,1,0:T(8,128)(2,1)S(1)}, bf16[3,1,32,2560]{3,2,1,0:T(8,128)(2,1)S(1)}, u32[]{:S(2)}, u32[]{:S(2)}) collective-permute-start(bf16[3,1,32,2560]{3,2,1,0:T(8,128)(2,1)S(1)} %get-tuple-element.50), channel_id=1, source_target_pairs={{0,3},{3,0},{4,7},{7,4},{8,11},{11,8},{12,15},{15,12},{16,19},{19,... | collective-permute-start | bytes 1474568 | tf_op jit(solution)/shard_map/ppermute | solution.py:696
  24.4 0.7 shard_map.82
  25.1 0.7 collective-permute-start.4
  25.8 1.3 %collective-permute-start.3 = (bf16[3,1,32,2560]{3,2,1,0:T(8,128)(2,1)S(1)}, bf16[3,1,32,2560]{3,2,1,0:T(8,128)(2,1)S(1)}, u32[]{:S(2)}, u32[]{:S(2)}) collective-permute-start(bf16[3,1,32,2560]{3,2,1,0:T(8,128)(2,1)S(1)} %get-tuple-element.47.refs_9_.refs_5_.refs_14_), channel_id=1, source_target_pairs={{1,3},{2,0},{5,7},{6,4},{9,11},{10,8},{13,15},{14,12},{17,19},{18,... | collective-permute-start | bytes 1474568 | tf_op jit(solution)/shard_map/ppermute | solution.py:696
  27.1 1.1 %collective-permute-done.5.refs_3_.refs_6_ = bf16[3,1,32,2560]{3,2,1,0:T(8,128)(2,1)S(1)} collective-permute-done((bf16[3,1,32,2560]{3,2,1,0:T(8,128)(2,1)S(1)}, bf16[3,1,32,2560]{3,2,1,0:T(8,128)(2,1)S(1)}, u32[]{:S(2)}, u32[]{:S(2)}) %collective-permute-start.5) | collective-permute-done | bytes 491552 | tf_op jit(solution)/shard_map/ppermute | solution.py:696
  28.3 7.8 %collective-permute-done.6.refs_4_.refs_7_ = bf16[3,1,32,2560]{3,2,1,0:T(8,128)(2,1)S(1)} collective-permute-done((bf16[3,1,32,2560]{3,2,1,0:T(8,128)(2,1)S(1)}, bf16[3,1,32,2560]{3,2,1,0:T(8,128)(2,1)S(1)}, u32[]{:S(2)}, u32[]{:S(2)}) %collective-permute-start.6) | collective-permute-done | bytes 491552 | tf_op jit(solution)/shard_map/ppermute | solution.py:696
  36.1 1.2 %shard_map.84 = (bf16[3,32,2560]{2,1,0:T(8,128)(2,1)S(1)}, bf16[3,32,2560]{2,1,0:T(8,128)(2,1)S(1)}) custom-call(s32[4]{0:T(128)S(1)} %copy-done, bf16[3,1,32,2560]{3,2,1,0:T(8,128)(2,1)S(1)} %get-tuple-element.40.refs_7_.refs_1_.refs_5_.refs_4_, bf16[3,1,32,2560]{3,2,1,0:T(8,128)(2,1)S(1)} %collective-permute-done.1.refs_2_.refs_6_.refs_5_, ...), custom_call_target="tpu_custom_call" | custom-call | flops 2300000000 | bytes 65536 | tf_op jit(solution)/shard_map/pallas_call | solution.py:335
  37.3 1.3 %collective-permute-start.9 = (bf16[3,32,2560]{2,1,0:T(8,128)(2,1)S(1)}, bf16[3,32,2560]{2,1,0:T(8,128)(2,1)S(1)}, u32[]{:S(2)}, u32[]{:S(2)}) collective-permute-start(bf16[3,32,2560]{2,1,0:T(8,128)(2,1)S(1)} %get-tuple-element.54), channel_id=1, source_target_pairs={{4,12},{8,0},{5,13},{9,1},{6,14},{10,2},{7,15},{11,3},{20,28},{24,... | collective-permute-start | bytes 1474568 | tf_op jit(solution)/shard_map/ppermute | solution.py:707
  38.6 5.5 %collective-permute-start.10 = (bf16[3,32,2560]{2,1,0:T(8,128)(2,1)S(1)}, bf16[3,32,2560]{2,1,0:T(8,128)(2,1)S(1)}, u32[]{:S(2)}, u32[]{:S(2)}) collective-permute-start(bf16[3,32,2560]{2,1,0:T(8,128)(2,1)S(1)} %get-tuple-element.55), channel_id=1, source_target_pairs={{0,12},{12,0},{1,13},{13,1},{2,14},{14,2},{3,15},{15,3},{16,28},{2... | collective-permute-start | bytes 1474568 | tf_op jit(solution)/shard_map/ppermute | solution.py:707
  44.7 1.6 %shard_map.83 = (bf16[3,32,2560]{2,1,0:T(8,128)(2,1)S(1)}, bf16[3,32,2560]{2,1,0:T(8,128)(2,1)S(1)}, bf16[3,32,2560]{2,1,0:T(8,128)(2,1)S(1)}) custom-call(s32[4]{0:T(128)S(1)} %copy-done, bf16[3,1,32,2560]{3,2,1,0:T(8,128)(2,1)S(1)} %get-tuple-element.40.refs_7_.refs_1_.refs_5_.refs_4_, ...), custom_call_target="tpu_custom_call" | custom-call | flops 2300000000 | bytes 65536 | tf_op jit(solution)/shard_map/pallas_call | solution.py:335
  46.4 2.2 %collective-permute-start.7 = (bf16[3,32,2560]{2,1,0:T(8,128)(2,1)S(1)}, bf16[3,32,2560]{2,1,0:T(8,128)(2,1)S(1)}, u32[]{:S(2)}, u32[]{:S(2)}) collective-permute-start(bf16[3,32,2560]{2,1,0:T(8,128)(2,1)S(1)} %get-tuple-element.51), channel_id=1, source_target_pairs={{0,4},{4,0},{8,12},{12,8},{1,5},{5,1},{9,13},{13,9},{2,6},{6,2},{1... | collective-permute-start | bytes 1474568 | tf_op jit(solution)/shard_map/ppermute | solution.py:707
  48.6 4.5 %collective-permute-start.8 = (bf16[3,32,2560]{2,1,0:T(8,128)(2,1)S(1)}, bf16[3,32,2560]{2,1,0:T(8,128)(2,1)S(1)}, u32[]{:S(2)}, u32[]{:S(2)}) collective-permute-start(bf16[3,32,2560]{2,1,0:T(8,128)(2,1)S(1)} %get-tuple-element.52), channel_id=1, source_target_pairs={{0,8},{12,4},{1,9},{13,5},{2,10},{14,6},{3,11},{15,7},{16,24},{28,... | collective-permute-start | bytes 1474568 | tf_op jit(solution)/shard_map/ppermute | solution.py:707
  53.1 0.7 collective-permute-start.11
  53.8 19.1 %collective-permute-done.9.refs_9_ = bf16[3,32,2560]{2,1,0:T(8,128)(2,1)S(1)} collective-permute-done((bf16[3,32,2560]{2,1,0:T(8,128)(2,1)S(1)}, bf16[3,32,2560]{2,1,0:T(8,128)(2,1)S(1)}, u32[]{:S(2)}, u32[]{:S(2)}) %collective-permute-start.9) | collective-permute-done | bytes 491552 | tf_op jit(solution)/shard_map/ppermute | solution.py:707
  72.9 14.2 %shard_map.85 = (bf16[12,32,2560]{2,1,0:T(8,128)(2,1)}, f32[8,256]{1,0:T(8,128)S(1)}) custom-call(s32[4]{0:T(128)S(1)} %copy-done, bf16[2304,256]{1,0:T(8,128)(2,1)S(1)} %get-tuple-element.34.refs_8_.refs_1_, bf16[2304,256]{1,0:T(8,128)(2,1)S(1)} %get-tuple-element.35.refs_2_, bf16[256,256]{1,0:T(8,128)(2,1)S(1)} %get-tuple-element.36.refs_3_, ...), custom_call_target="tpu_custom_call" | custom-call | flops 11500000256 | bytes 65536 | tf_op jit(solution)/shard_map/pallas_call | solution.py:598
  87.8 1.2 %shard_map.87 = (bf16[12,32,2560]{2,1,0:T(8,128)(2,1)}, f32[8,256]{1,0:T(8,128)}) custom-call(s32[4]{0:T(128)S(1)} %copy-done, bf16[2304,256]{1,0:T(8,128)(2,1)S(1)} %get-tuple-element.34.refs_8_.refs_1_, bf16[2304,256]{1,0:T(8,128)(2,1)S(1)} %get-tuple-element.35.refs_2_, ...), custom_call_target="tpu_custom_call", output_to_operand_aliasing={{0}: (12, {})} | custom-call | flops 5750000128 | bytes 65536 | tf_op jit(solution)/shard_map/pallas_call | solution.py:598
  (26 shorter events, 2.3 us)
Async XLA Ops:
  1.2 4.7 %copy-start = (s32[4]{0:T(128)S(1)}, s32[4]{0:T(128)}, u32[]{:S(2)}) copy-start(s32[4]{0:T(128)} %pad_add_fusion.place_ref.refs_0_) | copy-start | bytes 52
  1.2 4.7 %copy-start.5 = (s32[24]{0:T(128)S(1)}, s32[24]{0:T(128)}, u32[]{:S(2)}) copy-start(s32[24]{0:T(128)} %partner_ref.1) | copy-start | bytes 292
  4.7 6.3 %collective-permute-start = (bf16[14,16,2560]{2,1,0:T(8,128)(2,1)}, bf16[14,16,2560]{2,1,0:T(8,128)(2,1)S(1)}, u32[]{:S(2)}, u32[]{:S(2)}) collective-permute-start(bf16[14,16,2560]{2,1,0:T(8,128)(2,1)} %get-tuple-element.37), channel_id=1, source_target_pairs={{0,1},{1,0},{2,3},{3,2},{4,5},{5,4},{6,7},{7,6},{8,9},{9,8},{10,11... | collective-permute-start | bytes 3440648 | tf_op jit(solution)/shard_map/ppermute | solution.py:642
  5.2 19.2 %collective-permute-start.2 = (bf16[14,16,2560]{2,1,0:T(8,128)(2,1)}, bf16[14,16,2560]{2,1,0:T(8,128)(2,1)S(1)}, u32[]{:S(2)}, u32[]{:S(2)}) collective-permute-start(bf16[14,16,2560]{2,1,0:T(8,128)(2,1)} %get-tuple-element.42), channel_id=1, source_target_pairs={{1,2},{2,1},{5,6},{6,5},{9,10},{10,9},{13,14},{14,13},{17,18},{18,... | collective-permute-start | bytes 3440648 | tf_op jit(solution)/shard_map/ppermute | solution.py:641
  7.3 1.4 %copy-start.6 = (f32[31]{0:T(128)S(1)}, f32[31]{0:T(128)}, u32[]{:S(2)}) copy-start(f32[31]{0:T(128)} %taps_ref.1) | copy-start | bytes 376
  8.7 2.3 %copy-start.1 = (bf16[12,32,2560]{2,1,0:T(8,128)(2,1)S(1)}, bf16[12,32,2560]{2,1,0:T(8,128)(2,1)}, u32[]{:S(2)}) copy-start(bf16[12,32,2560]{2,1,0:T(8,128)(2,1)} %refs_1_.1) | copy-start | bytes 5898244
  8.7 2.3 %copy-start.2 = (bf16[32,2560]{1,0:T(8,128)(2,1)S(1)}, bf16[32,2560]{1,0:T(8,128)(2,1)}, u32[]{:S(2)}) copy-start(bf16[32,2560]{1,0:T(8,128)(2,1)} %refs_3_.1) | copy-start | bytes 491524
  8.7 2.3 %copy-start.3 = (bf16[32,2560]{1,0:T(8,128)(2,1)S(1)}, bf16[32,2560]{1,0:T(8,128)(2,1)}, u32[]{:S(2)}) copy-start(bf16[32,2560]{1,0:T(8,128)(2,1)} %refs_4_.1) | copy-start | bytes 491524
  17.0 10.2 %collective-permute-start.1 = (bf16[3,1,32,2560]{3,2,1,0:T(8,128)(2,1)S(1)}, bf16[3,1,32,2560]{3,2,1,0:T(8,128)(2,1)S(1)}, u32[]{:S(2)}, u32[]{:S(2)}) collective-permute-start(bf16[3,1,32,2560]{3,2,1,0:T(8,128)(2,1)S(1)} %get-tuple-element.41), channel_id=1, source_target_pairs={{0,1},{1,0},{2,3},{3,2},{4,5},{5,4},{6,7},{7,6},{8,9},{9,8},{10,11... | collective-permute-start | bytes 1474568 | tf_op jit(solution)/shard_map/ppermute | solution.py:696
  19.2 9.1 %collective-permute-start.5 = (bf16[3,1,32,2560]{3,2,1,0:T(8,128)(2,1)S(1)}, bf16[3,1,32,2560]{3,2,1,0:T(8,128)(2,1)S(1)}, u32[]{:S(2)}, u32[]{:S(2)}) collective-permute-start(bf16[3,1,32,2560]{3,2,1,0:T(8,128)(2,1)S(1)} %get-tuple-element.49), channel_id=1, source_target_pairs={{0,2},{3,1},{4,6},{7,5},{8,10},{11,9},{12,14},{15,13},{16,18},{19,... | collective-permute-start | bytes 1474568 | tf_op jit(solution)/shard_map/ppermute | solution.py:696
  22.0 14.1 %collective-permute-start.6 = (bf16[3,1,32,2560]{3,2,1,0:T(8,128)(2,1)S(1)}, bf16[3,1,32,2560]{3,2,1,0:T(8,128)(2,1)S(1)}, u32[]{:S(2)}, u32[]{:S(2)}) collective-permute-start(bf16[3,1,32,2560]{3,2,1,0:T(8,128)(2,1)S(1)} %get-tuple-element.50), channel_id=1, source_target_pairs={{0,3},{3,0},{4,7},{7,4},{8,11},{11,8},{12,15},{15,12},{16,19},{19,... | collective-permute-start | bytes 1474568 | tf_op jit(solution)/shard_map/ppermute | solution.py:696
  25.1 19.1 %collective-permute-start.4 = (bf16[3,1,32,2560]{3,2,1,0:T(8,128)(2,1)S(1)}, bf16[3,1,32,2560]{3,2,1,0:T(8,128)(2,1)S(1)}, u32[]{:S(2)}, u32[]{:S(2)}) collective-permute-start(bf16[3,1,32,2560]{3,2,1,0:T(8,128)(2,1)S(1)} %get-tuple-element.48), channel_id=1, source_target_pairs={{1,2},{2,1},{5,6},{6,5},{9,10},{10,9},{13,14},{14,13},{17,18},{18,... | collective-permute-start | bytes 1474568 | tf_op jit(solution)/shard_map/ppermute | solution.py:696
  25.8 18.9 %collective-permute-start.3 = (bf16[3,1,32,2560]{3,2,1,0:T(8,128)(2,1)S(1)}, bf16[3,1,32,2560]{3,2,1,0:T(8,128)(2,1)S(1)}, u32[]{:S(2)}, u32[]{:S(2)}) collective-permute-start(bf16[3,1,32,2560]{3,2,1,0:T(8,128)(2,1)S(1)} %get-tuple-element.47.refs_9_.refs_5_.refs_14_), channel_id=1, source_target_pairs={{1,3},{2,0},{5,7},{6,4},{9,11},{10,8},{13,15},{14,12},{17,19},{18,... | collective-permute-start | bytes 1474568 | tf_op jit(solution)/shard_map/ppermute | solution.py:696
  37.3 35.6 %collective-permute-start.9 = (bf16[3,32,2560]{2,1,0:T(8,128)(2,1)S(1)}, bf16[3,32,2560]{2,1,0:T(8,128)(2,1)S(1)}, u32[]{:S(2)}, u32[]{:S(2)}) collective-permute-start(bf16[3,32,2560]{2,1,0:T(8,128)(2,1)S(1)} %get-tuple-element.54), channel_id=1, source_target_pairs={{4,12},{8,0},{5,13},{9,1},{6,14},{10,2},{7,15},{11,3},{20,28},{24,... | collective-permute-start | bytes 1474568 | tf_op jit(solution)/shard_map/ppermute | solution.py:707
  38.6 34.3 %copy-start.4 = (s32[256]{0:T(256)S(1)}, s32[256]{0:T(256)}, u32[]{:S(2)}) copy-start(s32[256]{0:T(256)} %param.11) | copy-start | bytes 3076
  38.6 34.2 %collective-permute-start.10 = (bf16[3,32,2560]{2,1,0:T(8,128)(2,1)S(1)}, bf16[3,32,2560]{2,1,0:T(8,128)(2,1)S(1)}, u32[]{:S(2)}, u32[]{:S(2)}) collective-permute-start(bf16[3,32,2560]{2,1,0:T(8,128)(2,1)S(1)} %get-tuple-element.55), channel_id=1, source_target_pairs={{0,12},{12,0},{1,13},{13,1},{2,14},{14,2},{3,15},{15,3},{16,28},{2... | collective-permute-start | bytes 1474568 | tf_op jit(solution)/shard_map/ppermute | solution.py:707
  46.4 26.5 %collective-permute-start.7 = (bf16[3,32,2560]{2,1,0:T(8,128)(2,1)S(1)}, bf16[3,32,2560]{2,1,0:T(8,128)(2,1)S(1)}, u32[]{:S(2)}, u32[]{:S(2)}) collective-permute-start(bf16[3,32,2560]{2,1,0:T(8,128)(2,1)S(1)} %get-tuple-element.51), channel_id=1, source_target_pairs={{0,4},{4,0},{8,12},{12,8},{1,5},{5,1},{9,13},{13,9},{2,6},{6,2},{1... | collective-permute-start | bytes 1474568 | tf_op jit(solution)/shard_map/ppermute | solution.py:707
  48.6 38.5 %collective-permute-start.8 = (bf16[3,32,2560]{2,1,0:T(8,128)(2,1)S(1)}, bf16[3,32,2560]{2,1,0:T(8,128)(2,1)S(1)}, u32[]{:S(2)}, u32[]{:S(2)}) collective-permute-start(bf16[3,32,2560]{2,1,0:T(8,128)(2,1)S(1)} %get-tuple-element.52), channel_id=1, source_target_pairs={{0,8},{12,4},{1,9},{13,5},{2,10},{14,6},{3,11},{15,7},{16,24},{28,... | collective-permute-start | bytes 1474568 | tf_op jit(solution)/shard_map/ppermute | solution.py:707
  53.1 34.7 %collective-permute-start.11 = (bf16[3,32,2560]{2,1,0:T(8,128)(2,1)S(1)}, bf16[3,32,2560]{2,1,0:T(8,128)(2,1)S(1)}, u32[]{:S(2)}, u32[]{:S(2)}) collective-permute-start(bf16[3,32,2560]{2,1,0:T(8,128)(2,1)S(1)} %get-tuple-element.59), channel_id=1, source_target_pairs={{4,8},{8,4},{5,9},{9,5},{6,10},{10,6},{7,11},{11,7},{20,24},{24,20... | collective-permute-start | bytes 1474568 | tf_op jit(solution)/shard_map/ppermute | solution.py:707

commit v6 on v5

--- a/solution.py
+++ b/solution.py
@@ -519,7 +519,7 @@
         width = CELL + SPAN
         started = []
         for number, part in enumerate(parts):
-            low, high = (0, late) if part == 0 else (late, ang_count)
+            low, high = (0 if part == 0 else late, late if parts == (0,) else ang_count)
 
             def lines(span, low=low, high=high):
                 if loads:
@@ -533,8 +533,9 @@
                 here = slice(block * TILE, (block + 1) * TILE)
                 y_ref[low * groups : high * groups, :, here] = values.reshape((high - low) * groups, lines_each, TILE)
 
-            ramp_lines(lines, cols // 2, *ramp_refs, store)
-            for lane in range(low, high):
+            if number == 0:
+                ramp_lines(lines, cols // 2, *ramp_refs, store)
+            for lane in range(low, high) if number == 0 else ():
                 target = out_ref.at[pl.ds((turn ^ lane) * groups, groups)]
                 source = y_ref.at[(lane - base) * groups : (lane - base + 1) * groups]
                 started.append(pltpu.make_async_copy(source, target, out_sems.at[lane]))
@@ -550,7 +551,7 @@
 
             lead_ref, mate_ref, *stacks = refs
             if loads:
-                pick_lines(known[:high], cols, picks[part], lead_ref, mate_ref)
+                pick_lines(known[: late if part == 0 else ang_count], cols, picks[part], lead_ref, mate_ref)
             else:
                 are_leads = (turn ^ late) < ang_count // 2
                 add_lines(

time: 89.5 us -> 88.5 us (0.989)
  the two profiles are of different devices: /device:TPU:0 before, /device:TPU:19 now
where the time goes in v6:
time: 88.5 us; the launch traced here: 87.7 us
  waiting for transfers between devices  34.8 us (39%)
  Pallas kernels  34.1 us (39%)
  starting transfers between devices  17 us (19%)
  between operations  1.09 us (1%)
    ppermute x5, waiting for transfers between devices, send(): return lax.ppermute(lines, 'ang', pairs)  21.2 us
    pallas_call x3, Pallas kernels, finish(): pl.pallas_call(skipping(kernel, len(args) - 1), out_shape=[jax.ShapeDtype...  16.2 us
    ppermute x5, waiting for transfers between devices, exchange(): lax.ppermute(sent, 'row', [(i, i ^ step) for i in range(row_count) if wan...  13.6 us
    ppermute x5, starting transfers between devices, exchange(): lax.ppermute(sent, 'row', [(i, i ^ step) for i in range(row_count) if wan...  8.02 us
    ppermute x5, starting transfers between devices, send(): return lax.ppermute(lines, 'ang', pairs)  7.54 us
    pallas_call x2, Pallas kernels, lowpass_call(): pl.pallas_call(skipping(functools.partial(kernel, groups, row_count, uppe...  6.73 us
    pallas_call x1, Pallas kernels, edges(): pl.pallas_call(functools.partial(edge_kernel, planes, rows), out_shape=[j...  3.45 us
    pallas_call x2, Pallas kernels, route(): pl.pallas_call(skipping(functools.partial(route_kernel, row_count, upper,...  2.87 us
  transfers between devices with their start and end apart: 12, of which 6 were waited for; matrix products, arithmetic and copies ran while one was open for 0% of the time, Pallas kernels for 28%

profile of v6, /device:TPU:19, one launch (start us, length us, event | category | flops | bytes accessed | tf_op | source)
XLA Modules:
  0.0 87.7 jit_solution(7584889815226572283)
XLA Ops:
  1.2 3.5 %shard_map.78 = (bf16[14,16,2560]{2,1,0:T(8,128)(2,1)}, bf16[14,16,2560]{2,1,0:T(8,128)(2,1)}) custom-call(s32[4]{0:T(128)} %pad_add_fusion.place_ref.refs_0_, bf16[12,32,2560]{2,1,0:T(8,128)(2,1)} %refs_1_.1, bf16[32,2560]{1,0:T(8,128)(2,1)} %refs_3_.1, bf16[32,2560]{1,0:T(8,128)(2,1)} %refs_4_.1), custom_call_target="tpu_custom_call" | custom-call | flops 2300000000 | bytes 65536 | tf_op jit(solution)/shard_map/pallas_call | solution.py:153
  4.7 0.7 collective-permute-start
  5.4 0.7 collective-permute-start.2
  6.2 1.4 %shard_map.81 = (bf16[256,384]{1,0:T(8,128)(2,1)S(1)}, bf16[256,512]{1,0:T(8,128)(2,1)S(1)}) custom-call(s32[4]{0:T(128)S(1)} %copy-done, s32[24]{0:T(128)S(1)} %copy-done.5), custom_call_target="tpu_custom_call" | custom-call | flops 1724999936 | bytes 65536 | tf_op jit(solution)/shard_map/pallas_call | solution.py:668
  7.5 1.3 %shard_map.77 = (bf16[2304,256]{1,0:T(8,128)(2,1)S(1)}, bf16[2304,256]{1,0:T(8,128)(2,1)S(1)}, bf16[256,256]{1,0:T(8,128)(2,1)S(1)}) custom-call(), custom_call_target="tpu_custom_call" | custom-call | flops 2070000000 | bytes 65536 | tf_op jit(solution)/shard_map/pallas_call | solution.py:657
  8.9 2.2 %shard_map.79 = (bf16[256,256]{1,0:T(8,128)(2,1)S(1)}, bf16[256,64]{1,0:T(8,128)(2,1)S(1)}, bf16[2,512,256]{2,1,0:T(8,128)(2,1)S(1)}) custom-call(s32[4]{0:T(128)S(1)} %copy-done, f32[31]{0:T(128)S(1)} %copy-done.6), custom_call_target="tpu_custom_call" | custom-call | flops 2300000000 | bytes 65536 | tf_op jit(solution)/shard_map/pallas_call | solution.py:645
  11.2 6.0 %shard_map.80 = (bf16[3,1,32,2560]{3,2,1,0:T(8,128)(2,1)S(1)}, bf16[3,1,32,2560]{3,2,1,0:T(8,128)(2,1)S(1)}, bf16[3,1,32,2560]{3,2,1,0:T(8,128)(2,1)S(1)}, bf16[...) custom-call(s32[4]{0:T(128)S(1)} %copy-done, ...), custom_call_target="tpu_custom_call" | custom-call | flops 7474999808 | bytes 65536 | tf_op jit(solution)/shard_map/pallas_call | solution.py:301
  17.4 2.7 %collective-permute-start.5 = (bf16[3,1,32,2560]{3,2,1,0:T(8,128)(2,1)S(1)}, bf16[3,1,32,2560]{3,2,1,0:T(8,128)(2,1)S(1)}, u32[]{:S(2)}, u32[]{:S(2)}) collective-permute-start(bf16[3,1,32,2560]{3,2,1,0:T(8,128)(2,1)S(1)} %get-tuple-element.49), channel_id=1, source_target_pairs={{0,2},{3,1},{4,6},{7,5},{8,10},{11,9},{12,14},{15,13},{16,18},{19,... | collective-permute-start | bytes 1474568 | tf_op jit(solution)/shard_map/ppermute | solution.py:697
  20.1 3.1 %collective-permute-start.6 = (bf16[3,1,32,2560]{3,2,1,0:T(8,128)(2,1)S(1)}, bf16[3,1,32,2560]{3,2,1,0:T(8,128)(2,1)S(1)}, u32[]{:S(2)}, u32[]{:S(2)}) collective-permute-start(bf16[3,1,32,2560]{3,2,1,0:T(8,128)(2,1)S(1)} %get-tuple-element.50), channel_id=1, source_target_pairs={{0,3},{3,0},{4,7},{7,4},{8,11},{11,8},{12,15},{15,12},{16,19},{19,... | collective-permute-start | bytes 1474568 | tf_op jit(solution)/shard_map/ppermute | solution.py:697
  23.3 0.7 shard_map.82
  24.7 1.3 %collective-permute-start.3 = (bf16[3,1,32,2560]{3,2,1,0:T(8,128)(2,1)S(1)}, bf16[3,1,32,2560]{3,2,1,0:T(8,128)(2,1)S(1)}, u32[]{:S(2)}, u32[]{:S(2)}) collective-permute-start(bf16[3,1,32,2560]{3,2,1,0:T(8,128)(2,1)S(1)} %get-tuple-element.47.refs_9_.refs_5_.refs_14_), channel_id=1, source_target_pairs={{1,3},{2,0},{5,7},{6,4},{9,11},{10,8},{13,15},{14,12},{17,19},{18,... | collective-permute-start | bytes 1474568 | tf_op jit(solution)/shard_map/ppermute | solution.py:697
  26.4 9.2 %collective-permute-done.6.refs_4_.refs_7_ = bf16[3,1,32,2560]{3,2,1,0:T(8,128)(2,1)S(1)} collective-permute-done((bf16[3,1,32,2560]{3,2,1,0:T(8,128)(2,1)S(1)}, bf16[3,1,32,2560]{3,2,1,0:T(8,128)(2,1)S(1)}, u32[]{:S(2)}, u32[]{:S(2)}) %collective-permute-start.6) | collective-permute-done | bytes 491552 | tf_op jit(solution)/shard_map/ppermute | solution.py:697
  35.6 1.2 %shard_map.84 = (bf16[3,32,2560]{2,1,0:T(8,128)(2,1)S(1)}, bf16[3,32,2560]{2,1,0:T(8,128)(2,1)S(1)}) custom-call(s32[4]{0:T(128)S(1)} %copy-done, bf16[3,1,32,2560]{3,2,1,0:T(8,128)(2,1)S(1)} %get-tuple-element.40.refs_7_.refs_1_.refs_5_.refs_4_, bf16[3,1,32,2560]{3,2,1,0:T(8,128)(2,1)S(1)} %collective-permute-done.1.refs_2_.refs_6_.refs_5_, ...), custom_call_target="tpu_custom_call" | custom-call | flops 2300000000 | bytes 65536 | tf_op jit(solution)/shard_map/pallas_call | solution.py:335
  36.9 2.0 %collective-permute-start.9 = (bf16[3,32,2560]{2,1,0:T(8,128)(2,1)S(1)}, bf16[3,32,2560]{2,1,0:T(8,128)(2,1)S(1)}, u32[]{:S(2)}, u32[]{:S(2)}) collective-permute-start(bf16[3,32,2560]{2,1,0:T(8,128)(2,1)S(1)} %get-tuple-element.54), channel_id=1, source_target_pairs={{4,12},{8,0},{5,13},{9,1},{6,14},{10,2},{7,15},{11,3},{20,28},{24,... | collective-permute-start | bytes 1474568 | tf_op jit(solution)/shard_map/ppermute | solution.py:708
  39.6 4.0 %collective-permute-done.3.refs_7_.refs_6_ = bf16[3,1,32,2560]{3,2,1,0:T(8,128)(2,1)S(1)} collective-permute-done((bf16[3,1,32,2560]{3,2,1,0:T(8,128)(2,1)S(1)}, bf16[3,1,32,2560]{3,2,1,0:T(8,128)(2,1)S(1)}, u32[]{:S(2)}, u32[]{:S(2)}) %collective-permute-start.3) | collective-permute-done | bytes 491552 | tf_op jit(solution)/shard_map/ppermute | solution.py:697
  43.6 1.6 %shard_map.83 = (bf16[3,32,2560]{2,1,0:T(8,128)(2,1)S(1)}, bf16[3,32,2560]{2,1,0:T(8,128)(2,1)S(1)}, bf16[3,32,2560]{2,1,0:T(8,128)(2,1)S(1)}) custom-call(s32[4]{0:T(128)S(1)} %copy-done, bf16[3,1,32,2560]{3,2,1,0:T(8,128)(2,1)S(1)} %get-tuple-element.40.refs_7_.refs_1_.refs_5_.refs_4_, ...), custom_call_target="tpu_custom_call" | custom-call | flops 2300000000 | bytes 65536 | tf_op jit(solution)/shard_map/pallas_call | solution.py:335
  45.2 1.7 %collective-permute-start.7 = (bf16[3,32,2560]{2,1,0:T(8,128)(2,1)S(1)}, bf16[3,32,2560]{2,1,0:T(8,128)(2,1)S(1)}, u32[]{:S(2)}, u32[]{:S(2)}) collective-permute-start(bf16[3,32,2560]{2,1,0:T(8,128)(2,1)S(1)} %get-tuple-element.51), channel_id=1, source_target_pairs={{0,4},{4,0},{8,12},{12,8},{1,5},{5,1},{9,13},{13,9},{2,6},{6,2},{1... | collective-permute-start | bytes 1474568 | tf_op jit(solution)/shard_map/ppermute | solution.py:708
  46.9 1.3 %collective-permute-start.8 = (bf16[3,32,2560]{2,1,0:T(8,128)(2,1)S(1)}, bf16[3,32,2560]{2,1,0:T(8,128)(2,1)S(1)}, u32[]{:S(2)}, u32[]{:S(2)}) collective-permute-start(bf16[3,32,2560]{2,1,0:T(8,128)(2,1)S(1)} %get-tuple-element.52), channel_id=1, source_target_pairs={{0,8},{12,4},{1,9},{13,5},{2,10},{14,6},{3,11},{15,7},{16,24},{28,... | collective-permute-start | bytes 1474568 | tf_op jit(solution)/shard_map/ppermute | solution.py:708
  48.2 1.9 %collective-permute-start.11 = (bf16[3,32,2560]{2,1,0:T(8,128)(2,1)S(1)}, bf16[3,32,2560]{2,1,0:T(8,128)(2,1)S(1)}, u32[]{:S(2)}, u32[]{:S(2)}) collective-permute-start(bf16[3,32,2560]{2,1,0:T(8,128)(2,1)S(1)} %get-tuple-element.59), channel_id=1, source_target_pairs={{4,8},{8,4},{5,9},{9,5},{6,10},{10,6},{7,11},{11,7},{20,24},{24,20... | collective-permute-start | bytes 1474568 | tf_op jit(solution)/shard_map/ppermute | solution.py:708
  50.1 9.1 %collective-permute-done.9.refs_9_ = bf16[3,32,2560]{2,1,0:T(8,128)(2,1)S(1)} collective-permute-done((bf16[3,32,2560]{2,1,0:T(8,128)(2,1)S(1)}, bf16[3,32,2560]{2,1,0:T(8,128)(2,1)S(1)}, u32[]{:S(2)}, u32[]{:S(2)}) %collective-permute-start.9) | collective-permute-done | bytes 491552 | tf_op jit(solution)/shard_map/ppermute | solution.py:708
  59.2 9.7 %collective-permute-done.7.refs_8_.refs_5_ = bf16[3,32,2560]{2,1,0:T(8,128)(2,1)S(1)} collective-permute-done((bf16[3,32,2560]{2,1,0:T(8,128)(2,1)S(1)}, bf16[3,32,2560]{2,1,0:T(8,128)(2,1)S(1)}, u32[]{:S(2)}, u32[]{:S(2)}) %collective-permute-start.7) | collective-permute-done | bytes 491552 | tf_op jit(solution)/shard_map/ppermute | solution.py:708
  69.5 2.4 %collective-permute-done.8.refs_9_.refs_6_ = bf16[3,32,2560]{2,1,0:T(8,128)(2,1)S(1)} collective-permute-done((bf16[3,32,2560]{2,1,0:T(8,128)(2,1)S(1)}, bf16[3,32,2560]{2,1,0:T(8,128)(2,1)S(1)}, u32[]{:S(2)}, u32[]{:S(2)}) %collective-permute-start.8) | collective-permute-done | bytes 491552 | tf_op jit(solution)/shard_map/ppermute | solution.py:708
  71.9 9.4 %shard_map.86 = (bf16[12,32,2560]{2,1,0:T(8,128)(2,1)}, f32[8,1152]{1,0:T(8,128)S(1)}, bf16[3,32,2560]{2,1,0:T(8,128)(2,1)S(1)}, bf16[128,2560]{1,0:T(8,128)(2,1)S(1)}, bf16[128,3072]{1,0:T(8,128)(2,1)S(1)}) custom-call(s32[4]{0:T(128)S(1)} %copy-done, bf16[2304,256]{1,0:T(8,128)(2,1)S(1)} %get-tuple-element.34.refs_8_.refs_1_, ...), custom_call_target="tpu_custom_call", output_to_operand_aliasing={{0}: (12, {})} | custom-call | flops 5750000128 | bytes 65536 | tf_op jit(solution)/shard_map/pallas_call | solution.py:599
  81.3 6.2 %shard_map.87 = (bf16[12,32,2560]{2,1,0:T(8,128)(2,1)}, f32[8,256]{1,0:T(8,128)}) custom-call(s32[4]{0:T(128)S(1)} %copy-done, bf16[2304,256]{1,0:T(8,128)(2,1)S(1)} %get-tuple-element.34.refs_8_.refs_1_, bf16[2304,256]{1,0:T(8,128)(2,1)S(1)} %get-tuple-element.35.refs_2_, ...), custom_call_target="tpu_custom_call", output_to_operand_aliasing={{0}: (12, {})} | custom-call | flops 5750000128 | bytes 65536 | tf_op jit(solution)/shard_map/pallas_call | solution.py:599
  (26 shorter events, 3.2 us)
Async XLA Ops:
  1.2 4.9 %copy-start = (s32[4]{0:T(128)S(1)}, s32[4]{0:T(128)}, u32[]{:S(2)}) copy-start(s32[4]{0:T(128)} %pad_add_fusion.place_ref.refs_0_) | copy-start | bytes 52
  1.2 4.9 %copy-start.5 = (s32[24]{0:T(128)S(1)}, s32[24]{0:T(128)}, u32[]{:S(2)}) copy-start(s32[24]{0:T(128)} %partner_ref.1) | copy-start | bytes 292
  4.7 6.5 %collective-permute-start = (bf16[14,16,2560]{2,1,0:T(8,128)(2,1)}, bf16[14,16,2560]{2,1,0:T(8,128)(2,1)S(1)}, u32[]{:S(2)}, u32[]{:S(2)}) collective-permute-start(bf16[14,16,2560]{2,1,0:T(8,128)(2,1)} %get-tuple-element.37), channel_id=1, source_target_pairs={{0,1},{1,0},{2,3},{3,2},{4,5},{5,4},{6,7},{7,6},{8,9},{9,8},{10,11... | collective-permute-start | bytes 3440648 | tf_op jit(solution)/shard_map/ppermute | solution.py:643
  5.4 17.8 %collective-permute-start.2 = (bf16[14,16,2560]{2,1,0:T(8,128)(2,1)}, bf16[14,16,2560]{2,1,0:T(8,128)(2,1)S(1)}, u32[]{:S(2)}, u32[]{:S(2)}) collective-permute-start(bf16[14,16,2560]{2,1,0:T(8,128)(2,1)} %get-tuple-element.42), channel_id=1, source_target_pairs={{1,2},{2,1},{5,6},{6,5},{9,10},{10,9},{13,14},{14,13},{17,18},{18,... | collective-permute-start | bytes 3440648 | tf_op jit(solution)/shard_map/ppermute | solution.py:642
  7.5 1.4 %copy-start.6 = (f32[31]{0:T(128)S(1)}, f32[31]{0:T(128)}, u32[]{:S(2)}) copy-start(f32[31]{0:T(128)} %taps_ref.1) | copy-start | bytes 376
  8.9 2.3 %copy-start.1 = (bf16[12,32,2560]{2,1,0:T(8,128)(2,1)S(1)}, bf16[12,32,2560]{2,1,0:T(8,128)(2,1)}, u32[]{:S(2)}) copy-start(bf16[12,32,2560]{2,1,0:T(8,128)(2,1)} %refs_1_.1) | copy-start | bytes 5898244
  8.9 2.3 %copy-start.2 = (bf16[32,2560]{1,0:T(8,128)(2,1)S(1)}, bf16[32,2560]{1,0:T(8,128)(2,1)}, u32[]{:S(2)}) copy-start(bf16[32,2560]{1,0:T(8,128)(2,1)} %refs_3_.1) | copy-start | bytes 491524
  8.9 2.3 %copy-start.3 = (bf16[32,2560]{1,0:T(8,128)(2,1)S(1)}, bf16[32,2560]{1,0:T(8,128)(2,1)}, u32[]{:S(2)}) copy-start(bf16[32,2560]{1,0:T(8,128)(2,1)} %refs_4_.1) | copy-start | bytes 491524
  17.2 8.8 %collective-permute-start.1 = (bf16[3,1,32,2560]{3,2,1,0:T(8,128)(2,1)S(1)}, bf16[3,1,32,2560]{3,2,1,0:T(8,128)(2,1)S(1)}, u32[]{:S(2)}, u32[]{:S(2)}) collective-permute-start(bf16[3,1,32,2560]{3,2,1,0:T(8,128)(2,1)S(1)} %get-tuple-element.41), channel_id=1, source_target_pairs={{0,1},{1,0},{2,3},{3,2},{4,5},{5,4},{6,7},{7,6},{8,9},{9,8},{10,11... | collective-permute-start | bytes 1474568 | tf_op jit(solution)/shard_map/ppermute | solution.py:697
  17.4 9.0 %collective-permute-start.5 = (bf16[3,1,32,2560]{3,2,1,0:T(8,128)(2,1)S(1)}, bf16[3,1,32,2560]{3,2,1,0:T(8,128)(2,1)S(1)}, u32[]{:S(2)}, u32[]{:S(2)}) collective-permute-start(bf16[3,1,32,2560]{3,2,1,0:T(8,128)(2,1)S(1)} %get-tuple-element.49), channel_id=1, source_target_pairs={{0,2},{3,1},{4,6},{7,5},{8,10},{11,9},{12,14},{15,13},{16,18},{19,... | collective-permute-start | bytes 1474568 | tf_op jit(solution)/shard_map/ppermute | solution.py:697
  20.1 15.5 %collective-permute-start.6 = (bf16[3,1,32,2560]{3,2,1,0:T(8,128)(2,1)S(1)}, bf16[3,1,32,2560]{3,2,1,0:T(8,128)(2,1)S(1)}, u32[]{:S(2)}, u32[]{:S(2)}) collective-permute-start(bf16[3,1,32,2560]{3,2,1,0:T(8,128)(2,1)S(1)} %get-tuple-element.50), channel_id=1, source_target_pairs={{0,3},{3,0},{4,7},{7,4},{8,11},{11,8},{12,15},{15,12},{16,19},{19,... | collective-permute-start | bytes 1474568 | tf_op jit(solution)/shard_map/ppermute | solution.py:697
  24.0 15.6 %collective-permute-start.4 = (bf16[3,1,32,2560]{3,2,1,0:T(8,128)(2,1)S(1)}, bf16[3,1,32,2560]{3,2,1,0:T(8,128)(2,1)S(1)}, u32[]{:S(2)}, u32[]{:S(2)}) collective-permute-start(bf16[3,1,32,2560]{3,2,1,0:T(8,128)(2,1)S(1)} %get-tuple-element.48), channel_id=1, source_target_pairs={{1,2},{2,1},{5,6},{6,5},{9,10},{10,9},{13,14},{14,13},{17,18},{18,... | collective-permute-start | bytes 1474568 | tf_op jit(solution)/shard_map/ppermute | solution.py:697
  24.7 18.9 %collective-permute-start.3 = (bf16[3,1,32,2560]{3,2,1,0:T(8,128)(2,1)S(1)}, bf16[3,1,32,2560]{3,2,1,0:T(8,128)(2,1)S(1)}, u32[]{:S(2)}, u32[]{:S(2)}) collective-permute-start(bf16[3,1,32,2560]{3,2,1,0:T(8,128)(2,1)S(1)} %get-tuple-element.47.refs_9_.refs_5_.refs_14_), channel_id=1, source_target_pairs={{1,3},{2,0},{5,7},{6,4},{9,11},{10,8},{13,15},{14,12},{17,19},{18,... | collective-permute-start | bytes 1474568 | tf_op jit(solution)/shard_map/ppermute | solution.py:697
  36.9 22.3 %collective-permute-start.9 = (bf16[3,32,2560]{2,1,0:T(8,128)(2,1)S(1)}, bf16[3,32,2560]{2,1,0:T(8,128)(2,1)S(1)}, u32[]{:S(2)}, u32[]{:S(2)}) collective-permute-start(bf16[3,32,2560]{2,1,0:T(8,128)(2,1)S(1)} %get-tuple-element.54), channel_id=1, source_target_pairs={{4,12},{8,0},{5,13},{9,1},{6,14},{10,2},{7,15},{11,3},{20,28},{24,... | collective-permute-start | bytes 1474568 | tf_op jit(solution)/shard_map/ppermute | solution.py:708
  38.9 30.0 %copy-start.4 = (s32[256]{0:T(256)S(1)}, s32[256]{0:T(256)}, u32[]{:S(2)}) copy-start(s32[256]{0:T(256)} %param.11) | copy-start | bytes 3076
  38.9 20.3 %collective-permute-start.10 = (bf16[3,32,2560]{2,1,0:T(8,128)(2,1)S(1)}, bf16[3,32,2560]{2,1,0:T(8,128)(2,1)S(1)}, u32[]{:S(2)}, u32[]{:S(2)}) collective-permute-start(bf16[3,32,2560]{2,1,0:T(8,128)(2,1)S(1)} %get-tuple-element.55), channel_id=1, source_target_pairs={{0,12},{12,0},{1,13},{13,1},{2,14},{14,2},{3,15},{15,3},{16,28},{2... | collective-permute-start | bytes 1474568 | tf_op jit(solution)/shard_map/ppermute | solution.py:708
  45.2 23.6 %collective-permute-start.7 = (bf16[3,32,2560]{2,1,0:T(8,128)(2,1)S(1)}, bf16[3,32,2560]{2,1,0:T(8,128)(2,1)S(1)}, u32[]{:S(2)}, u32[]{:S(2)}) collective-permute-start(bf16[3,32,2560]{2,1,0:T(8,128)(2,1)S(1)} %get-tuple-element.51), channel_id=1, source_target_pairs={{0,4},{4,0},{8,12},{12,8},{1,5},{5,1},{9,13},{13,9},{2,6},{6,2},{1... | collective-permute-start | bytes 1474568 | tf_op jit(solution)/shard_map/ppermute | solution.py:708
  46.9 25.0 %collective-permute-start.8 = (bf16[3,32,2560]{2,1,0:T(8,128)(2,1)S(1)}, bf16[3,32,2560]{2,1,0:T(8,128)(2,1)S(1)}, u32[]{:S(2)}, u32[]{:S(2)}) collective-permute-start(bf16[3,32,2560]{2,1,0:T(8,128)(2,1)S(1)} %get-tuple-element.52), channel_id=1, source_target_pairs={{0,8},{12,4},{1,9},{13,5},{2,10},{14,6},{3,11},{15,7},{16,24},{28,... | collective-permute-start | bytes 1474568 | tf_op jit(solution)/shard_map/ppermute | solution.py:708
  48.2 33.1 %collective-permute-start.11 = (bf16[3,32,2560]{2,1,0:T(8,128)(2,1)S(1)}, bf16[3,32,2560]{2,1,0:T(8,128)(2,1)S(1)}, u32[]{:S(2)}, u32[]{:S(2)}) collective-permute-start(bf16[3,32,2560]{2,1,0:T(8,128)(2,1)S(1)} %get-tuple-element.59), channel_id=1, source_target_pairs={{4,8},{8,4},{5,9},{9,5},{6,10},{10,6},{7,11},{11,7},{20,24},{24,20... | collective-permute-start | bytes 1474568 | tf_op jit(solution)/shard_map/ppermute | solution.py:708
